TPU v7x, 128 devices: a whole 4x4x4 slice. The times are simulated.
128 devices in a mesh: wide: 32 (over x, z_lo, y), narrow: 4 (over z_hi, core).
Axes of the slice: x: 4, y: 4, z: 4 (z_hi: 2, z_lo: 2; z = z_hi * 2 + z_lo), core: 2. Of those that a mesh axis runs over, the one named last changes fastest.
Arguments:
- velocity: bfloat16 [3, 512, 32, 2, 1024], P(None, 'wide', None, None, 'narrow'), may hold values from -6 to 6
- inverses: bfloat16 [8, 32, 32], replicated, may hold values from -2.4 to 2.4, as said below
- class_index: int32 [512, 1024], P('wide', 'narrow'), may hold values from 0 to 7
- keep_count: int32 [512], P('wide'), may hold values from 256 to 512, as said below
Outputs:
- advanced: float32 [3, 512, 32, 2, 1024], P(None, 'wide', None, None, 'narrow')
Inputs may be any that keep to these rules, and one draw needn't show every extreme that they name: `inverses`: dense matrices standing for each wavenumber class's inverse of the implicit wall-normal operator. Mode (kx, m) of the products is kept where |m| < keep_count[kx].
All inputs are finite; a program needn't handle non-finite values.
Results may differ from a plain program's by a relative error of at most 0.0045.
Values may be sent and summed in bfloat16 or wider, within the bound.
No kernel may reach another device: no remote copies, remote signals or barrier semaphores. Data moves between devices by JAX's collectives and lax.ppermute only.
A program may use at most 64 MiB of HBM per device.

v0:
```python
import math

import jax
import jax.numpy as jnp
from jax import lax
from jax.sharding import PartitionSpec as P

KX = 512
KZ = 1024
NCLASS = 8
PX = 1536
PZ = 1536


def z_table():
    mode_index = jnp.arange(KZ, dtype=jnp.int32)
    wavenumber = jnp.where(mode_index < KZ // 2, mode_index, mode_index - KZ)
    points = jnp.arange(PZ, dtype=jnp.int32)
    phases = wavenumber[:, None] * points[None, :] % PZ
    angles = 2.0 * math.pi / PZ * phases.astype(jnp.float32)
    cos_part = jnp.cos(angles)
    sin_part = jnp.sin(angles)
    top_half = jnp.concatenate([cos_part, sin_part], axis=1)
    low_half = jnp.concatenate([-sin_part, cos_part], axis=1)
    return jnp.concatenate([top_half, low_half], axis=0).astype(jnp.bfloat16)


def x_tables(kx_values):
    points = jnp.arange(PX, dtype=jnp.int32)
    phases = kx_values[:, None] * points[None, :] % PX
    angles = 2.0 * math.pi / PX * phases.astype(jnp.float32)
    basis = jnp.stack([jnp.cos(angles), -jnp.sin(angles)], axis=1)
    weights = jnp.where(kx_values == 0, 1.0, 2.0).astype(jnp.float32)
    return ((weights[:, None, None] * basis).astype(jnp.bfloat16), basis.astype(jnp.bfloat16))


def body(velocity, inverses, class_index, keep_count):
    n_wide = lax.axis_size("wide")
    kx_wide = velocity.shape[1]
    y_total = velocity.shape[2]
    kz_quarter = velocity.shape[4]
    y_local = y_total // n_wide
    planes = lax.all_to_all(
        lax.all_to_all(velocity, "wide", split_axis=2, concat_axis=1, tiled=True),
        "narrow",
        split_axis=1,
        concat_axis=4,
        tiled=True,
    )
    kx_values = jnp.arange(KX, dtype=jnp.int32)
    z_basis = z_table()
    x_synth, x_basis = x_tables(kx_values)
    kx_rows = planes.shape[1]
    spread = jnp.dot(planes.reshape(-1, 2 * KZ), z_basis, preferred_element_type=jnp.float32)
    spread = spread.astype(jnp.bfloat16).reshape(3, kx_rows, y_local, 2, PZ)
    fields = jnp.einsum(
        "ckyrb,kra->cyab",
        lax.all_to_all(spread, "narrow", split_axis=4, concat_axis=1, tiled=True),
        x_synth,
        preferred_element_type=jnp.float32,
    ) * (0.5 / math.sqrt(KX * KZ))
    product = (fields * fields[1:2]).astype(jnp.bfloat16)
    folded = jnp.einsum("cyab,kra->ckyrb", product, x_basis, preferred_element_type=jnp.float32)
    folded = (folded / PX).astype(jnp.bfloat16)
    pieces = lax.all_to_all(folded, "narrow", split_axis=1, concat_axis=4, tiled=True)
    item_count = pieces.shape[0]
    flat_modes = pieces.reshape(-1, 2 * PZ)
    spectra = jnp.dot(flat_modes, z_basis.T, preferred_element_type=jnp.float32)
    spectra = spectra * (2.0 * math.sqrt(KX * KZ) / PZ)
    nonlinear = spectra.astype(jnp.bfloat16).reshape(
        item_count, pieces.shape[1], pieces.shape[2], 2, KZ
    )
    half_way = lax.all_to_all(nonlinear, "narrow", split_axis=4, concat_axis=1, tiled=True)
    returned = lax.all_to_all(half_way, "wide", split_axis=1, concat_axis=2, tiled=True)
    kz_here = lax.axis_index("narrow") * kz_quarter + jnp.arange(kz_quarter, dtype=jnp.int32)
    wavenumber = jnp.where(kz_here < KZ // 2, kz_here, kz_here - KZ)
    kx_here = lax.axis_index("wide") * kx_wide + jnp.arange(kx_wide, dtype=jnp.int32)
    mean_mode = (kx_here[:, None] == 0) & (wavenumber[None, :] == 0)
    keep_mask = (jnp.abs(wavenumber)[None, :] < keep_count[:, None]) & jnp.logical_not(mean_mode)
    kept = jnp.where(keep_mask[None, :, None, None, :], returned.astype(jnp.float32), 0.0)
    right_side = (velocity.astype(jnp.float32) + 0.5 * kept).astype(jnp.bfloat16)
    solved = jnp.zeros(right_side.shape, jnp.float32)
    for block_id in range(NCLASS):
        applied = jnp.einsum(
            "yz,ckzrj->ckyrj", inverses[block_id], right_side, preferred_element_type=jnp.float32
        )
        solved = jnp.where((class_index == block_id)[None, :, None, None, :], applied, solved)
    return solved


def solution(mesh):
    in_specs = (P(None, "wide", None, None, "narrow"), P(), P("wide", "narrow"), P("wide"))
    out_specs = P(None, "wide", None, None, "narrow")
    return jax.shard_map(body, mesh=mesh, in_specs=in_specs, out_specs=out_specs, check_vma=False)
```

profile of v0, /device:TPU:1, one launch (start us, length us, event | category | flops | bytes accessed | tf_op | source)
XLA Modules:
  0.0 288.1 jit_solution(14442045957634652089)
XLA Ops:
  0.0 3.1 %copy.76 = bf16[3,16,32,2,256]{4,1,3,0,2:T(8,128)(2,1)S(1)} copy(bf16[3,16,32,2,256]{4,3,2,1,0:T(2,128)(2,1)} %param.4) | data formatting | bytes 3145728 | tf_op args[0]
  3.1 29.9 %all_to_all.90 = bf16[3,16,32,2,256]{4,1,3,0,2:T(8,128)(2,1)S(1)} all-to-all(bf16[3,16,32,2,256]{4,1,3,0,2:T(8,128)(2,1)S(1)} %copy.76), channel_id=1, replica_groups=mesh['wide'=32,'narrow'=4] {'wide'}, dimensions={2} | all-to-all | bytes 3145728 | tf_op jit(solution)/shard_map/all_to_all | solution.py:44
  33.0 0.1 copy.77
  33.2 2.8 copy.78
  35.9 8.1 %all-to-all-start.1 = ((bf16[3,512,1,2,256]{4,3,0,2,1:T(2,128)(2,1)}), bf16[3,512,1,2,256]{4,3,0,2,1:T(2,128)(2,1)S(1)}, u32[]{:S(2)}, u32[]{:S(2)}) async-start(bf16[3,512,1,2,256]{4,3,0,2,1:T(2,128)(2,1)} %copy.78), calls=%async_computation.1 | async-start | bytes 3145728 | tf_op jit(solution)/shard_map/all_to_all | solution.py:43
  44.1 29.5 %fusion.7 = (bf16[1024,1536]{1,0:T(8,128)(2,1)}, bf16[1024,1536]{1,0:T(8,128)(2,1)}, bf16[1024,1536]{1,0:T(8,128)(2,1)}) fusion(s32[1024]{0:T(1024)S(1)} %compare_select_fusion), kind=kLoop, calls=%fused_computation.15 | loop fusion | flops 20447232 | bytes 9441280 | tf_op jit(solution)/shard_map/convert.8
  73.5 0.0 all-to-all-done.1
  73.5 2.0 copy.134
  75.6 1.2 reshape.181
  76.8 16.8 %fusion.10 = bf16[384,3072]{0,1:T(8,128)(2,1)} fusion(bf16[384,2048]{1,0:T(8,128)(2,1)S(1)} %reshape.181, bf16[1024,1536]{1,0:T(8,128)(2,1)} %get-tuple-element.15, bf16[1024,1536]{1,0:T(8,128)(2,1)} %get-tuple-element.14, bf16[1024,1536]{1,0:T(8,128)(2,1)} %get-tuple-element.13), kind=kOutput, calls=%fused_computation.22 | convolution fusion | flops 4883349504 | bytes 13369344 | tf_op jit(solution)/shard_map/dot_general | solution.py:54
  93.6 5.9 %reshape.201 = bf16[3,128,1,2,1536]{1,0,4,3,2:T(4,128)(2,1)S(1)} reshape(bf16[384,3072]{0,1:T(8,128)(2,1)} %fusion.10) | data formatting | bytes 4718592 | tf_op jit(solution)/shard_map/reshape | solution.py:55
  99.5 8.7 %copy.81 = bf16[3,128,1,2,1536]{1,3,2,0,4:T(2,128)(2,1)} copy(bf16[3,128,1,2,1536]{1,0,4,3,2:T(4,128)(2,1)S(1)} %reshape.201) | data formatting | bytes 4718592 | tf_op jit(solution)/shard_map/reshape | solution.py:55
  108.2 4.8 %all-to-all-start.2 = ((bf16[3,128,1,2,1536]{1,3,2,0,4:T(2,128)(2,1)}), bf16[3,128,1,2,1536]{1,3,2,0,4:T(2,128)(2,1)S(1)}, u32[]{:S(2)}, u32[]{:S(2)}) async-start(bf16[3,128,1,2,1536]{1,3,2,0,4:T(2,128)(2,1)} %copy.81), calls=%async_computation.2 | async-start | bytes 4718592 | tf_op jit(solution)/shard_map/all_to_all | solution.py:58
  113.0 14.0 %sine_negate_fusion = (f32[512,1,1536]{2,0,1:T(8,128)}, f32[512,1,1536]{2,0,1:T(8,128)}) fusion(), kind=kLoop, calls=%fused_computation.39 | loop fusion | flops 7864320 | bytes 6291456 | tf_op jit(solution)/shard_map/neg | solution.py:32
  126.9 15.2 %all-to-all-done.2 = bf16[3,128,1,2,1536]{1,3,2,0,4:T(2,128)(2,1)S(1)} async-done(((bf16[3,128,1,2,1536]{1,3,2,0,4:T(2,128)(2,1)}), bf16[3,128,1,2,1536]{1,3,2,0,4:T(2,128)(2,1)S(1)}, u32[]{:S(2)}, u32[]{:S(2)}) %all-to-all-start.2) | async-done | bytes 2359328 | tf_op jit(solution)/shard_map/all_to_all | solution.py:58
  142.1 5.4 %copy.82 = bf16[3,128,1,2,4,384]{5,1,4,3,0,2:T(8,128)(2,1)} copy(bf16[3,128,1,2,4,384]{1,3,0,5,4,2:T(2,128)(2,1)S(1)} %bitcast.143) | data formatting | bytes 4718592 | tf_op jit(solution)/shard_map/all_to_all | solution.py:58
  147.5 7.4 %fusion.21 = f32[1536,3,384,1]{2,0,3,1:T(8,128)S(1)} fusion(bf16[3,512,2,384]{3,1,2,0:T(8,128)(2,1)} %bitcast.152, f32[512,1,1536]{2,0,1:T(8,128)} %get-tuple-element.16, f32[512,1,1536]{2,0,1:T(8,128)} %get-tuple-element.17, f32[512]{0:T(512)S(1)} %fusion.68), kind=kOutput, calls=%fused_computation.31 | convolution fusion | flops 3628597248 | bytes 15730688 | tf_op jit(solution)/shard_map/ckyrb,kra->cyab/dot_general | solution.py:56
  154.9 0.0 copy-start.2
  154.9 0.6 fusion
  155.5 0.0 copy-start.1
  155.6 0.2 fusion.32
  155.8 1.0 copy-done.2
  156.8 1.1 copy-done.1
  157.9 4.6 %fusion.31 = bf16[3,512,1,2,384]{4,1,0,3,2:T(8,128)(2,1)S(1)} fusion(f32[1536,3,384,1]{2,0,3,1:T(8,128)S(1)} %fusion.21, f32[1536,384]{1,0:T(8,128)S(1)} %fusion.32, f32[512,1,1536]{2,0,1:T(8,128)S(1)} %copy-done.1, f32[512,1,1536]{2,0,1:T(8,128)S(1)} %copy-done.2), kind=kOutput, calls=%fused_computation.45 | convolution fusion | flops 3636068352 | bytes 18087936 | tf_op jit(solution)/shard_map/cyab,kra->ckyrb/dot_general | solution.py:63
  162.6 2.4 copy.84
  165.0 32.7 %all_to_all.91 = bf16[3,512,1,2,384]{4,3,2,0,1:T(2,128)(2,1)S(1)} all-to-all(bf16[3,512,1,2,384]{4,3,2,0,1:T(2,128)(2,1)S(1)} %copy.84), channel_id=1, replica_groups=mesh['wide'=32,'narrow'=4] {'narrow'}, dimensions={1} | all-to-all | bytes 4718592 | tf_op jit(solution)/shard_map/all_to_all | solution.py:65
  197.7 3.0 %copy.133 = bf16[3,4,128,1,2,384]{5,1,4,2,0,3:T(4,128)(2,1)S(1)} copy(bf16[3,4,128,1,2,384]{5,4,0,2,1,3:T(2,128)(2,1)S(1)} %bitcast.144) | data formatting | bytes 4718592 | tf_op jit(solution)/shard_map/all_to_all | solution.py:65
  200.7 3.0 %reshape.185 = bf16[384,3072]{1,0:T(8,128)(2,1)} reshape(bf16[3,128,1,2,4,384]{5,4,3,1,0,2:T(4,128)(2,1)S(1)} %bitcast.145) | data formatting | bytes 4718592 | tf_op jit(solution)/shard_map/reshape | solution.py:67
  203.8 15.4 %multiply_convert_fusion.2 = bf16[384,2048]{1,0:T(8,128)(2,1)S(1)} fusion(bf16[384,3072]{1,0:T(8,128)(2,1)} %reshape.185, bf16[1024,1536]{1,0:T(8,128)(2,1)} %get-tuple-element.15, bf16[1024,1536]{1,0:T(8,128)(2,1)} %get-tuple-element.14, bf16[1024,1536]{1,0:T(8,128)(2,1)} %get-tuple-element.13), kind=kOutput, calls=%fused_computation.37 | convolution fusion | flops 4883742720 | bytes 13369344 | tf_op jit(solution)/shard_map/dot_general | solution.py:68
  219.2 1.2 reshape.186
  220.4 2.5 copy.86
  222.9 24.0 %all_to_all.92 = bf16[3,128,1,2,1024]{1,3,0,2,4:T(2,128)(2,1)S(1)} all-to-all(bf16[3,128,1,2,1024]{1,3,0,2,4:T(2,128)(2,1)S(1)} %copy.86), channel_id=1, replica_groups=mesh['wide'=32,'narrow'=4] {'narrow'}, dimensions={4} | all-to-all | bytes 3145728 | tf_op jit(solution)/shard_map/all_to_all | solution.py:73
  246.9 0.2 copy.87
  247.1 0.7 copy.88
  247.9 0.0 copy-start.5
  247.9 0.0 copy-start.4
  247.9 2.8 copy.89
  250.6 0.0 copy-start
  250.6 4.3 %all-to-all-start.5 = ((bf16[3,512,1,2,256]{4,3,0,2,1:T(2,128)(2,1)}), bf16[3,512,1,2,256]{4,3,0,2,1:T(2,128)(2,1)S(1)}, u32[]{:S(2)}, u32[]{:S(2)}) async-start(bf16[3,512,1,2,256]{4,3,0,2,1:T(2,128)(2,1)} %copy.89), calls=%async_computation.5 | async-start | bytes 3145728 | tf_op jit(solution)/shard_map/all_to_all | solution.py:74
  255.0 0.0 copy-done.5
  255.0 0.1 not_and_fusion
  255.1 0.0 copy-done.4
  255.1 19.9 %all-to-all-done.5 = bf16[3,512,1,2,256]{4,3,0,2,1:T(2,128)(2,1)S(1)} async-done(((bf16[3,512,1,2,256]{4,3,0,2,1:T(2,128)(2,1)}), bf16[3,512,1,2,256]{4,3,0,2,1:T(2,128)(2,1)S(1)}, u32[]{:S(2)}, u32[]{:S(2)}) %all-to-all-start.5) | async-done | bytes 1572896 | tf_op jit(solution)/shard_map/all_to_all | solution.py:74
  275.0 0.2 copy.90
  275.2 0.0 copy-start.3
  275.2 0.0 copy-done
  275.2 1.3 fusion.25
  276.5 0.0 copy-done.3
  276.5 0.6 fusion.37
  277.2 0.6 fusion.39
  277.8 0.6 fusion.41
  278.5 0.6 fusion.43
  279.1 0.6 fusion.45
  279.8 0.6 fusion.47
  280.5 0.6 fusion.49
  281.1 2.4 select_bitcast_fusion
  283.5 4.4 %copy.99 = f32[3,16,32,2,256]{4,3,2,1,0:T(2,128)} copy(f32[3,16,32,2,256]{4,2,3,1,0:T(8,128)S(1)} %select_bitcast_fusion) | data formatting | bytes 6291456 | tf_op jit(solution)/shard_map/jit(_where)/select_n | solution.py:87
  (6 shorter events, 0.1 us)
Async XLA Ops:
  35.9 37.6 %all-to-all-start.1 = ((bf16[3,512,1,2,256]{4,3,0,2,1:T(2,128)(2,1)}), bf16[3,512,1,2,256]{4,3,0,2,1:T(2,128)(2,1)S(1)}, u32[]{:S(2)}, u32[]{:S(2)}) async-start(bf16[3,512,1,2,256]{4,3,0,2,1:T(2,128)(2,1)} %copy.78), calls=%async_computation.1 | async-start | bytes 3145728 | tf_op jit(solution)/shard_map/all_to_all | solution.py:43
  108.2 33.9 %all-to-all-start.2 = ((bf16[3,128,1,2,1536]{1,3,2,0,4:T(2,128)(2,1)}), bf16[3,128,1,2,1536]{1,3,2,0,4:T(2,128)(2,1)S(1)}, u32[]{:S(2)}, u32[]{:S(2)}) async-start(bf16[3,128,1,2,1536]{1,3,2,0,4:T(2,128)(2,1)} %copy.81), calls=%async_computation.2 | async-start | bytes 4718592 | tf_op jit(solution)/shard_map/all_to_all | solution.py:58
  154.9 1.9 copy-start.2
  155.5 2.4 copy-start.1
  247.9 7.1 %copy-start.5 = (s32[16]{0:T(128)S(1)}, s32[16]{0:T(128)}, u32[]{:S(2)}) copy-start(s32[16]{0:T(128)} %param.7) | copy-start | bytes 196
  247.9 7.2 %copy-start.4 = (s32[16,256]{1,0:T(8,128)S(1)}, s32[16,256]{1,0:T(8,128)}, u32[]{:S(2)}) copy-start(s32[16,256]{1,0:T(8,128)} %param.6) | copy-start | bytes 49156
  250.6 24.6 %copy-start = (bf16[3,16,32,2,256]{4,3,2,1,0:T(2,128)(2,1)S(1)}, bf16[3,16,32,2,256]{4,3,2,1,0:T(2,128)(2,1)}, u32[]{:S(2)}) copy-start(bf16[3,16,32,2,256]{4,3,2,1,0:T(2,128)(2,1)} %param.4) | copy-start | bytes 4718596
  250.6 24.3 %all-to-all-start.5 = ((bf16[3,512,1,2,256]{4,3,0,2,1:T(2,128)(2,1)}), bf16[3,512,1,2,256]{4,3,0,2,1:T(2,128)(2,1)S(1)}, u32[]{:S(2)}, u32[]{:S(2)}) async-start(bf16[3,512,1,2,256]{4,3,0,2,1:T(2,128)(2,1)} %copy.89), calls=%async_computation.5 | async-start | bytes 3145728 | tf_op jit(solution)/shard_map/all_to_all | solution.py:74
  275.2 1.3 copy-start.3
where the time goes:
time: 294 us; the launch traced here: 288 us
  blocking collectives  86.7 us (29%)
  local copies, waits for them, and re-layouts  51.8 us (18%)
  matrix products  51.2 us (17%)
  other arithmetic  45.7 us (16%)
  waiting for transfers between devices  35.1 us (12%)
  starting transfers between devices  17.2 us (6%)
    all_to_all x1, blocking collectives, body(): lax.all_to_all(folded, 'narrow', split_axis=1, concat_axis=4, tiled=True)  32.7 us
    all_to_all x1, blocking collectives, body(): lax.all_to_all(velocity, 'wide', split_axis=2, concat_axis=1, tiled=True)  29.9 us
    another operation x1, other arithmetic  29.5 us
    all_to_all x1, blocking collectives, body(): lax.all_to_all(nonlinear, 'narrow', split_axis=4, concat_axis=1, tiled=True)  24 us
    all_to_all x1, waiting for transfers between devices, body(): lax.all_to_all(half_way, 'wide', split_axis=1, concat_axis=2, tiled=True)  19.9 us
    dot_general x1, matrix products, body(): jnp.dot(planes.reshape(-1, 2 * KZ), z_basis, preferred_element_type=jnp.f...  16.8 us
    dot_general x1, matrix products, body(): spectra = jnp.dot(flat_modes, z_basis.T, preferred_element_type=jnp.float32)  15.4 us
    all_to_all x1, waiting for transfers between devices, body(): lax.all_to_all(spread, 'narrow', split_axis=4, concat_axis=1, tiled=True)  15.2 us
  transfers between devices with their start and end apart: 3, of which 2 were waited for; matrix products, arithmetic and copies ran while one was open for 15% of the time, Pallas kernels for 0%

commit v1 on v0

v1 whole, which is shorter than its diff:
```python
import functools
import math

import jax
import jax.numpy as jnp
import ml_dtypes
import numpy as np
from jax import lax
from jax.experimental import pallas as pl
from jax.experimental.pallas import tpu as pltpu
from jax.sharding import Mesh
from jax.sharding import PartitionSpec as P

KX = 512
KZ = 1024
NCLASS = 8
PX = 1536
PZ = 1536
HALF = PX // 2
NY = 32
BF = jnp.bfloat16
VMEM = 60 * 1024 * 1024
COLUMN = ("zl", "zh", "core")
PLANE = ("x", "y")
KX_ORDER = np.concatenate([np.arange(0, 16, 2), np.arange(1, 16, 2)])


def angles(wavenumbers, points, period):
    phases = (wavenumbers[:, None] * points[None, :]) % period
    scaled = np.float32(2.0 * math.pi / period) * phases.astype(np.float32)
    return scaled.astype(np.float64)


def z_table():
    index = np.arange(KZ)
    wavenumber = np.where(index < KZ // 2, index, index - KZ)
    theta = angles(wavenumber, np.arange(PZ), PZ)
    cos_part, sin_part = np.cos(theta), np.sin(theta)
    top = np.concatenate([cos_part, sin_part], axis=1)
    low = np.concatenate([-sin_part, cos_part], axis=1)
    return np.concatenate([top, low], axis=0).astype(np.float32).astype(ml_dtypes.bfloat16)


def x_tables():
    x, y, zl, i = np.meshgrid(np.arange(4), np.arange(4), np.arange(2), np.arange(8), indexing="ij")
    synth, fold = [], []
    for parity in range(2):
        kx = (x * 8 + zl * 4 + y) * 16 + 2 * i + parity
        theta = angles(kx.reshape(-1), np.arange(HALF), PX).reshape(4, 4, 2, 8, HALF)
        basis = np.stack([np.cos(theta), -np.sin(theta)], axis=2).astype(np.float32)
        weight = np.where(kx == 0, 1.0, 2.0).astype(np.float32)[:, :, None, :, :, None]
        synth.append((weight * basis).reshape(512, HALF).T)
        fold.append(basis.reshape(512, HALF))
    return (
        np.stack(synth).astype(ml_dtypes.bfloat16),
        np.stack(fold).astype(ml_dtypes.bfloat16),
    )


def pack_matrix():
    matrix = np.zeros((256, 256), np.float32)
    for t in range(2):
        for plane in range(4):
            for ri in range(2):
                for k in range(16):
                    row = ((t * 4 + plane) * 2 + ri) * 16 + k
                    matrix[row, KX_ORDER[k] * 16 + plane * 4 + t * 2 + ri] = 1.0
    return matrix.astype(ml_dtypes.bfloat16)


def dot(a, b):
    return jnp.dot(a, b, preferred_element_type=jnp.float32)


def pack_kernel(v_ref, p_ref, out_ref):
    for group in range(8):
        rows = [v_ref[c, :, group * 16 : group * 16 + 16, :].reshape(256, 128) for c in range(3)]
        moved = dot(p_ref[...], jnp.concatenate(rows, axis=1)).astype(BF)
        for c in range(3):
            part = moved[:, c * 128 : c * 128 + 128].reshape(2, 4, 2, 16, 128)
            for t in range(2):
                out_ref[group, c, :, :, :, t * 128 : t * 128 + 128] = part[t]


def synth_kernel(r_ref, table_ref, out_ref, lhs):
    @pl.when((pl.program_id(0) == 0) & (pl.program_id(1) == 0))
    def _():
        for zl in range(2):
            for quarter in range(4):
                for ri in range(2):
                    part = r_ref[zl * 4 + quarter, :, :, ri].reshape(192, 256)
                    lhs[zl * 192 : zl * 192 + 192, pl.ds(ri * KZ + quarter * 256, 256)] = part

    lines = dot(lhs[...], table_ref[...])
    for half in range(2):
        part = lines[:, half * 384 : half * 384 + 384].reshape(2, 3, 4, 2, 8, 384)
        for plane in range(4):
            for c in range(3):
                piece = part[:, c, plane]
                mixed = jnp.concatenate([piece[zl, parity] for parity in range(2) for zl in range(2)], axis=0)
                out_ref[plane, half, c, 0] = mixed.astype(BF)


def middle_kernel(d_ref, synth_ref, fold_ref, out_ref, prod, *, scale):
    block = 256
    for step in range(HALF // block):
        rows = slice(step * block, step * block + block)
        fields = []
        for c in range(3):
            even = dot(synth_ref[0, rows, :], d_ref[:, c, :, 0:16, :].reshape(512, 384))
            odd = dot(synth_ref[1, rows, :], d_ref[:, c, :, 16:32, :].reshape(512, 384))
            fields.append((even + odd, even - odd))
        for c in range(3):
            low = fields[c][0] * fields[1][0]
            high = fields[c][1] * fields[1][1]
            prod[c, 0, rows, :] = (low + high).astype(BF)
            prod[c, 1, rows, :] = (low - high).astype(BF)
    for c in range(3):
        for parity in range(2):
            spectra = dot(fold_ref[parity], prod[c, parity]) * scale
            out_ref[:, c, :, parity * 16 : parity * 16 + 16, :] = spectra.astype(BF).reshape(16, 2, 16, 384)


def analyse_kernel(b_ref, table_ref, out_ref, lhs, *, scale):
    @pl.when((pl.program_id(0) == 0) & (pl.program_id(1) == 0))
    def _():
        for plane in range(4):
            for quarter in range(4):
                for ri in range(2):
                    part = b_ref[plane * 4 + quarter, :, ri].reshape(96, 384)
                    lhs[plane * 96 : plane * 96 + 96, pl.ds(ri * PZ + quarter * 384, 384)] = part

    spectra = scale * lax.dot_general(
        lhs[...], table_ref[...], (((1,), (1,)), ((), ())), preferred_element_type=jnp.float32
    )
    part = spectra.reshape(4, 3, 2, 2, 8, 512)
    for core in range(2):
        for zl in range(2):
            for c in range(3):
                for plane in range(4):
                    piece = part[plane, c, :, zl, :, core * 256 : core * 256 + 256]
                    out_ref[zl, 0, core, c, plane, 0] = piece.reshape(16, 256).astype(BF)


def solve_kernel(n_ref, v_ref, p_ref, w_ref, class_ref, keep_ref, out_ref, right):
    for group in range(8):
        rows = []
        for c in range(3):
            both = [
                n_ref[group, c, :, :, :, t * 128 : t * 128 + 128].reshape(128, 128) for t in range(2)
            ]
            rows.append(jnp.concatenate(both, axis=0))
        moved = dot(p_ref[...], jnp.concatenate(rows, axis=1))
        for c in range(3):
            part = moved[:, c * 128 : c * 128 + 128].reshape(16, 16, 128)
            keep = keep_ref[...]
            kept = part * jnp.concatenate([keep, keep], axis=1)
            old = v_ref[c, :, group * 16 : group * 16 + 16, :].astype(jnp.float32)
            right[:, group * 16 : group * 16 + 16, c * 128 : c * 128 + 128] = (old + kept).astype(BF)

    def one(k, _):
        applied = dot(w_ref[...], right[k]).reshape(NCLASS, 16, 8, 384)
        classes = class_ref[k]
        classes = jnp.concatenate([classes] * 3, axis=1)
        total = applied[0]
        for index in range(1, NCLASS):
            total = jnp.where((classes == index)[None], applied[index], total)
        for c in range(3):
            out_ref[c, k] = total[:, :, c * 128 : c * 128 + 128].reshape(128, 128)
        return 0

    lax.fori_loop(0, 16, one, 0)


def params():
    return pltpu.CompilerParams(vmem_limit_bytes=VMEM)


def body(velocity, inverses, class_index, keep_count):
    scale_x = (0.5 / math.sqrt(KX * KZ)) ** 2 / PX
    scale_z = 2.0 * math.sqrt(KX * KZ) / PZ
    z_basis = jnp.asarray(z_table())
    x_synth, x_fold = (jnp.asarray(t) for t in x_tables())
    mover = pack_matrix()
    lines = velocity.reshape(3, 16, NY, 2, 2, 128).transpose(0, 1, 2, 4, 3, 5).reshape(3, 16, 128, 128)
    packed = pl.pallas_call(
        pack_kernel,
        out_shape=jax.ShapeDtypeStruct((8, 3, 4, 2, 16, 256), BF),
        compiler_params=params(),
        name="pack",
    )(lines, jnp.asarray(mover))
    column = lax.all_to_all(packed, COLUMN, split_axis=0, concat_axis=0, tiled=True)
    spread = pl.pallas_call(
        synth_kernel,
        grid=(2, 2),
        in_specs=[
            pl.BlockSpec((8, 3, 4, 2, 16, 256), lambda r, q: (0,) * 6),
            pl.BlockSpec((2 * KZ, 768), lambda r, q: (0, r * 2 + q)),
        ],
        out_specs=pl.BlockSpec((4, 2, 3, 1, 32, 384), lambda r, q: (0, q, 0, r, 0, 0)),
        out_shape=jax.ShapeDtypeStruct((4, 4, 3, 2, 32, 384), BF),
        scratch_shapes=[pltpu.VMEM((384, 2 * KZ), BF)],
        compiler_params=params(),
        name="synth",
    )(column, z_basis)
    planes = lax.all_to_all(spread.reshape(16, 3, 2, 32, 384), PLANE, split_axis=0, concat_axis=0, tiled=True)
    folded = pl.pallas_call(
        functools.partial(middle_kernel, scale=scale_x),
        out_shape=jax.ShapeDtypeStruct((16, 3, 2, 32, 384), BF),
        scratch_shapes=[pltpu.VMEM((3, 2, HALF, 384), BF)],
        compiler_params=params(),
        name="middle",
    )(planes, x_synth, x_fold)
    pieces = lax.all_to_all(folded, PLANE, split_axis=0, concat_axis=0, tiled=True)
    nonlinear = pl.pallas_call(
        functools.partial(analyse_kernel, scale=scale_z),
        grid=(2, 2),
        in_specs=[
            pl.BlockSpec((16, 3, 2, 32, 384), lambda r, h: (0,) * 5),
            pl.BlockSpec((512, 2 * PZ), lambda r, h: (r * 2 + h, 0)),
        ],
        out_specs=pl.BlockSpec((2, 1, 2, 3, 4, 1, 16, 256), lambda r, h: (0, h, 0, 0, 0, r, 0, 0)),
        out_shape=jax.ShapeDtypeStruct((2, 2, 2, 3, 4, 2, 16, 256), BF),
        scratch_shapes=[pltpu.VMEM((384, 2 * PZ), BF)],
        compiler_params=params(),
        name="analyse",
    )(pieces, z_basis)
    returned = lax.all_to_all(
        nonlinear.reshape(8, 3, 4, 2, 16, 256), COLUMN, split_axis=0, concat_axis=0, tiled=True
    )

    kz_here = (lax.axis_index("zh") * 2 + lax.axis_index("core")) * 256 + jnp.arange(256, dtype=jnp.int32)
    wavenumber = jnp.where(kz_here < KZ // 2, kz_here, kz_here - KZ)
    wide = lax.axis_index("x") * 8 + lax.axis_index("zl") * 4 + lax.axis_index("y")
    kx_here = wide * 16 + jnp.arange(16, dtype=jnp.int32)
    mean_mode = (kx_here[:, None] == 0) & (wavenumber[None, :] == 0)
    keep_mask = (jnp.abs(wavenumber)[None, :] < keep_count[:, None]) & jnp.logical_not(mean_mode)

    def by_row(values):
        halves = values.reshape(16, 1, 2, 1, 128)
        return jnp.broadcast_to(halves, (16, 2, 2, 2, 128)).reshape(16, 8, 128)

    keep = by_row(jnp.where(keep_mask, 0.5, 0.0).astype(jnp.float32))
    classes = by_row(class_index)
    operators = jnp.einsum("nyz,ab->nyazb", inverses, jnp.eye(4, dtype=BF))
    operators = operators.reshape(NCLASS * 128, 128)
    solved = pl.pallas_call(
        solve_kernel,
        out_shape=jax.ShapeDtypeStruct((3, 16, 128, 128), jnp.float32),
        scratch_shapes=[pltpu.VMEM((16, 128, 384), BF)],
        compiler_params=params(),
        name="solve",
    )(returned, lines, jnp.asarray(mover.T), operators, classes, keep)
    return solved.reshape(3, 16, NY, 2, 2, 128).transpose(0, 1, 2, 4, 3, 5).reshape(3, 16, NY, 2, 256)


def solution(mesh):
    fine = Mesh(mesh.devices.reshape(4, 2, 4, 2, 2), ("x", "zl", "y", "zh", "core"))
    wide, narrow = ("x", "zl", "y"), ("zh", "core")
    in_specs = (P(None, wide, None, None, narrow), P(), P(wide, narrow), P(wide))
    out_specs = P(None, wide, None, None, narrow)
    return jax.shard_map(body, mesh=fine, in_specs=in_specs, out_specs=out_specs, check_vma=False)
```

time: 294 us -> 170 us (0.58); the launches traced: 288 us -> 169 us
  matrix products: 51.2 us -> 0 us
  Pallas kernels: 0 us -> 42.6 us
  other arithmetic: 45.7 us -> 4.16 us
  waiting for transfers between devices: 35.1 us -> 0.01 us
  local copies, waits for them, and re-layouts: 51.8 us -> 18.2 us
  blocking collectives: 86.7 us -> 97.4 us
  starting transfers between devices: 17.2 us -> 6.97 us
    dot_general x12 -> x0, matrix products: 51.2 us -> none  [the longest x1 16.8 us: body(): jnp.dot(planes.reshape(-1, 2 * KZ), z_basis, preferred_element_type=jnp.f...]
    pallas_call x0 -> x5, Pallas kernels: none -> 42.6 us  [the longest x1 10.1 us: body(): pl.pallas_call(functools.partial(analyse_kernel, scale=scale_z), grid=(2,...]
    all_to_all x3 -> x1, waiting for transfers between devices: 35.1 us -> 0.01 us  [body(): lax.all_to_all(nonlinear.reshape(8, 3, 4, 2, 16, 256), COLUMN, split_axis...]
    another operation x1, other arithmetic: 29.5 us -> 0.01 us
    all_to_all x9 -> x0, local copies, waits for them, and re-layouts: 17.2 us -> none  [the longest x1 5.39 us: body(): lax.all_to_all(spread, 'narrow', split_axis=4, concat_axis=1, tiled=True)]
    neg x1 -> x0, other arithmetic: 14 us -> none  [x_tables(): basis = jnp.stack([jnp.cos(angles), -jnp.sin(angles)], axis=1)]
    all_to_all x3, blocking collectives: 86.7 us -> 97.4 us  [the longest x1 37 us: body(): lax.all_to_all(spread.reshape(16, 3, 2, 32, 384), PLANE, split_axis=0, co...]
    all_to_all x3 -> x1, starting transfers between devices: 17.2 us -> 6.97 us  [body(): lax.all_to_all(nonlinear.reshape(8, 3, 4, 2, 16, 256), COLUMN, split_axis...]
  transfers between devices with their start and end apart: 3 -> 1, of which waited for: 2 -> 0; matrix products, arithmetic and copies ran while one was open for 15% -> 12% of each run, Pallas kernels for 0% -> 0%
where the time goes in v1:
time: 170 us; the launch traced here: 169 us
  blocking collectives  97.4 us (57%)
  Pallas kernels  42.6 us (25%)
  local copies, waits for them, and re-layouts  18.2 us (11%)
  starting transfers between devices  6.97 us (4%)
  other arithmetic  4.16 us (2%)
    all_to_all x1, blocking collectives, body(): lax.all_to_all(spread.reshape(16, 3, 2, 32, 384), PLANE, split_axis=0, co...  37 us
    all_to_all x1, blocking collectives, body(): lax.all_to_all(folded, PLANE, split_axis=0, concat_axis=0, tiled=True)  33 us
    all_to_all x1, blocking collectives, body(): lax.all_to_all(packed, COLUMN, split_axis=0, concat_axis=0, tiled=True)  27.4 us
    reshape x1, local copies, waits for them, and re-layouts, body(): operators = operators.reshape(NCLASS * 128, 128)  16.8 us
    pallas_call x1, Pallas kernels, body(): pl.pallas_call(functools.partial(analyse_kernel, scale=scale_z), grid=(2,...  10.1 us
    pallas_call x1, Pallas kernels, body(): pl.pallas_call(solve_kernel, out_shape=jax.ShapeDtypeStruct((3, 16, 128,...  9.99 us
    pallas_call x1, Pallas kernels, body(): pl.pallas_call(synth_kernel, grid=(2, 2), in_specs=[pl.BlockSpec((8, 3, 4...  9.89 us
    pallas_call x1, Pallas kernels, body(): pl.pallas_call(functools.partial(middle_kernel, scale=scale_x), out_shape...  9.37 us
  transfers between devices with their start and end apart: 1, of which 0 were waited for; matrix products, arithmetic and copies ran while one was open for 12% of the time, Pallas kernels for 0%

profile of v1, /device:TPU:1, one launch (start us, length us, event | category | flops | bytes accessed | tf_op | source)
XLA Modules:
  0.0 169.4 jit_solution(4711423686703921145)
XLA Ops:
  0.0 3.2 %pack.1 = bf16[8,3,4,2,16,256]{5,4,3,2,1,0:T(8,128)(2,1)} custom-call(bf16[3,16,128,128]{3,2,1,0:T(8,128)(2,1)} %bitcast.19, bf16[256,256]{1,0:T(8,128)(2,1)} %constant.57.clone.p_ref), custom_call_target="tpu_custom_call" | custom-call | tf_op jit(solution)/shard_map/pack/pallas_call | solution.py:186
  3.2 27.4 %all_to_all.20.r_ref = bf16[8,3,4,2,16,256]{5,4,3,2,1,0:T(8,128)(2,1)} all-to-all(bf16[8,3,4,2,16,256]{5,4,3,2,1,0:T(8,128)(2,1)} %pack.1), channel_id=1, replica_groups=mesh['x'=4,'zl'=2,'y'=4,'zh'=2,'core'=2] {'zl','zh','core'}, dimensions={0} | all-to-all | bytes 3145728 | tf_op jit(solution)/shard_map/all_to_all | solution.py:192
  30.7 9.9 %synth.1 = bf16[4,4,3,2,32,384]{5,4,3,2,1,0:T(8,128)(2,1)} custom-call(bf16[8,3,4,2,16,256]{5,4,3,2,1,0:T(8,128)(2,1)} %all_to_all.20.r_ref, bf16[2048,3072]{1,0:T(8,128)(2,1)} %constant.54.clone.table_ref), custom_call_target="tpu_custom_call" | custom-call | tf_op jit(solution)/shard_map/synth/pallas_call | solution.py:193
  40.6 37.0 %all_to_all.21.d_ref = bf16[16,3,2,32,384]{4,3,2,1,0:T(8,128)(2,1)} all-to-all(bf16[16,3,2,32,384]{4,3,2,1,0:T(8,128)(2,1)} %bitcast.18), channel_id=1, replica_groups=mesh['x'=4,'zl'=2,'y'=4,'zh'=2,'core'=2] {'x','y'}, dimensions={0} | all-to-all | bytes 4718592 | tf_op jit(solution)/shard_map/all_to_all | solution.py:206
  77.6 9.4 %middle.1 = bf16[16,3,2,32,384]{4,3,2,1,0:T(8,128)(2,1)} custom-call(bf16[16,3,2,32,384]{4,3,2,1,0:T(8,128)(2,1)} %all_to_all.21.d_ref, bf16[2,768,512]{2,1,0:T(8,128)(2,1)} %constant.55.clone.synth_ref, bf16[2,512,768]{2,1,0:T(8,128)(2,1)} %constant.56.clone.fold_ref), custom_call_target="tpu_custom_call" | custom-call | tf_op jit(solution)/shard_map/middle/pallas_call | solution.py:207
  86.9 33.0 %all_to_all.22.b_ref = bf16[16,3,2,32,384]{4,3,2,1,0:T(8,128)(2,1)} all-to-all(bf16[16,3,2,32,384]{4,3,2,1,0:T(8,128)(2,1)} %middle.1), channel_id=1, replica_groups=mesh['x'=4,'zl'=2,'y'=4,'zh'=2,'core'=2] {'x','y'}, dimensions={0} | all-to-all | bytes 4718592 | tf_op jit(solution)/shard_map/all_to_all | solution.py:214
  119.9 10.1 %analyse.1 = bf16[2,2,2,3,4,2,16,256]{7,6,5,4,3,2,1,0:T(8,128)(2,1)} custom-call(bf16[16,3,2,32,384]{4,3,2,1,0:T(8,128)(2,1)} %all_to_all.22.b_ref, bf16[2048,3072]{1,0:T(8,128)(2,1)} %constant.54.clone.table_ref), custom_call_target="tpu_custom_call" | custom-call | tf_op jit(solution)/shard_map/analyse/pallas_call | solution.py:215
  130.0 0.0 copy-start.1
  130.0 7.0 %all-to-all-start.3 = ((bf16[8,3,4,2,16,256]{5,4,3,2,1,0:T(8,128)(2,1)}), bf16[8,3,4,2,16,256]{5,4,3,2,1,0:T(8,128)(2,1)S(1)}, u32[]{:S(2)}, u32[]{:S(2)}) async-start(bf16[8,3,4,2,16,256]{5,4,3,2,1,0:T(8,128)(2,1)} %bitcast.21), calls=%async_computation.3 | async-start | bytes 3145728 | tf_op jit(solution)/shard_map/all_to_all | solution.py:228
  137.0 0.0 copy-done.1
  137.0 4.0 %multiply_bitcast_fusion = bf16[8,32,4,32,4]{4,3,2,1,0:T(8,128)(2,1)} fusion(bf16[8,32,32]{2,1,0:T(8,128)(2,1)S(1)} %copy-done.1, bf16[4,4]{1,0:T(4,128)(2,1)S(1)} %fusion), kind=kLoop, calls=%fused_computation | loop fusion | flops 131072 | bytes 278560 | tf_op jit(solution)/shard_map/nyz,ab->nyazb/transpose | solution.py:245
  141.0 0.0 copy-start.2
  141.0 0.0 copy-start.3
  141.0 16.8 %reshape.83.w_ref = bf16[1024,128]{1,0:T(8,128)(2,1)} reshape(bf16[8,32,4,32,4]{4,3,2,1,0:T(8,128)(2,1)} %multiply_bitcast_fusion) | data formatting | bytes 524288 | tf_op jit(solution)/shard_map/reshape | solution.py:246
  157.8 0.0 copy-done.2
  157.9 0.0 copy-done.3
  157.9 0.1 and_select_fusion
  158.0 0.0 all-to-all-done.3.n_ref
  158.0 0.0 copy-start
  158.0 0.7 broadcast_in_dim.25
  158.7 0.6 broadcast_in_dim.28
  159.4 0.0 copy-done
  159.4 10.0 %solve.1 = f32[3,16,128,128]{3,2,1,0:T(8,128)} custom-call(bf16[8,3,4,2,16,256]{5,4,3,2,1,0:T(8,128)(2,1)} %copy-done, bf16[3,16,128,128]{3,2,1,0:T(8,128)(2,1)} %bitcast.20, bf16[256,256]{1,0:T(8,128)(2,1)} %constant.58.clone.p_ref, bf16[1024,128]{1,0:T(8,128)(2,1)} %reshape.83.w_ref, s32[16,8,128]{2,1,0:T(8,128)} %bitcast.22, f32[16,8,128]{2,1,0:T(8,128)} %bitcast.23), custom_call_target="tpu_custom_call" | custom-call | tf_op jit(solution)/shard_map/solve/pallas_call | solution.py:247
  (5 shorter events, 0.1 us)
Async XLA Ops:
  130.0 7.0 %copy-start.1 = (bf16[8,32,32]{2,1,0:T(8,128)(2,1)S(1)}, bf16[8,32,32]{2,1,0:T(8,128)(2,1)}, u32[]{:S(2)}) copy-start(bf16[8,32,32]{2,1,0:T(8,128)(2,1)} %param.10) | copy-start | bytes 49156
  130.0 28.0 %all-to-all-start.3 = ((bf16[8,3,4,2,16,256]{5,4,3,2,1,0:T(8,128)(2,1)}), bf16[8,3,4,2,16,256]{5,4,3,2,1,0:T(8,128)(2,1)S(1)}, u32[]{:S(2)}, u32[]{:S(2)}) async-start(bf16[8,3,4,2,16,256]{5,4,3,2,1,0:T(8,128)(2,1)} %bitcast.21), calls=%async_computation.3 | async-start | bytes 3145728 | tf_op jit(solution)/shard_map/all_to_all | solution.py:228
  141.0 16.8 %copy-start.2 = (s32[16,256]{1,0:T(8,128)S(1)}, s32[16,256]{1,0:T(8,128)}, u32[]{:S(2)}) copy-start(s32[16,256]{1,0:T(8,128)} %param.11) | copy-start | bytes 49156
  141.0 16.9 %copy-start.3 = (s32[16]{0:T(128)S(1)}, s32[16]{0:T(128)}, u32[]{:S(2)}) copy-start(s32[16]{0:T(128)} %param.12) | copy-start | bytes 196
  158.0 1.3 copy-start

commit v2 on v0

v2 whole, which is shorter than its diff:
```python
import functools
import math

import jax
import jax.numpy as jnp
import ml_dtypes
import numpy as np
from jax import lax
from jax.experimental import pallas as pl
from jax.experimental.pallas import tpu as pltpu
from jax.sharding import Mesh
from jax.sharding import PartitionSpec as P

KX = 512
KZ = 1024
NCLASS = 8
PX = 1536
PZ = 1536
HALF = PX // 2
NY = 32
BF = jnp.bfloat16
VMEM = 28 * 1024 * 1024
COLUMN = ("zl", "zh")
ORDER = (1, 0, 2)

def angles(wavenumbers, points, period):
    phases = (wavenumbers[:, None] * points[None, :]) % period
    scaled = np.float32(2.0 * math.pi / period) * phases.astype(np.float32)
    return scaled.astype(np.float64)


def z_tables():
    tables = []
    for parity in range(2):
        index = np.arange(parity, KZ, 2)
        wavenumber = np.where(index < KZ // 2, index, index - KZ)
        theta = angles(wavenumber, np.arange(HALF), PZ)
        tables.append(np.stack([np.cos(theta), np.sin(theta)]))
    return np.stack(tables).astype(np.float32).astype(ml_dtypes.bfloat16)


def x_tables():
    x, y, zl, i = np.meshgrid(np.arange(4), np.arange(4), np.arange(2), np.arange(8), indexing="ij")
    synth, fold = [], []
    for parity in range(2):
        kx = (x * 8 + zl * 4 + y) * 16 + 2 * i + parity
        theta = angles(kx.reshape(-1), np.arange(HALF), PX).reshape(4, 4, 2, 8, HALF)
        basis = np.stack([np.cos(theta), -np.sin(theta)], axis=2).astype(np.float32)
        weight = np.where(kx == 0, 1.0, 2.0).astype(np.float32)[:, :, None, :, :, None]
        synth.append((weight * basis).reshape(512, HALF).T)
        fold.append(basis.reshape(512, HALF))
    return (
        np.stack(synth).astype(ml_dtypes.bfloat16),
        np.stack(fold).astype(ml_dtypes.bfloat16),
    )


def mover(turned):
    row, column = (lax.broadcasted_iota(jnp.int32, (256, 256), axis) for axis in (turned, 1 - turned))
    kx = ((row & 7) << 1) | ((row >> 3) & 1)
    source = (kx << 4) | (((row >> 5) & 3) << 2) | ((row >> 7) << 1) | ((row >> 4) & 1)
    return (column == source).astype(jnp.float32).astype(BF)


def sorter(turned):
    row, column = (lax.broadcasted_iota(jnp.int32, (256, 256), axis) for axis in (turned, 1 - turned))
    return (row == (((column & 127) << 1) | (column >> 7))).astype(jnp.float32).astype(BF)


def wait(copies):
    for copy in copies:
        copy.wait()


def dot(a, b):
    return jnp.dot(a, b, preferred_element_type=jnp.float32)


def place_kernel(inv_ref, w_ref):
    row, column = (lax.broadcasted_iota(jnp.int32, (128, 128), axis) for axis in range(2))
    same = row % 4 == column % 4
    tall = (row[:, :32] // 4 == column[:, :32]).astype(BF)
    wide = (lax.broadcasted_iota(jnp.int32, (32, 128), 0) == lax.broadcasted_iota(jnp.int32, (32, 128), 1) // 4).astype(BF)
    for index in range(NCLASS):
        rows = dot(tall, inv_ref[index]).astype(BF)
        w_ref[:, index * 128 : index * 128 + 128] = jnp.where(same, dot(rows, wide), 0.0).astype(BF)


def cut_kernel(pos, v_hbm, o0, o1, o2, sems):
    copies = []
    for c, out in enumerate((o0, o1, o2)):
        for z in range(4):
            first = pl.multiple_of(z * 32 + (1 - pos[3]) * 16, 16)
            copies.append(pltpu.make_async_copy(v_hbm.at[c, :, pl.ds(first, 16)], out.at[z], sems.at[c, z]))
            copies[-1].start()
    wait(copies)


def pack_kernel(pos, v_hbm, *refs, parts, preload):
    nc = len(parts)
    other_refs, refs = refs[:nc], refs[nc:]
    if preload:
        table_hbm, refs = refs[0], refs[1:]
    outs, refs = refs[:4], refs[4:]
    if preload:
        table_ref, refs = refs[0], refs[1:]
    v_ref, sems = refs
    copies = []
    for i, c in enumerate(parts):
        for z in range(4):
            first = pl.multiple_of(z * 32 + pos[3] * 16, 16)
            copies.append(pltpu.make_async_copy(v_hbm.at[c, :, pl.ds(first, 16)], v_ref.at[i, z], sems.at[4 * i + z]))
            copies[-1].start()
    if preload:
        table_copy = pltpu.make_async_copy(table_hbm, table_ref, sems.at[4 * nc])
        table_copy.start()
    move, sort = mover(0), sorter(0)
    wait(copies)
    places = [(step, core) for step in range(4) for core in range(2)]
    parts = []
    for step, core in places:
        z = lax.rem(pos[2] + step, 4)
        parts += [(other_refs[i] if core else v_ref.at[i])[z].reshape(256, 128) for i in range(nc)]
    moved = dot(move, jnp.concatenate(parts, axis=1)).astype(BF)
    parts = []
    for i in range(8 * nc):
        part = moved[:, i * 128 : i * 128 + 128]
        parts.append(jnp.concatenate([part[:128], part[128:]], axis=1))
    moved = dot(jnp.concatenate(parts, axis=0), sort).astype(BF)
    for i, (step, core) in enumerate(places):
        outs[step][core] = moved[i * nc * 128 : (i + 1) * nc * 128].reshape(nc, 4, 2, 16, 256)
    if preload:
        table_copy.wait()


def gather_kernel(b0, b1, b2, b3, *rest):
    out_ref = rest[-1]
    for step, block in enumerate((b0, b1, b2, b3)):
        out_ref[step] = block[1]


def z_copies(table_hbm, table_ref, sems):
    return [pltpu.make_async_copy(table_hbm.at[p], table_ref.at[p], sems.at[p]) for p in range(2)]


def synth_kernel(pos, r0, r1, r2, r3, table, out_ref, lhs, *rest, nc):
    table_ref = table
    if rest:
        table_ref, sems = rest
        copies = z_copies(table, table_ref, sems)
        for copy in copies:
            copy.start()
    for step, block in enumerate((r0, r1, r2, r3)):
        z = lax.rem(pos[2] + 4 - step, 4)
        for core in range(2):
            quarter = (z // 2) * 2 + lax.rem(pos[3] + core, 2)
            lanes = pl.ds(pl.multiple_of(quarter * 128, 128), 128)
            for ri in range(2):
                rows = pl.ds(pl.multiple_of(ri * (128 * nc) + lax.rem(z, 2) * (64 * nc), 64), 64 * nc)
                part = block[core, :, :, ri].reshape(64 * nc, 256)
                for parity in range(2):
                    lhs[parity, rows, lanes] = part[:, parity * 128 : parity * 128 + 128]
    if rest:
        wait(copies)
    n = 128 * nc
    sums = []
    for parity in range(2):
        by_cos = dot(lhs[parity], table_ref[parity, 0])
        by_sin = dot(lhs[parity], table_ref[parity, 1])
        sums.append((by_cos[:n] - by_sin[n:], by_sin[:n] + by_cos[n:]))
    for ri in range(2):
        even, odd = sums[0][ri], sums[1][ri]
        for half, both in enumerate((even + odd, even - odd)):
            part = both.reshape(2, nc, 4, 2, 8, HALF)
            for plane in range(4):
                for c in range(nc):
                    mixed = [part[zl, c, plane, parity] for parity in range(2) for zl in range(2)]
                    mixed = jnp.concatenate(mixed, axis=0).astype(BF)
                    for quarter in range(2):
                        out_ref[plane * 4 + half * 2 + quarter, c, ri] = mixed[:, quarter * 384 : quarter * 384 + 384]


def middle_kernel(d_ref, *rest, scale, nc, first):
    if first:
        synth_hbm, fold_hbm, *outs, wall_ref, data, prod, synth_ref, fold_ref, sems = rest
    else:
        wall_ref, synth_hbm, fold_hbm, *outs, data, prod, synth_ref, fold_ref, sems = rest
    synth_copy = pltpu.make_async_copy(synth_hbm, synth_ref, sems.at[0])
    fold_copy = pltpu.make_async_copy(fold_hbm, fold_ref, sems.at[1])
    synth_copy.start()
    for parity in range(2):
        for c in range(nc):
            part = d_ref[:, c, :, parity * 16 : parity * 16 + 16, :].reshape(512, 384)
            data[parity, :, c * 384 : c * 384 + 384] = part
    synth_copy.wait()
    fold_copy.start()
    for step in range(3):
        rows = slice(step * 256, step * 256 + 256)
        even = dot(synth_ref[0, rows, :], data[0])
        odd = dot(synth_ref[1, rows, :], data[1])
        low, high = even + odd, even - odd
        if first:
            wall_ref[0, rows, :] = low
            wall_ref[1, rows, :] = high
        for c in range(nc):
            lanes = slice(c * 384, c * 384 + 384)
            if first:
                one, two = low * low, high * high
            else:
                one, two = low[:, lanes] * wall_ref[0, rows, :], high[:, lanes] * wall_ref[1, rows, :]
            prod[0, rows, lanes] = (one + two).astype(BF)
            prod[1, rows, lanes] = (one - two).astype(BF)
    fold_copy.wait()
    for parity in range(2):
        spectra = (dot(fold_ref[parity], prod[parity]) * scale).astype(BF)
        for c in range(nc):
            part = spectra[:, c * 384 : c * 384 + 384].reshape(16, 2, 16, 384)
            outs[c][:, 0, :, parity * 16 : parity * 16 + 16, :] = part


def analyse_kernel(pos, b_ref, table_hbm, o0, o1, o2, o3, lhs, modes, table_ref, sems, *, scale, nc):
    copies = z_copies(table_hbm, table_ref, sems)
    for copy in copies:
        copy.start()
    n = 128 * nc
    for plane in range(4):
        for quarter in range(2):
            for ri in range(2):
                low = b_ref[plane * 4 + quarter, :, ri].reshape(32 * nc, 384).astype(jnp.float32)
                high = b_ref[plane * 4 + quarter + 2, :, ri].reshape(32 * nc, 384).astype(jnp.float32)
                rows = slice(ri * n + plane * 32 * nc, ri * n + plane * 32 * nc + 32 * nc)
                lanes = slice(quarter * 384, quarter * 384 + 384)
                lhs[0, rows, lanes] = (low + high).astype(BF)
                lhs[1, rows, lanes] = (low - high).astype(BF)
    for parity in range(2):
        copies[parity].wait()
        by_cos, by_sin = (
            lax.dot_general(
                lhs[parity], table_ref[parity, i], (((1,), (1,)), ((), ())), preferred_element_type=jnp.float32
            )
            for i in range(2)
        )
        for ri, spectra in enumerate((by_cos[:n] + by_sin[n:], by_cos[n:] - by_sin[:n])):
            part = (spectra * scale).reshape(4, nc, 2, 2, 8, 512)
            for zl in range(2):
                for quarter in range(4):
                    for plane in range(4):
                        for c in range(nc):
                            piece = part[plane, c, :, zl, :, quarter * 128 : quarter * 128 + 128]
                            block = (quarter // 2) * 2 + zl
                            lanes = slice(parity * 128, parity * 128 + 128)
                            modes[block, quarter % 2, c, plane, ri, :, lanes] = piece.reshape(16, 128).astype(BF)
    for step, out in enumerate((o0, o1, o2, o3)):
        for other in range(2):
            out[other] = modes[lax.rem(pos[2] + step, 4), lax.rem(pos[3] + other, 2)]


def solve_kernel(pos, count_ref, n0, n1, n2, n3, other_ref, v_ref, w_ref, class_ref, *rest, c, place):
    out_ref, right, done, sems = rest[-4:]
    move, sort = mover(1), sorter(1)
    row = lax.broadcasted_iota(jnp.int32, (16, 16, 128), 1)
    kx = lax.broadcasted_iota(jnp.int32, (16, 16, 128), 0)
    lane = lax.broadcasted_iota(jnp.int32, (16, 16, 128), 2)
    index = ((pos[2] // 2) * 2 + pos[3]) * 256 + lane + 128 * (lax.rem(row, 4) // 2)
    wavenumber = jnp.where(index < KZ // 2, index, index - KZ)
    counts = jnp.concatenate([jnp.full((1, 16, 128), count_ref[k], jnp.int32) for k in range(16)], axis=0)
    mean = (kx + pos[4] == 0) & (wavenumber == 0)
    half = jnp.where((jnp.abs(wavenumber) < counts) & jnp.logical_not(mean), 0.5, 0.0).astype(jnp.float32)
    own = (n0, n1, n2, n3)
    places = [(step, other) for step in range(4) for other in range(2)]
    parts = [other_ref[step, place] if other else own[step][0, place] for step, other in places]
    both = dot(jnp.concatenate([part.reshape(128, 256) for part in parts], axis=0), sort).astype(BF)
    both = [both[i * 128 : i * 128 + 128] for i in range(8)]
    both = [jnp.concatenate([part[:, :128], part[:, 128:]], axis=0) for part in both]
    moved = dot(move, jnp.concatenate(both, axis=1))
    for i, (step, other) in enumerate(places):
        group = lax.rem(pos[2] + 4 - step, 4) * 2 + lax.rem(pos[3] + other, 2)
        rows = pl.ds(pl.multiple_of(group * 16, 16), 16)
        old = v_ref[c, :, rows, :].astype(jnp.float32)
        new = (old + moved[:, i * 128 : i * 128 + 128].reshape(16, 16, 128) * half).astype(BF)
        for k in range(16):
            right[k // 2, rows, (k % 2) * 128 : (k % 2) * 128 + 128] = new[k]

    early = (lax.broadcasted_iota(jnp.int32, (16, 128), 0) & 3) < 2
    copies = []
    for pair in range(8):
        classes = []
        for k in range(2):
            line = class_ref[pair * 2 + k : pair * 2 + k + 1, :]
            classes.append(jnp.where(early, line[:, :128], line[:, 128:]))
        classes = jnp.concatenate(classes, axis=1)
        line = right[pair].reshape(8, 16, 256)
        masked = []
        for index in range(NCLASS):
            chosen = (classes == index).astype(jnp.float32).astype(BF)
            masked.append((line * chosen[None]).reshape(128, 256))
        total = dot(w_ref[...], jnp.concatenate(masked, axis=0))
        for k in range(2):
            done[pair * 2 + k] = total[:, k * 128 : k * 128 + 128]
        block = pl.ds(pair * 2, 2)
        copies.append(pltpu.make_async_copy(done.at[block], out_ref.at[c, block], sems.at[pair]))
        copies[-1].start()
    wait(copies)


MICROSECONDS = {
    "cut": 1, "place": 1, "gather": 1, "pack": 3, "solve": 3,
    "synth_first": 3, "synth_second": 40, "middle": 4, "analyse": 4,
}


def cost(name):
    return pl.CostEstimate(flops=MICROSECONDS[name] * 10**9, bytes_accessed=2**20, transcendentals=0)


def params():
    return pltpu.CompilerParams(vmem_limit_bytes=VMEM)


def in_hbm(array):
    return pltpu.with_memory_space_constraint(array, pltpu.HBM)


def spec(memory):
    return pl.BlockSpec(memory_space=memory)


def call(kernel, name, outs, args, tables, scratch, flops, scalars=1):
    specs = [spec(pltpu.SMEM)] * scalars + [spec(pltpu.VMEM)] * (len(args) - scalars) + [spec(pltpu.HBM)] * len(tables)
    return pl.pallas_call(
        kernel,
        in_specs=specs,
        out_specs=[spec(pltpu.VMEM)] * len(outs),
        out_shape=outs,
        scratch_shapes=scratch,
        compiler_params=params(),
        cost_estimate=cost(name),
        name=name,
    )(*args, *tables)


def shift(block, axes, step, size):
    places = [0, 2, 1, 3] if axes == COLUMN else range(size)
    return lax.ppermute(block, axes, [(places[j], places[(j + step) % size]) for j in range(size)])


def along_z(blocks):
    moved = {s: shift(blocks[s], COLUMN, s, 4) for s in (1, 3, 2)}
    return [blocks[0], moved[1], moved[2], moved[3]]


def across(moved, *earlier):
    shape = moved[0].shape[1:]
    other = pl.pallas_call(
        gather_kernel,
        in_specs=[spec(pltpu.VMEM)] * 4 + [spec(pl.ANY)] * len(earlier),
        out_specs=spec(pltpu.VMEM),
        out_shape=jax.ShapeDtypeStruct((4, *shape), BF),
        compiler_params=params(),
        cost_estimate=cost("gather"),
        name="gather",
    )(*moved, *earlier)
    return (*moved, shift(other, "core", 1, 2))


def plane(blocks):
    return lax.all_to_all(blocks, ("x", "y"), split_axis=0, concat_axis=0, tiled=True)


def after(value, *earlier):
    return lax.optimization_barrier((value, *earlier))[0]


def body(velocity, inverses, class_index, keep_count):
    scale_x = (0.5 / math.sqrt(KX * KZ)) ** 2 / PX
    scale_z = 2.0 * math.sqrt(KX * KZ) / PZ
    z_basis, x_synth, x_fold = (in_hbm(jnp.asarray(t)) for t in (z_tables(), *x_tables()))
    z_scratch = [pltpu.VMEM((2, 2, 512, HALF), BF), pltpu.SemaphoreType.DMA((2,))]
    lines = velocity.reshape(3, 16, NY, 2, 2, 128).transpose(0, 1, 2, 4, 3, 5).reshape(3, 16, 128, 128)
    x, y, zl = (lax.axis_index(name) for name in ("x", "y", "zl"))
    pos = jnp.stack([x, y, lax.axis_index("zh") * 2 + zl, lax.axis_index("core"), (x * 8 + zl * 4 + y) * 16])

    def mode_shape(nc):
        return jax.ShapeDtypeStruct((2, nc, 4, 2, 16, 256), BF)

    def plane_shape(nc):
        return jax.ShapeDtypeStruct((16, nc, 2, 32, 384), BF)

    table_shape = pltpu.VMEM((2, 2, 512, HALF), BF)

    def pack(parts, preload):
        nc = len(parts)
        args = [pos, in_hbm(lines), *[others[c] for c in parts]] + [z_basis] * preload
        specs = [spec(pltpu.SMEM), spec(pltpu.HBM)] + [spec(pltpu.VMEM)] * nc + [spec(pltpu.HBM)] * preload
        return pl.pallas_call(
            functools.partial(pack_kernel, parts=parts, preload=preload),
            in_specs=specs,
            out_specs=[spec(pltpu.VMEM)] * (4 + preload),
            out_shape=[mode_shape(nc)] * 4 + [table_shape] * preload,
            scratch_shapes=[pltpu.VMEM((nc, 4, 16, 16, 128), BF), pltpu.SemaphoreType.DMA((4 * nc + 1,))],
            compiler_params=params(),
            cost_estimate=cost("pack"),
            name="pack",
        )(*args)

    def synth(blocks, table):
        nc = blocks[0].shape[1]
        kernel = functools.partial(synth_kernel, nc=nc)
        scratch = [pltpu.VMEM((2, 256 * nc, 512), BF)]
        args, tables = (pos, *blocks), (z_basis,)
        if table is None:
            scratch += z_scratch
        else:
            args, tables = (pos, *blocks, table), ()
        return call(kernel, "synth_first" if table is not None else "synth_second", [plane_shape(nc)], args, tables, scratch, nc * 1.5e9)[0]

    def middle(block, wall=None):
        nc, first = block.shape[1], wall is None
        outs, args = [plane_shape(1)] * nc, (block,)
        if first:
            outs.append(jax.ShapeDtypeStruct((2, HALF, 384), jnp.float32))
        else:
            args = (block, wall)
        scratch = [pltpu.VMEM((2, 512, nc * 384), BF), pltpu.VMEM((2, HALF, nc * 384), BF)]
        scratch += [pltpu.VMEM((2, HALF, 512), BF), pltpu.VMEM((2, 512, HALF), BF), pltpu.SemaphoreType.DMA((2,))]
        kernel = functools.partial(middle_kernel, scale=scale_x, nc=nc, first=first)
        return call(kernel, "middle", outs, args, (x_synth, x_fold), scratch, 2e9, scalars=0)

    def analyse(block):
        nc = block.shape[1]
        scratch = [pltpu.VMEM((2, 256 * nc, HALF), BF), pltpu.VMEM((4, 2, nc, 4, 2, 16, 256), BF), *z_scratch]
        kernel = functools.partial(analyse_kernel, scale=scale_z, nc=nc)
        return call(kernel, "analyse", [mode_shape(nc)] * 4, (pos, block), (z_basis,), scratch, nc * 1.5e9)

    def solve(c, place, blocks, solved):
        args = [pos, keep_count, *blocks, lines, operators, class_index]
        specs = [spec(pltpu.SMEM)] * 2 + [spec(pltpu.VMEM)] * (len(args) - 2)
        aliases = {}
        if solved is not None:
            specs.append(spec(pl.ANY))
            aliases = {len(args): 0}
            args.append(solved)
        return pl.pallas_call(
            functools.partial(solve_kernel, c=c, place=place),
            in_specs=specs,
            out_specs=spec(pl.ANY),
            out_shape=jax.ShapeDtypeStruct((3, 16, 128, 128), jnp.float32),
            scratch_shapes=[
                pltpu.VMEM((8, 128, 256), BF),
                pltpu.VMEM((16, 128, 128), jnp.float32),
                pltpu.SemaphoreType.DMA((8,)),
            ],
            input_output_aliases=aliases,
            compiler_params=params(),
            cost_estimate=cost("solve"),
            name="solve",
        )(*args)

    operators = pl.pallas_call(
        place_kernel,
        out_shape=jax.ShapeDtypeStruct((128, NCLASS * 128), BF),
        compiler_params=params(),
        cost_estimate=cost("place"),
        name="place",
    )(inverses)

    one, two = (1,), (0, 2)
    pieces = pl.pallas_call(
        cut_kernel,
        in_specs=[spec(pltpu.SMEM), spec(pltpu.HBM)],
        out_specs=[spec(pltpu.VMEM)] * 3,
        out_shape=[jax.ShapeDtypeStruct((4, 16, 16, 128), BF)] * 3,
        scratch_shapes=[pltpu.SemaphoreType.DMA((3, 4))],
        compiler_params=params(),
        cost_estimate=cost("cut"),
        name="cut",
    )(pos, in_hbm(lines))
    others = {c: shift(pieces[c], "core", 1, 2) for c in (1, 0, 2)}
    packed_one = pack(one, False)
    *packed_two, table = pack(two, True)
    lines_one = synth(along_z(packed_one), table)
    lines_two = synth(along_z(packed_two), None)
    plane_one = plane(lines_one)
    plane_two = plane(after(lines_two, plane_one))
    folded_v, wall = middle(plane_one)
    folded_u, folded_w = middle(plane_two, wall)
    back_v = plane(after(folded_v, plane_two))
    back_u = plane(after(folded_u, back_v))
    modes_v = analyse(back_v)
    back_w = plane(after(folded_w, back_u, *modes_v))
    modes_u, modes_w = analyse(back_u), analyse(back_w)
    moved_v, moved_u, moved_w = (along_z(modes) for modes in (modes_v, modes_u, modes_w))
    all_v = across(moved_v, modes_u[0])
    solved = solve(1, 0, all_v, None)
    all_u = across(moved_u, modes_w[0])
    solved = solve(0, 0, all_u, solved)
    all_w = across(moved_w, all_u[4])
    solved = solve(2, 0, all_w, solved)
    return solved.reshape(3, 16, NY, 2, 2, 128).transpose(0, 1, 2, 4, 3, 5).reshape(3, 16, NY, 2, 256)


def solution(mesh):
    fine = Mesh(mesh.devices.reshape(4, 2, 4, 2, 2), ("x", "zl", "y", "zh", "core"))
    wide, narrow = ("x", "zl", "y"), ("zh", "core")
    in_specs = (P(None, wide, None, None, narrow), P(), P(wide, narrow), P(wide))
    out_specs = P(None, wide, None, None, narrow)
    return jax.shard_map(body, mesh=fine, in_specs=in_specs, out_specs=out_specs, check_vma=False)
```

time: 294 us -> 141 us (0.48); the launches traced: 288 us -> 140 us
  blocking collectives: 86.7 us -> 0 us
  matrix products: 51.2 us -> 0 us
  local copies, waits for them, and re-layouts: 51.8 us -> 3.17 us
  other arithmetic: 45.7 us -> 0 us
  Pallas kernels: 0 us -> 43.1 us
  starting transfers between devices: 17.2 us -> 53.5 us
  waiting for transfers between devices: 35.1 us -> 39.5 us
    all_to_all x3 -> x0, blocking collectives: 86.7 us -> none  [the longest x1 32.7 us: body(): lax.all_to_all(folded, 'narrow', split_axis=1, concat_axis=4, tiled=True)]
    dot_general x12 -> x0, matrix products: 51.2 us -> none  [the longest x1 16.8 us: body(): jnp.dot(planes.reshape(-1, 2 * KZ), z_basis, preferred_element_type=jnp.f...]
    pallas_call x0 -> x17, Pallas kernels: none -> 43.1 us  [the longest x7 28 us: call(): pl.pallas_call(kernel, in_specs=specs, out_specs=[spec(pltpu.VMEM)] * len...]
    another operation x1 -> x0, other arithmetic: 29.5 us -> none
    ppermute x0 -> x21, starting transfers between devices: none -> 28.8 us  [shift(): lax.ppermute(block, axes, [(places[j], places[(j + step) % size]) for j i...]
    reshape x6 -> x0, local copies, waits for them, and re-layouts: 22.5 us -> none  [the longest x2 14.6 us: body(): spread = spread.astype(jnp.bfloat16).reshape(3, kx_rows, y_local, 2, PZ)]
    all_to_all x9 -> x0, local copies, waits for them, and re-layouts: 17.2 us -> none  [the longest x1 5.39 us: body(): lax.all_to_all(spread, 'narrow', split_axis=4, concat_axis=1, tiled=True)]
    neg x1 -> x0, other arithmetic: 14 us -> none  [x_tables(): basis = jnp.stack([jnp.cos(angles), -jnp.sin(angles)], axis=1)]
  transfers between devices with their start and end apart: 3 -> 26, of which waited for: 2 -> 13; matrix products, arithmetic and copies ran while one was open for 15% -> 0% of each run, Pallas kernels for 0% -> 28%
where the time goes in v2:
time: 141 us; the launch traced here: 140 us
  starting transfers between devices  53.5 us (38%)
  Pallas kernels  43.1 us (31%)
  waiting for transfers between devices  39.5 us (28%)
  local copies, waits for them, and re-layouts  3.17 us (2%)
    all_to_all x5, waiting for transfers between devices, plane(): lax.all_to_all(blocks, ('x', 'y'), split_axis=0, concat_axis=0, tiled=True)  28.8 us
    ppermute x21, starting transfers between devices, shift(): lax.ppermute(block, axes, [(places[j], places[(j + step) % size]) for j i...  28.8 us
    pallas_call x7, Pallas kernels, call(): pl.pallas_call(kernel, in_specs=specs, out_specs=[spec(pltpu.VMEM)] * len...  28 us
    all_to_all x5, starting transfers between devices, plane(): lax.all_to_all(blocks, ('x', 'y'), split_axis=0, concat_axis=0, tiled=True)  24.7 us
    ppermute x21, waiting for transfers between devices, shift(): lax.ppermute(block, axes, [(places[j], places[(j + step) % size]) for j i...  10.7 us
    pallas_call x3, Pallas kernels, solve(): pl.pallas_call(functools.partial(solve_kernel, c=c, place=place), in_spec...  8.04 us
    pallas_call x2, Pallas kernels, pack(): pl.pallas_call(functools.partial(pack_kernel, parts=parts, preload=preloa...  4.85 us
    unnamed x12, local copies, waits for them, and re-layouts  3.09 us
  transfers between devices with their start and end apart: 26, of which 13 were waited for; matrix products, arithmetic and copies ran while one was open for 0% of the time, Pallas kernels for 28%

profile of v2, /device:TPU:1, one launch (start us, length us, event | category | flops | bytes accessed | tf_op | source)
XLA Modules:
  0.0 139.7 jit_solution(12312698065448716295)
XLA Ops:
  0.0 0.1 stack.23.pos
  0.1 1.8 %cut.1 = (bf16[4,16,16,128]{3,2,1,0:T(8,128)(2,1)S(1)}, bf16[4,16,16,128]{3,2,1,0:T(8,128)(2,1)S(1)}, bf16[4,16,16,128]{3,2,1,0:T(8,128)(2,1)S(1)}) custom-call(s32[5]{0:T(128)S(1)} %stack.23.pos, bf16[3,16,128,128]{3,2,1,0:T(8,128)(2,1)} %bitcast.15), custom_call_target="tpu_custom_call" | custom-call | flops 1000000000 | bytes 1048576 | tf_op jit(solution)/shard_map/cut/pallas_call | solution.py:468
  1.9 1.5 %collective-permute-start.5 = (bf16[4,16,16,128]{3,2,1,0:T(8,128)(2,1)S(1)}, bf16[4,16,16,128]{3,2,1,0:T(8,128)(2,1)S(1)}, u32[]{:S(2)}, u32[]{:S(2)}) collective-permute-start(bf16[4,16,16,128]{3,2,1,0:T(8,128)(2,1)S(1)} %get-tuple-element.43), channel_id=1, source_target_pairs={{0,1},{1,0},{2,3},{3,2},{4,5},{5,4},{6,7},{7,6},{8,9},{9,8},{10,11... | collective-permute-start | bytes 786440 | tf_op jit(solution)/shard_map/ppermute | solution.py:344
  3.4 0.1 collective-permute-start
  3.5 0.4 collective-permute-start.1
  3.9 0.7 collective-permute-done.5.refs_0_
  4.6 2.0 %pack.3 = (bf16[2,1,4,2,16,256]{5,4,3,2,1,0:T(8,128)(2,1)S(1)}, bf16[2,1,4,2,16,256]{5,4,3,2,1,0:T(8,128)(2,1)S(1)}, bf16[2,1,4,2,16,256]{5,4,3,2,1,0:T(8,128)(2,1)S(1)}, bf16[2,1,4,2,16,256]{5,4,3,2,1,0:T(8,128)(2,1)S(1)}) custom-call(s32[5]{0:T(128)S(1)} %stack.23.pos, bf16[3,16,128,128]{3,2,1,0:T(8,128)(2,1)} %bitcast.16, ...), custom_call_target="tpu_custom_call" | custom-call | flops 3000000000 | bytes 1048576 | tf_op jit(solution)/shard_map/pack/pallas_call | solution.py:395
  6.6 1.8 %collective-permute-start.6 = (bf16[2,1,4,2,16,256]{5,4,3,2,1,0:T(8,128)(2,1)S(1)}, bf16[2,1,4,2,16,256]{5,4,3,2,1,0:T(8,128)(2,1)S(1)}, u32[]{:S(2)}, u32[]{:S(2)}) collective-permute-start(bf16[2,1,4,2,16,256]{5,4,3,2,1,0:T(8,128)(2,1)S(1)} %get-tuple-element.45), channel_id=1, source_target_pairs={{0,16},{16,2},{2,18},{18,0},{1,17},{17,3},{3,19},{19,1},{4,20},{20... | collective-permute-start | bytes 393224 | tf_op jit(solution)/shard_map/ppermute | solution.py:344
  8.4 3.3 %collective-permute-start.7 = (bf16[2,1,4,2,16,256]{5,4,3,2,1,0:T(8,128)(2,1)S(1)}, bf16[2,1,4,2,16,256]{5,4,3,2,1,0:T(8,128)(2,1)S(1)}, u32[]{:S(2)}, u32[]{:S(2)}) collective-permute-start(bf16[2,1,4,2,16,256]{5,4,3,2,1,0:T(8,128)(2,1)S(1)} %get-tuple-element.46), channel_id=1, source_target_pairs={{0,2},{16,18},{2,0},{18,16},{1,3},{17,19},{3,1},{19,17},{4,6},{20,... | collective-permute-start | bytes 393224 | tf_op jit(solution)/shard_map/ppermute | solution.py:344
  11.7 0.7 collective-permute-start.8
  12.4 0.0 collective-permute-done.refs_0_
  12.5 0.0 collective-permute-done.1.refs_1_
  12.5 2.8 %pack.2 = (bf16[2,2,4,2,16,256]{5,4,3,2,1,0:T(8,128)(2,1)S(1)}, bf16[2,2,4,2,16,256]{5,4,3,2,1,0:T(8,128)(2,1)S(1)}, bf16[2,2,4,2,16,256]{5,4,3,2,1,0:T(8,128)(2...) custom-call(s32[5]{0:T(128)S(1)} %stack.23.pos, bf16[3,16,128,128]{3,2,1,0:T(8,128)(2,1)} %bitcast.17, ...), custom_call_target="tpu_custom_call" | custom-call | flops 3000000000 | bytes 1048576 | tf_op jit(solution)/shard_map/pack/pallas_call | solution.py:395
  15.3 0.8 collective-permute-start.2
  16.1 0.5 collective-permute-start.3
  16.5 0.0 collective-permute-done.6.r1
  16.5 2.0 %collective-permute-start.4 = (bf16[2,2,4,2,16,256]{5,4,3,2,1,0:T(8,128)(2,1)S(1)}, bf16[2,2,4,2,16,256]{5,4,3,2,1,0:T(8,128)(2,1)S(1)}, u32[]{:S(2)}, u32[]{:S(2)}) collective-permute-start(bf16[2,2,4,2,16,256]{5,4,3,2,1,0:T(8,128)(2,1)S(1)} %get-tuple-element.42), channel_id=1, source_target_pairs={{0,18},{16,0},{2,16},{18,2},{1,19},{17,1},{3,17},{19,3},{4,22},{20... | collective-permute-start | bytes 786440 | tf_op jit(solution)/shard_map/ppermute | solution.py:344
  18.6 2.5 %synth_first.1 = bf16[16,1,2,32,384]{4,3,2,1,0:T(8,128)(2,1)} custom-call(s32[5]{0:T(128)S(1)} %stack.23.pos, bf16[2,1,4,2,16,256]{5,4,3,2,1,0:T(8,128)(2,1)S(1)} %get-tuple-element.44.r0, bf16[2,1,4,2,16,256]{5,4,3,2,1,0:T(8,128)(2,1)S(1)} %collective-permute-done.6.r1, bf16[2,1,4,2,16,256]{5,4,3,2,1,0:T(8,128)(2,1)S(1)} %collective-permute-done.7.r2, ...), custom_call_target="tpu_custom_call" | custom-call | flops 3000000000 | bytes 1048576 | tf_op jit(solution)/shard_map/synth_first/pallas_call | solution.py:330
  21.1 6.8 %all-to-all-start = ((bf16[16,1,2,32,384]{4,3,2,1,0:T(8,128)(2,1)}), bf16[16,1,2,32,384]{4,3,2,1,0:T(8,128)(2,1)S(1)}, u32[]{:S(2)}, u32[]{:S(2)}) async-start(bf16[16,1,2,32,384]{4,3,2,1,0:T(8,128)(2,1)} %synth_first.1), calls=%async_computation | async-start | bytes 1572864 | tf_op jit(solution)/shard_map/all_to_all | solution.py:367
  27.8 1.2 collective-permute-done.3.r2
  29.1 0.9 collective-permute-done.4.r3
  30.0 5.6 %synth_second.1 = bf16[16,2,2,32,384]{4,3,2,1,0:T(8,128)(2,1)} custom-call(s32[5]{0:T(128)S(1)} %stack.23.pos, bf16[2,2,4,2,16,256]{5,4,3,2,1,0:T(8,128)(2,1)S(1)} %get-tuple-element.39.r0, bf16[2,2,4,2,16,256]{5,4,3,2,1,0:T(8,128)(2,1)S(1)} %collective-permute-done.2.r1, bf16[2,2,4,2,16,256]{5,4,3,2,1,0:T(8,128)(2,1)S(1)} %collective-permute-done.3.r2, ...), custom_call_target="tpu_custom_call" | custom-call | flops 40000000000 | bytes 1048576 | tf_op jit(solution)/shard_map/synth_second/pallas_call | solution.py:330
  35.5 4.3 %all-to-all-done.d_ref = bf16[16,1,2,32,384]{4,3,2,1,0:T(8,128)(2,1)S(1)} async-done(((bf16[16,1,2,32,384]{4,3,2,1,0:T(8,128)(2,1)}), bf16[16,1,2,32,384]{4,3,2,1,0:T(8,128)(2,1)S(1)}, u32[]{:S(2)}, u32[]{:S(2)}) %all-to-all-start) | async-done | bytes 786464 | tf_op jit(solution)/shard_map/all_to_all | solution.py:367
  39.8 4.5 %all-to-all-start.1 = ((bf16[16,2,2,32,384]{4,3,2,1,0:T(8,128)(2,1)}), bf16[16,2,2,32,384]{4,3,2,1,0:T(8,128)(2,1)S(1)}, u32[]{:S(2)}, u32[]{:S(2)}) async-start(bf16[16,2,2,32,384]{4,3,2,1,0:T(8,128)(2,1)} %synth_second.1), calls=%async_computation.1 | async-start | bytes 3145728 | tf_op jit(solution)/shard_map/all_to_all | solution.py:367
  44.3 4.7 %middle.2 = (bf16[16,1,2,32,384]{4,3,2,1,0:T(8,128)(2,1)}, f32[2,768,384]{2,1,0:T(8,128)S(1)}) custom-call(bf16[16,1,2,32,384]{4,3,2,1,0:T(8,128)(2,1)S(1)} %all-to-all-done.d_ref, bf16[2,768,512]{2,1,0:T(8,128)(2,1)} %constant.34.clone.rest_0_.rest_1_, bf16[2,512,768]{2,1,0:T(8,128)(2,1)} %constant.35.clone.rest_1_.rest_2_), custom_call_target="tpu_custom_call" | custom-call | flops 4000000000 | bytes 1048576 | tf_op jit(solution)/shard_map/middle/pallas_call | solution.py:330
  49.0 0.0 copy-start.4
  49.1 1.4 copy-done.4
  50.5 14.0 %all-to-all-done.1.d_ref = bf16[16,2,2,32,384]{4,3,2,1,0:T(8,128)(2,1)S(1)} async-done(((bf16[16,2,2,32,384]{4,3,2,1,0:T(8,128)(2,1)}), bf16[16,2,2,32,384]{4,3,2,1,0:T(8,128)(2,1)S(1)}, u32[]{:S(2)}, u32[]{:S(2)}) %all-to-all-start.1) | async-done | bytes 1572896 | tf_op jit(solution)/shard_map/all_to_all | solution.py:367
  64.4 5.2 %all-to-all-start.2 = ((bf16[16,1,2,32,384]{4,3,2,1,0:T(8,128)(2,1)}), bf16[16,1,2,32,384]{4,3,2,1,0:T(8,128)(2,1)S(1)}, u32[]{:S(2)}, u32[]{:S(2)}) async-start(bf16[16,1,2,32,384]{4,3,2,1,0:T(8,128)(2,1)} %get-tuple-element.54), calls=%async_computation.2 | async-start | bytes 1572864 | tf_op jit(solution)/shard_map/all_to_all | solution.py:367
  69.7 0.0 copy-start.5
  69.7 1.7 %copy-done.5 = f32[2,768,384]{2,1,0:T(8,128)S(1)} copy-done((f32[2,768,384]{2,1,0:T(8,128)S(1)}, f32[2,768,384]{2,1,0:T(8,128)}, u32[]{:S(2)}) %copy-start.5) | copy-done | bytes 2359320
  71.3 5.5 %middle.3 = (bf16[16,1,2,32,384]{4,3,2,1,0:T(8,128)(2,1)}, bf16[16,1,2,32,384]{4,3,2,1,0:T(8,128)(2,1)}) custom-call(bf16[16,2,2,32,384]{4,3,2,1,0:T(8,128)(2,1)S(1)} %all-to-all-done.1.d_ref, f32[2,768,384]{2,1,0:T(8,128)S(1)} %copy-done.5, bf16[2,768,512]{2,1,0:T(8,128)(2,1)} %constant.34.clone.rest_0_.rest_1_, ...), custom_call_target="tpu_custom_call" | custom-call | flops 4000000000 | bytes 1048576 | tf_op jit(solution)/shard_map/middle/pallas_call | solution.py:330
  76.8 3.3 %all-to-all-done.2.b_ref = bf16[16,1,2,32,384]{4,3,2,1,0:T(8,128)(2,1)S(1)} async-done(((bf16[16,1,2,32,384]{4,3,2,1,0:T(8,128)(2,1)}), bf16[16,1,2,32,384]{4,3,2,1,0:T(8,128)(2,1)S(1)}, u32[]{:S(2)}, u32[]{:S(2)}) %all-to-all-start.2) | async-done | bytes 786464 | tf_op jit(solution)/shard_map/all_to_all | solution.py:367
  80.2 4.7 %all-to-all-start.3 = ((bf16[16,1,2,32,384]{4,3,2,1,0:T(8,128)(2,1)}), bf16[16,1,2,32,384]{4,3,2,1,0:T(8,128)(2,1)S(1)}, u32[]{:S(2)}, u32[]{:S(2)}) async-start(bf16[16,1,2,32,384]{4,3,2,1,0:T(8,128)(2,1)} %get-tuple-element.55), calls=%async_computation.3 | async-start | bytes 1572864 | tf_op jit(solution)/shard_map/all_to_all | solution.py:367
  84.8 0.0 copy-start.1
  84.8 3.2 %analyse.3 = (bf16[2,1,4,2,16,256]{5,4,3,2,1,0:T(8,128)(2,1)S(1)}, bf16[2,1,4,2,16,256]{5,4,3,2,1,0:T(8,128)(2,1)S(1)}, bf16[2,1,4,2,16,256]{5,4,3,2,1,0:T(8,128)(2,1)S(1)}, bf16[2,1,4,2,16,256]{5,4,3,2,1,0:T(8,128)(2,1)S(1)}) custom-call(s32[5]{0:T(128)S(1)} %stack.23.pos, bf16[16,1,2,32,384]{4,3,2,1,0:T(8,128)(2,1)S(1)} %all-to-all-done.2.b_ref, ...), custom_call_target="tpu_custom_call" | custom-call | flops 4000000000 | bytes 1048576 | tf_op jit(solution)/shard_map/analyse/pallas_call | solution.py:330
  88.1 7.2 %all-to-all-done.3.b_ref = bf16[16,1,2,32,384]{4,3,2,1,0:T(8,128)(2,1)S(1)} async-done(((bf16[16,1,2,32,384]{4,3,2,1,0:T(8,128)(2,1)}), bf16[16,1,2,32,384]{4,3,2,1,0:T(8,128)(2,1)S(1)}, u32[]{:S(2)}, u32[]{:S(2)}) %all-to-all-start.3) | async-done | bytes 786464 | tf_op jit(solution)/shard_map/all_to_all | solution.py:367
  95.3 3.6 %all-to-all-start.4 = ((bf16[16,1,2,32,384]{4,3,2,1,0:T(8,128)(2,1)}), bf16[16,1,2,32,384]{4,3,2,1,0:T(8,128)(2,1)S(1)}, u32[]{:S(2)}, u32[]{:S(2)}) async-start(bf16[16,1,2,32,384]{4,3,2,1,0:T(8,128)(2,1)} %get-tuple-element.60), calls=%async_computation.4 | async-start | bytes 1572864 | tf_op jit(solution)/shard_map/all_to_all | solution.py:367
  98.9 0.4 place.1.w_ref
  99.3 0.6 collective-permute-start.17
  99.9 2.0 %collective-permute-start.18 = (bf16[2,1,4,2,16,256]{5,4,3,2,1,0:T(8,128)(2,1)S(1)}, bf16[2,1,4,2,16,256]{5,4,3,2,1,0:T(8,128)(2,1)S(1)}, u32[]{:S(2)}, u32[]{:S(2)}) collective-permute-start(bf16[2,1,4,2,16,256]{5,4,3,2,1,0:T(8,128)(2,1)S(1)} %get-tuple-element.58), channel_id=1, source_target_pairs={{0,2},{16,18},{2,0},{18,16},{1,3},{17,19},{3,1},{19,17},{4,6},{20,... | collective-permute-start | bytes 393224 | tf_op jit(solution)/shard_map/ppermute | solution.py:344
  101.8 0.5 collective-permute-start.19
  102.4 3.2 %analyse.5 = (bf16[2,1,4,2,16,256]{5,4,3,2,1,0:T(8,128)(2,1)S(1)}, bf16[2,1,4,2,16,256]{5,4,3,2,1,0:T(8,128)(2,1)S(1)}, bf16[2,1,4,2,16,256]{5,4,3,2,1,0:T(8,128)(2,1)S(1)}, bf16[2,1,4,2,16,256]{5,4,3,2,1,0:T(8,128)(2,1)S(1)}) custom-call(s32[5]{0:T(128)S(1)} %stack.23.pos, bf16[16,1,2,32,384]{4,3,2,1,0:T(8,128)(2,1)S(1)} %all-to-all-done.3.b_ref, ...), custom_call_target="tpu_custom_call" | custom-call | flops 4000000000 | bytes 1048576 | tf_op jit(solution)/shard_map/analyse/pallas_call | solution.py:330
  105.6 0.2 collective-permute-done.17.b1.n1
  105.8 0.6 collective-permute-done.19.b3.n3
  106.4 6.5 %collective-permute-start.20 = (bf16[4,1,4,2,16,256]{5,4,3,2,1,0:T(8,128)(2,1)S(1)}, bf16[4,1,4,2,16,256]{5,4,3,2,1,0:T(8,128)(2,1)S(1)}, u32[]{:S(2)}, u32[]{:S(2)}) collective-permute-start(bf16[4,1,4,2,16,256]{5,4,3,2,1,0:T(8,128)(2,1)S(1)} %gather.5), channel_id=1, source_target_pairs={{0,1},{1,0},{2,3},{3,2},{4,5},{5,4},{6,7},{7,6},{8,9},{9,8},{10,11... | collective-permute-start | bytes 786440 | tf_op jit(solution)/shard_map/ppermute | solution.py:344
  112.9 0.4 collective-permute-start.12
  113.2 3.2 %collective-permute-start.13 = (bf16[2,1,4,2,16,256]{5,4,3,2,1,0:T(8,128)(2,1)S(1)}, bf16[2,1,4,2,16,256]{5,4,3,2,1,0:T(8,128)(2,1)S(1)}, u32[]{:S(2)}, u32[]{:S(2)}) collective-permute-start(bf16[2,1,4,2,16,256]{5,4,3,2,1,0:T(8,128)(2,1)S(1)} %get-tuple-element.67), channel_id=1, source_target_pairs={{0,2},{16,18},{2,0},{18,16},{1,3},{17,19},{3,1},{19,17},{4,6},{20,... | collective-permute-start | bytes 393224 | tf_op jit(solution)/shard_map/ppermute | solution.py:344
  116.5 3.2 %analyse.4 = (bf16[2,1,4,2,16,256]{5,4,3,2,1,0:T(8,128)(2,1)S(1)}, bf16[2,1,4,2,16,256]{5,4,3,2,1,0:T(8,128)(2,1)S(1)}, bf16[2,1,4,2,16,256]{5,4,3,2,1,0:T(8,128)(2,1)S(1)}, bf16[2,1,4,2,16,256]{5,4,3,2,1,0:T(8,128)(2,1)S(1)}) custom-call(s32[5]{0:T(128)S(1)} %stack.23.pos, bf16[16,1,2,32,384]{4,3,2,1,0:T(8,128)(2,1)S(1)} %all-to-all-done.4.b_ref, ...), custom_call_target="tpu_custom_call" | custom-call | flops 4000000000 | bytes 1048576 | tf_op jit(solution)/shard_map/analyse/pallas_call | solution.py:330
  119.7 0.0 copy-start
  119.7 0.0 copy-start.2
  119.7 0.0 copy-start.3
  119.8 3.1 %collective-permute-done.13.b2.n2 = bf16[2,1,4,2,16,256]{5,4,3,2,1,0:T(8,128)(2,1)S(1)} collective-permute-done((bf16[2,1,4,2,16,256]{5,4,3,2,1,0:T(8,128)(2,1)S(1)}, bf16[2,1,4,2,16,256]{5,4,3,2,1,0:T(8,128)(2,1)S(1)}, u32[]{:S(2)}, u32[]{:S(2)}) %collective-permute-start.13) | collective-permute-done | bytes 131104 | tf_op jit(solution)/shard_map/ppermute | solution.py:344
  122.9 0.9 collective-permute-start.15
  123.8 0.6 collective-permute-start.10
  124.4 1.8 %collective-permute-start.11 = (bf16[2,1,4,2,16,256]{5,4,3,2,1,0:T(8,128)(2,1)S(1)}, bf16[2,1,4,2,16,256]{5,4,3,2,1,0:T(8,128)(2,1)S(1)}, u32[]{:S(2)}, u32[]{:S(2)}) collective-permute-start(bf16[2,1,4,2,16,256]{5,4,3,2,1,0:T(8,128)(2,1)S(1)} %get-tuple-element.64), channel_id=1, source_target_pairs={{0,18},{16,0},{2,16},{18,2},{1,19},{17,1},{3,17},{19,3},{4,22},{20... | collective-permute-start | bytes 393224 | tf_op jit(solution)/shard_map/ppermute | solution.py:344
  126.2 0.3 collective-permute-start.9
  126.5 2.7 %solve.3.rest_0_ = f32[3,16,128,128]{3,2,1,0:T(8,128)} custom-call(s32[5]{0:T(128)S(1)} %stack.23.pos, s32[16]{0:T(128)S(1)} %copy-done.3, bf16[2,1,4,2,16,256]{5,4,3,2,1,0:T(8,128)(2,1)S(1)} %get-tuple-element.56.b0.n0, bf16[2,1,4,2,16,256]{5,4,3,2,1,0:T(8,128)(2,1)S(1)} %collective-permute-done.17.b1.n1, ...), custom_call_target="tpu_custom_call" | custom-call | flops 3000000000 | bytes 1048576 | tf_op jit(solution)/shard_map/solve/pallas_call | solution.py:443
  129.2 1.2 collective-permute-done.10.b2.n2
  130.4 2.5 %collective-permute-done.11.b3.n3 = bf16[2,1,4,2,16,256]{5,4,3,2,1,0:T(8,128)(2,1)S(1)} collective-permute-done((bf16[2,1,4,2,16,256]{5,4,3,2,1,0:T(8,128)(2,1)S(1)}, bf16[2,1,4,2,16,256]{5,4,3,2,1,0:T(8,128)(2,1)S(1)}, u32[]{:S(2)}, u32[]{:S(2)}) %collective-permute-start.11) | collective-permute-done | bytes 131104 | tf_op jit(solution)/shard_map/ppermute | solution.py:344
  132.9 0.3 collective-permute-done.9.b1.n1
  133.3 0.9 collective-permute-start.16
  134.2 2.7 %solve.4.rest_0_ = f32[3,16,128,128]{3,2,1,0:T(8,128)} custom-call(s32[5]{0:T(128)S(1)} %stack.23.pos, s32[16]{0:T(128)S(1)} %copy-done.3, bf16[2,1,4,2,16,256]{5,4,3,2,1,0:T(8,128)(2,1)S(1)} %get-tuple-element.65.b0.rest_0_.n0, bf16[2,1,4,2,16,256]{5,4,3,2,1,0:T(8,128)(2,1)S(1)} %collective-permute-done.12.b1.n1, ...), custom_call_target="tpu_custom_call", output_to_operand_aliasing={{}: (10, {})} | custom-call | flops 3000000000 | bytes 1048576 | tf_op jit(solution)/shard_map/solve/pallas_call | solution.py:443
  136.9 2.7 %solve.5 = f32[3,16,128,128]{3,2,1,0:T(8,128)} custom-call(s32[5]{0:T(128)S(1)} %stack.23.pos, s32[16]{0:T(128)S(1)} %copy-done.3, bf16[2,1,4,2,16,256]{5,4,3,2,1,0:T(8,128)(2,1)S(1)} %get-tuple-element.61.rest_0_.b0.n0, bf16[2,1,4,2,16,256]{5,4,3,2,1,0:T(8,128)(2,1)S(1)} %collective-permute-done.9.b1.n1, ...), custom_call_target="tpu_custom_call", output_to_operand_aliasing={{}: (10, {})} | custom-call | flops 3000000000 | bytes 1048576 | tf_op jit(solution)/shard_map/solve/pallas_call | solution.py:443
  (18 shorter events, 0.1 us)
Async XLA Ops:
  1.9 2.7 %collective-permute-start.5 = (bf16[4,16,16,128]{3,2,1,0:T(8,128)(2,1)S(1)}, bf16[4,16,16,128]{3,2,1,0:T(8,128)(2,1)S(1)}, u32[]{:S(2)}, u32[]{:S(2)}) collective-permute-start(bf16[4,16,16,128]{3,2,1,0:T(8,128)(2,1)S(1)} %get-tuple-element.43), channel_id=1, source_target_pairs={{0,1},{1,0},{2,3},{3,2},{4,5},{5,4},{6,7},{7,6},{8,9},{9,8},{10,11... | collective-permute-start | bytes 786440 | tf_op jit(solution)/shard_map/ppermute | solution.py:344
  3.4 9.0 %collective-permute-start = (bf16[4,16,16,128]{3,2,1,0:T(8,128)(2,1)S(1)}, bf16[4,16,16,128]{3,2,1,0:T(8,128)(2,1)S(1)}, u32[]{:S(2)}, u32[]{:S(2)}) collective-permute-start(bf16[4,16,16,128]{3,2,1,0:T(8,128)(2,1)S(1)} %get-tuple-element.37), channel_id=1, source_target_pairs={{0,1},{1,0},{2,3},{3,2},{4,5},{5,4},{6,7},{7,6},{8,9},{9,8},{10,11... | collective-permute-start | bytes 786440 | tf_op jit(solution)/shard_map/ppermute | solution.py:344
  3.5 9.0 %collective-permute-start.1 = (bf16[4,16,16,128]{3,2,1,0:T(8,128)(2,1)S(1)}, bf16[4,16,16,128]{3,2,1,0:T(8,128)(2,1)S(1)}, u32[]{:S(2)}, u32[]{:S(2)}) collective-permute-start(bf16[4,16,16,128]{3,2,1,0:T(8,128)(2,1)S(1)} %get-tuple-element.38), channel_id=1, source_target_pairs={{0,1},{1,0},{2,3},{3,2},{4,5},{5,4},{6,7},{7,6},{8,9},{9,8},{10,11... | collective-permute-start | bytes 786440 | tf_op jit(solution)/shard_map/ppermute | solution.py:344
  6.6 9.9 %collective-permute-start.6 = (bf16[2,1,4,2,16,256]{5,4,3,2,1,0:T(8,128)(2,1)S(1)}, bf16[2,1,4,2,16,256]{5,4,3,2,1,0:T(8,128)(2,1)S(1)}, u32[]{:S(2)}, u32[]{:S(2)}) collective-permute-start(bf16[2,1,4,2,16,256]{5,4,3,2,1,0:T(8,128)(2,1)S(1)} %get-tuple-element.45), channel_id=1, source_target_pairs={{0,16},{16,2},{2,18},{18,0},{1,17},{17,3},{3,19},{19,1},{4,20},{20... | collective-permute-start | bytes 393224 | tf_op jit(solution)/shard_map/ppermute | solution.py:344
  8.4 10.2 %collective-permute-start.7 = (bf16[2,1,4,2,16,256]{5,4,3,2,1,0:T(8,128)(2,1)S(1)}, bf16[2,1,4,2,16,256]{5,4,3,2,1,0:T(8,128)(2,1)S(1)}, u32[]{:S(2)}, u32[]{:S(2)}) collective-permute-start(bf16[2,1,4,2,16,256]{5,4,3,2,1,0:T(8,128)(2,1)S(1)} %get-tuple-element.46), channel_id=1, source_target_pairs={{0,2},{16,18},{2,0},{18,16},{1,3},{17,19},{3,1},{19,17},{4,6},{20,... | collective-permute-start | bytes 393224 | tf_op jit(solution)/shard_map/ppermute | solution.py:344
  11.7 6.9 %collective-permute-start.8 = (bf16[2,1,4,2,16,256]{5,4,3,2,1,0:T(8,128)(2,1)S(1)}, bf16[2,1,4,2,16,256]{5,4,3,2,1,0:T(8,128)(2,1)S(1)}, u32[]{:S(2)}, u32[]{:S(2)}) collective-permute-start(bf16[2,1,4,2,16,256]{5,4,3,2,1,0:T(8,128)(2,1)S(1)} %get-tuple-element.47), channel_id=1, source_target_pairs={{0,18},{16,0},{2,16},{18,2},{1,19},{17,1},{3,17},{19,3},{4,22},{20... | collective-permute-start | bytes 393224 | tf_op jit(solution)/shard_map/ppermute | solution.py:344
  15.3 12.6 %collective-permute-start.2 = (bf16[2,2,4,2,16,256]{5,4,3,2,1,0:T(8,128)(2,1)S(1)}, bf16[2,2,4,2,16,256]{5,4,3,2,1,0:T(8,128)(2,1)S(1)}, u32[]{:S(2)}, u32[]{:S(2)}) collective-permute-start(bf16[2,2,4,2,16,256]{5,4,3,2,1,0:T(8,128)(2,1)S(1)} %get-tuple-element.40), channel_id=1, source_target_pairs={{0,16},{16,2},{2,18},{18,0},{1,17},{17,3},{3,19},{19,1},{4,20},{20... | collective-permute-start | bytes 786440 | tf_op jit(solution)/shard_map/ppermute | solution.py:344
  16.1 13.0 %collective-permute-start.3 = (bf16[2,2,4,2,16,256]{5,4,3,2,1,0:T(8,128)(2,1)S(1)}, bf16[2,2,4,2,16,256]{5,4,3,2,1,0:T(8,128)(2,1)S(1)}, u32[]{:S(2)}, u32[]{:S(2)}) collective-permute-start(bf16[2,2,4,2,16,256]{5,4,3,2,1,0:T(8,128)(2,1)S(1)} %get-tuple-element.41), channel_id=1, source_target_pairs={{0,2},{16,18},{2,0},{18,16},{1,3},{17,19},{3,1},{19,17},{4,6},{20,... | collective-permute-start | bytes 786440 | tf_op jit(solution)/shard_map/ppermute | solution.py:344
  16.5 13.4 %collective-permute-start.4 = (bf16[2,2,4,2,16,256]{5,4,3,2,1,0:T(8,128)(2,1)S(1)}, bf16[2,2,4,2,16,256]{5,4,3,2,1,0:T(8,128)(2,1)S(1)}, u32[]{:S(2)}, u32[]{:S(2)}) collective-permute-start(bf16[2,2,4,2,16,256]{5,4,3,2,1,0:T(8,128)(2,1)S(1)} %get-tuple-element.42), channel_id=1, source_target_pairs={{0,18},{16,0},{2,16},{18,2},{1,19},{17,1},{3,17},{19,3},{4,22},{20... | collective-permute-start | bytes 786440 | tf_op jit(solution)/shard_map/ppermute | solution.py:344
  21.1 18.8 %all-to-all-start = ((bf16[16,1,2,32,384]{4,3,2,1,0:T(8,128)(2,1)}), bf16[16,1,2,32,384]{4,3,2,1,0:T(8,128)(2,1)S(1)}, u32[]{:S(2)}, u32[]{:S(2)}) async-start(bf16[16,1,2,32,384]{4,3,2,1,0:T(8,128)(2,1)} %synth_first.1), calls=%async_computation | async-start | bytes 1572864 | tf_op jit(solution)/shard_map/all_to_all | solution.py:367
  39.8 24.6 %all-to-all-start.1 = ((bf16[16,2,2,32,384]{4,3,2,1,0:T(8,128)(2,1)}), bf16[16,2,2,32,384]{4,3,2,1,0:T(8,128)(2,1)S(1)}, u32[]{:S(2)}, u32[]{:S(2)}) async-start(bf16[16,2,2,32,384]{4,3,2,1,0:T(8,128)(2,1)} %synth_second.1), calls=%async_computation.1 | async-start | bytes 3145728 | tf_op jit(solution)/shard_map/all_to_all | solution.py:367
  49.0 1.4 %copy-start.4 = (f32[2,768,384]{2,1,0:T(8,128)}, f32[2,768,384]{2,1,0:T(8,128)S(1)}, u32[]{:S(2)}) copy-start(f32[2,768,384]{2,1,0:T(8,128)S(1)} %get-tuple-element.50.rest_0_) | copy-start | bytes 7077892
  64.4 15.7 %all-to-all-start.2 = ((bf16[16,1,2,32,384]{4,3,2,1,0:T(8,128)(2,1)}), bf16[16,1,2,32,384]{4,3,2,1,0:T(8,128)(2,1)S(1)}, u32[]{:S(2)}, u32[]{:S(2)}) async-start(bf16[16,1,2,32,384]{4,3,2,1,0:T(8,128)(2,1)} %get-tuple-element.54), calls=%async_computation.2 | async-start | bytes 1572864 | tf_op jit(solution)/shard_map/all_to_all | solution.py:367
  69.7 1.7 %copy-start.5 = (f32[2,768,384]{2,1,0:T(8,128)S(1)}, f32[2,768,384]{2,1,0:T(8,128)}, u32[]{:S(2)}) copy-start(f32[2,768,384]{2,1,0:T(8,128)} %copy-done.4) | copy-start | bytes 7077892
  80.2 15.1 %all-to-all-start.3 = ((bf16[16,1,2,32,384]{4,3,2,1,0:T(8,128)(2,1)}), bf16[16,1,2,32,384]{4,3,2,1,0:T(8,128)(2,1)S(1)}, u32[]{:S(2)}, u32[]{:S(2)}) async-start(bf16[16,1,2,32,384]{4,3,2,1,0:T(8,128)(2,1)} %get-tuple-element.55), calls=%async_computation.3 | async-start | bytes 1572864 | tf_op jit(solution)/shard_map/all_to_all | solution.py:367
  84.8 14.1 %copy-start.1 = (bf16[8,32,32]{2,1,0:T(8,128)(2,1)S(1)}, bf16[8,32,32]{2,1,0:T(8,128)(2,1)}, u32[]{:S(2)}) copy-start(bf16[8,32,32]{2,1,0:T(8,128)(2,1)} %inv_ref.1) | copy-start | bytes 49156
  95.3 21.2 %all-to-all-start.4 = ((bf16[16,1,2,32,384]{4,3,2,1,0:T(8,128)(2,1)}), bf16[16,1,2,32,384]{4,3,2,1,0:T(8,128)(2,1)S(1)}, u32[]{:S(2)}, u32[]{:S(2)}) async-start(bf16[16,1,2,32,384]{4,3,2,1,0:T(8,128)(2,1)} %get-tuple-element.60), calls=%async_computation.4 | async-start | bytes 1572864 | tf_op jit(solution)/shard_map/all_to_all | solution.py:367
  99.3 6.5 %collective-permute-start.17 = (bf16[2,1,4,2,16,256]{5,4,3,2,1,0:T(8,128)(2,1)S(1)}, bf16[2,1,4,2,16,256]{5,4,3,2,1,0:T(8,128)(2,1)S(1)}, u32[]{:S(2)}, u32[]{:S(2)}) collective-permute-start(bf16[2,1,4,2,16,256]{5,4,3,2,1,0:T(8,128)(2,1)S(1)} %get-tuple-element.57), channel_id=1, source_target_pairs={{0,16},{16,2},{2,18},{18,0},{1,17},{17,3},{3,19},{19,1},{4,20},{20... | collective-permute-start | bytes 393224 | tf_op jit(solution)/shard_map/ppermute | solution.py:344
  99.9 5.9 %collective-permute-start.18 = (bf16[2,1,4,2,16,256]{5,4,3,2,1,0:T(8,128)(2,1)S(1)}, bf16[2,1,4,2,16,256]{5,4,3,2,1,0:T(8,128)(2,1)S(1)}, u32[]{:S(2)}, u32[]{:S(2)}) collective-permute-start(bf16[2,1,4,2,16,256]{5,4,3,2,1,0:T(8,128)(2,1)S(1)} %get-tuple-element.58), channel_id=1, source_target_pairs={{0,2},{16,18},{2,0},{18,16},{1,3},{17,19},{3,1},{19,17},{4,6},{20,... | collective-permute-start | bytes 393224 | tf_op jit(solution)/shard_map/ppermute | solution.py:344
  101.8 4.5 %collective-permute-start.19 = (bf16[2,1,4,2,16,256]{5,4,3,2,1,0:T(8,128)(2,1)S(1)}, bf16[2,1,4,2,16,256]{5,4,3,2,1,0:T(8,128)(2,1)S(1)}, u32[]{:S(2)}, u32[]{:S(2)}) collective-permute-start(bf16[2,1,4,2,16,256]{5,4,3,2,1,0:T(8,128)(2,1)S(1)} %get-tuple-element.59), channel_id=1, source_target_pairs={{0,18},{16,0},{2,16},{18,2},{1,19},{17,1},{3,17},{19,3},{4,22},{20... | collective-permute-start | bytes 393224 | tf_op jit(solution)/shard_map/ppermute | solution.py:344
  106.4 20.1 %collective-permute-start.20 = (bf16[4,1,4,2,16,256]{5,4,3,2,1,0:T(8,128)(2,1)S(1)}, bf16[4,1,4,2,16,256]{5,4,3,2,1,0:T(8,128)(2,1)S(1)}, u32[]{:S(2)}, u32[]{:S(2)}) collective-permute-start(bf16[4,1,4,2,16,256]{5,4,3,2,1,0:T(8,128)(2,1)S(1)} %gather.5), channel_id=1, source_target_pairs={{0,1},{1,0},{2,3},{3,2},{4,5},{5,4},{6,7},{7,6},{8,9},{9,8},{10,11... | collective-permute-start | bytes 786440 | tf_op jit(solution)/shard_map/ppermute | solution.py:344
  112.9 6.9 %collective-permute-start.12 = (bf16[2,1,4,2,16,256]{5,4,3,2,1,0:T(8,128)(2,1)S(1)}, bf16[2,1,4,2,16,256]{5,4,3,2,1,0:T(8,128)(2,1)S(1)}, u32[]{:S(2)}, u32[]{:S(2)}) collective-permute-start(bf16[2,1,4,2,16,256]{5,4,3,2,1,0:T(8,128)(2,1)S(1)} %get-tuple-element.66), channel_id=1, source_target_pairs={{0,16},{16,2},{2,18},{18,0},{1,17},{17,3},{3,19},{19,1},{4,20},{20... | collective-permute-start | bytes 393224 | tf_op jit(solution)/shard_map/ppermute | solution.py:344
  113.2 9.6 %collective-permute-start.13 = (bf16[2,1,4,2,16,256]{5,4,3,2,1,0:T(8,128)(2,1)S(1)}, bf16[2,1,4,2,16,256]{5,4,3,2,1,0:T(8,128)(2,1)S(1)}, u32[]{:S(2)}, u32[]{:S(2)}) collective-permute-start(bf16[2,1,4,2,16,256]{5,4,3,2,1,0:T(8,128)(2,1)S(1)} %get-tuple-element.67), channel_id=1, source_target_pairs={{0,2},{16,18},{2,0},{18,16},{1,3},{17,19},{3,1},{19,17},{4,6},{20,... | collective-permute-start | bytes 393224 | tf_op jit(solution)/shard_map/ppermute | solution.py:344
  116.5 6.4 %collective-permute-start.14 = (bf16[2,1,4,2,16,256]{5,4,3,2,1,0:T(8,128)(2,1)S(1)}, bf16[2,1,4,2,16,256]{5,4,3,2,1,0:T(8,128)(2,1)S(1)}, u32[]{:S(2)}, u32[]{:S(2)}) collective-permute-start(bf16[2,1,4,2,16,256]{5,4,3,2,1,0:T(8,128)(2,1)S(1)} %get-tuple-element.68), channel_id=1, source_target_pairs={{0,18},{16,0},{2,16},{18,2},{1,19},{17,1},{3,17},{19,3},{4,22},{20... | collective-permute-start | bytes 393224 | tf_op jit(solution)/shard_map/ppermute | solution.py:344
  119.7 6.8 %copy-start = (bf16[3,16,32,2,256]{4,3,2,1,0:T(2,128)(2,1)S(1)}, bf16[3,16,32,2,256]{4,3,2,1,0:T(2,128)(2,1)}, u32[]{:S(2)}) copy-start(bf16[3,16,32,2,256]{4,3,2,1,0:T(2,128)(2,1)} %param.7) | copy-start | bytes 4718596
  119.7 6.8 %copy-start.2 = (s32[16,256]{1,0:T(8,128)S(1)}, s32[16,256]{1,0:T(8,128)}, u32[]{:S(2)}) copy-start(s32[16,256]{1,0:T(8,128)} %class_ref.5) | copy-start | bytes 49156
  119.7 6.8 %copy-start.3 = (s32[16]{0:T(128)S(1)}, s32[16]{0:T(128)}, u32[]{:S(2)}) copy-start(s32[16]{0:T(128)} %count_ref.5) | copy-start | bytes 196
  122.9 10.4 %collective-permute-start.15 = (bf16[4,1,4,2,16,256]{5,4,3,2,1,0:T(8,128)(2,1)S(1)}, bf16[4,1,4,2,16,256]{5,4,3,2,1,0:T(8,128)(2,1)S(1)}, u32[]{:S(2)}, u32[]{:S(2)}) collective-permute-start(bf16[4,1,4,2,16,256]{5,4,3,2,1,0:T(8,128)(2,1)S(1)} %gather.3), channel_id=1, source_target_pairs={{0,1},{1,0},{2,3},{3,2},{4,5},{5,4},{6,7},{7,6},{8,9},{9,8},{10,11... | collective-permute-start | bytes 786440 | tf_op jit(solution)/shard_map/ppermute | solution.py:344
  123.8 6.6 %collective-permute-start.10 = (bf16[2,1,4,2,16,256]{5,4,3,2,1,0:T(8,128)(2,1)S(1)}, bf16[2,1,4,2,16,256]{5,4,3,2,1,0:T(8,128)(2,1)S(1)}, u32[]{:S(2)}, u32[]{:S(2)}) collective-permute-start(bf16[2,1,4,2,16,256]{5,4,3,2,1,0:T(8,128)(2,1)S(1)} %get-tuple-element.63), channel_id=1, source_target_pairs={{0,2},{16,18},{2,0},{18,16},{1,3},{17,19},{3,1},{19,17},{4,6},{20,... | collective-permute-start | bytes 393224 | tf_op jit(solution)/shard_map/ppermute | solution.py:344
  124.4 8.5 %collective-permute-start.11 = (bf16[2,1,4,2,16,256]{5,4,3,2,1,0:T(8,128)(2,1)S(1)}, bf16[2,1,4,2,16,256]{5,4,3,2,1,0:T(8,128)(2,1)S(1)}, u32[]{:S(2)}, u32[]{:S(2)}) collective-permute-start(bf16[2,1,4,2,16,256]{5,4,3,2,1,0:T(8,128)(2,1)S(1)} %get-tuple-element.64), channel_id=1, source_target_pairs={{0,18},{16,0},{2,16},{18,2},{1,19},{17,1},{3,17},{19,3},{4,22},{20... | collective-permute-start | bytes 393224 | tf_op jit(solution)/shard_map/ppermute | solution.py:344
  126.2 7.1 %collective-permute-start.9 = (bf16[2,1,4,2,16,256]{5,4,3,2,1,0:T(8,128)(2,1)S(1)}, bf16[2,1,4,2,16,256]{5,4,3,2,1,0:T(8,128)(2,1)S(1)}, u32[]{:S(2)}, u32[]{:S(2)}) collective-permute-start(bf16[2,1,4,2,16,256]{5,4,3,2,1,0:T(8,128)(2,1)S(1)} %get-tuple-element.62), channel_id=1, source_target_pairs={{0,16},{16,2},{2,18},{18,0},{1,17},{17,3},{3,19},{19,1},{4,20},{20... | collective-permute-start | bytes 393224 | tf_op jit(solution)/shard_map/ppermute | solution.py:344
  133.3 3.6 %collective-permute-start.16 = (bf16[4,1,4,2,16,256]{5,4,3,2,1,0:T(8,128)(2,1)S(1)}, bf16[4,1,4,2,16,256]{5,4,3,2,1,0:T(8,128)(2,1)S(1)}, u32[]{:S(2)}, u32[]{:S(2)}) collective-permute-start(bf16[4,1,4,2,16,256]{5,4,3,2,1,0:T(8,128)(2,1)S(1)} %gather.4), channel_id=1, source_target_pairs={{0,1},{1,0},{2,3},{3,2},{4,5},{5,4},{6,7},{7,6},{8,9},{9,8},{10,11... | collective-permute-start | bytes 786440 | tf_op jit(solution)/shard_map/ppermute | solution.py:344

commit v3 on v2

v3 whole, which is shorter than its diff:
```python
import functools
import math

import jax
import jax.numpy as jnp
import ml_dtypes
import numpy as np
from jax import lax
from jax.experimental import pallas as pl
from jax.experimental.pallas import tpu as pltpu
from jax.sharding import Mesh
from jax.sharding import PartitionSpec as P

KX = 512
KZ = 1024
NCLASS = 8
PX = 1536
PZ = 1536
HALF = PX // 2
NY = 32
BF = jnp.bfloat16
VMEM = 28 * 1024 * 1024
COLUMN = ("zl", "zh")
EARLY = 1
ORDER = (1, 0, 2)

def angles(wavenumbers, points, period):
    phases = (wavenumbers[:, None] * points[None, :]) % period
    scaled = np.float32(2.0 * math.pi / period) * phases.astype(np.float32)
    return scaled.astype(np.float64)


def z_tables():
    tables = []
    for parity in range(2):
        index = np.arange(parity, KZ, 2)
        wavenumber = np.where(index < KZ // 2, index, index - KZ)
        theta = angles(wavenumber, np.arange(HALF), PZ)
        tables.append(np.stack([np.cos(theta), np.sin(theta)]))
    return np.stack(tables).astype(np.float32).astype(ml_dtypes.bfloat16)


def x_tables():
    x, y, zl, i = np.meshgrid(np.arange(4), np.arange(4), np.arange(2), np.arange(8), indexing="ij")
    synth, fold = [], []
    for parity in range(2):
        kx = (x * 8 + zl * 4 + y) * 16 + 2 * i + parity
        theta = angles(kx.reshape(-1), np.arange(HALF), PX).reshape(4, 4, 2, 8, HALF)
        basis = np.stack([np.cos(theta), -np.sin(theta)], axis=2).astype(np.float32)
        weight = np.where(kx == 0, 1.0, 2.0).astype(np.float32)[:, :, None, :, :, None]
        synth.append((weight * basis).reshape(512, HALF).T)
        fold.append(basis.reshape(512, HALF))
    return (
        np.stack(synth).astype(ml_dtypes.bfloat16),
        np.stack(fold).astype(ml_dtypes.bfloat16),
    )


def mover(turned):
    row, column = (lax.broadcasted_iota(jnp.int32, (256, 256), axis) for axis in (turned, 1 - turned))
    kx = ((row & 7) << 1) | ((row >> 3) & 1)
    source = (kx << 4) | (((row >> 5) & 3) << 2) | ((row >> 7) << 1) | ((row >> 4) & 1)
    return (column == source).astype(jnp.float32).astype(BF)


def sorter(turned):
    row, column = (lax.broadcasted_iota(jnp.int32, (256, 256), axis) for axis in (turned, 1 - turned))
    return (row == (((column & 127) << 1) | (column >> 7))).astype(jnp.float32).astype(BF)


def wait(copies):
    for copy in copies:
        copy.wait()


def dot(a, b):
    return jnp.dot(a, b, preferred_element_type=jnp.float32)


def place_kernel(inv_ref, w_ref):
    row, column = (lax.broadcasted_iota(jnp.int32, (128, 128), axis) for axis in range(2))
    same = row % 4 == column % 4
    tall = (row[:, :32] // 4 == column[:, :32]).astype(BF)
    wide = (lax.broadcasted_iota(jnp.int32, (32, 128), 0) == lax.broadcasted_iota(jnp.int32, (32, 128), 1) // 4).astype(BF)
    for index in range(NCLASS):
        rows = dot(tall, inv_ref[index]).astype(BF)
        w_ref[:, index * 128 : index * 128 + 128] = jnp.where(same, dot(rows, wide), 0.0).astype(BF)


def cut_kernel(pos, v_hbm, out_ref, sems):
    copies = []
    for c in range(3):
        for z in range(4):
            first = pl.multiple_of(z * 32 + (1 - pos[3]) * 16, 16)
            copies.append(pltpu.make_async_copy(v_hbm.at[c, :, pl.ds(first, 16)], out_ref.at[c, z], sems.at[c, z]))
            copies[-1].start()
    wait(copies)


def pack_kernel(pos, v_hbm, other_ref, o0, o1, o2, o3, v_ref, sems):
    outs = (o0, o1, o2, o3)
    copies = []
    for c in range(3):
        for z in range(4):
            first = pl.multiple_of(z * 32 + pos[3] * 16, 16)
            copies.append(pltpu.make_async_copy(v_hbm.at[c, :, pl.ds(first, 16)], v_ref.at[c, z], sems.at[c, z]))
            copies[-1].start()
    move, sort = mover(0), sorter(0)
    wait(copies)
    places = [(step, core) for step in range(4) for core in range(2)]
    parts = []
    for step, core in places:
        z = lax.rem(pos[2] + step, 4)
        parts += [(other_ref if core else v_ref)[c, z].reshape(256, 128) for c in range(3)]
    moved = dot(move, jnp.concatenate(parts, axis=1)).astype(BF)
    parts = []
    for i in range(24):
        part = moved[:, i * 128 : i * 128 + 128]
        parts.append(jnp.concatenate([part[:128], part[128:]], axis=1))
    moved = dot(jnp.concatenate(parts, axis=0), sort).astype(BF)
    for i, (step, core) in enumerate(places):
        outs[step][core] = moved[i * 384 : (i + 1) * 384].reshape(3, 4, 2, 16, 256)


def hold_kernel(token, a0, a1, a2, o0, o1, o2):
    pass


def gather_kernel(n_ref, out_ref):
    out_ref[...] = n_ref[:, 1]


def z_copies(table_hbm, table_ref, sems):
    return [pltpu.make_async_copy(table_hbm.at[p], table_ref.at[p], sems.at[p]) for p in range(2)]


def synth_kernel(pos, r0, e1, e2, e3, l1, l2, l3, table_hbm, out_ref, lhs, table_ref, sems):
    nc = 3
    copies = z_copies(table_hbm, table_ref, sems)
    for copy in copies:
        copy.start()

    def fill(step, block):
        z = lax.rem(pos[2] + 4 - step, 4)
        for core in range(2):
            quarter = (z // 2) * 2 + lax.rem(pos[3] + core, 2)
            lanes = pl.ds(pl.multiple_of(quarter * 128, 128), 128)
            for ri in range(2):
                rows = pl.ds(pl.multiple_of(ri * (128 * nc) + lax.rem(z, 2) * (64 * nc), 64), 64 * nc)
                part = block[core, :, :, ri].reshape(64 * nc, 256)
                for parity in range(2):
                    lhs[parity, rows, lanes] = part[:, parity * 128 : parity * 128 + 128]

    fill(0, r0)

    @pl.when(pos[3] == EARLY)
    def _():
        for step, block in enumerate((e1, e2, e3)):
            fill(step + 1, block)

    @pl.when(pos[3] != EARLY)
    def _():
        for step, block in enumerate((l1, l2, l3)):
            fill(step + 1, block)

    n = 128 * nc
    sums = []
    for parity in range(2):
        copies[parity].wait()
        by_cos = dot(lhs[parity], table_ref[parity, 0])
        by_sin = dot(lhs[parity], table_ref[parity, 1])
        sums.append((by_cos[:n] - by_sin[n:], by_sin[:n] + by_cos[n:]))
    for ri in range(2):
        even, odd = sums[0][ri], sums[1][ri]
        for half, both in enumerate((even + odd, even - odd)):
            part = both.reshape(2, nc, 4, 2, 8, HALF)
            for plane in range(4):
                for c in range(nc):
                    mixed = [part[zl, c, plane, parity] for parity in range(2) for zl in range(2)]
                    mixed = jnp.concatenate(mixed, axis=0).astype(BF)
                    for quarter in range(2):
                        out_ref[plane * 4 + half * 2 + quarter, c, ri] = mixed[:, quarter * 384 : quarter * 384 + 384]


def middle_kernel(d_ref, synth_hbm, fold_hbm, out_ref, data, prod, synth_ref, fold_ref, sems, *, scale):
    synth_copy = pltpu.make_async_copy(synth_hbm, synth_ref, sems.at[0])
    fold_copy = pltpu.make_async_copy(fold_hbm, fold_ref, sems.at[1])
    synth_copy.start()
    for parity in range(2):
        for c in range(3):
            part = d_ref[:, c, :, parity * 16 : parity * 16 + 16, :].reshape(512, 384)
            data[parity, :, c * 384 : c * 384 + 384] = part
    synth_copy.wait()
    fold_copy.start()
    for step in range(3):
        rows = slice(step * 256, step * 256 + 256)
        even = dot(synth_ref[0, rows, :], data[0])
        odd = dot(synth_ref[1, rows, :], data[1])
        low, high = even + odd, even - odd
        for c in range(3):
            lanes = slice(c * 384, c * 384 + 384)
            one, two = low[:, lanes] * low[:, 384:768], high[:, lanes] * high[:, 384:768]
            prod[0, rows, lanes] = (one + two).astype(BF)
            prod[1, rows, lanes] = (one - two).astype(BF)
    fold_copy.wait()
    for parity in range(2):
        spectra = (dot(fold_ref[parity], prod[parity]) * scale).astype(BF)
        for c in range(3):
            part = spectra[:, c * 384 : c * 384 + 384].reshape(16, 2, 16, 384)
            out_ref[:, c, :, parity * 16 : parity * 16 + 16, :] = part


def analyse_kernel(pos, b_ref, table_hbm, out_ref, lhs, table_ref, sems, *, scale):
    nc = 3
    copies = z_copies(table_hbm, table_ref, sems)
    for copy in copies:
        copy.start()
    n = 128 * nc
    for plane in range(4):
        for quarter in range(2):
            for ri in range(2):
                low = b_ref[plane * 4 + quarter, :, ri].reshape(32 * nc, 384).astype(jnp.float32)
                high = b_ref[plane * 4 + quarter + 2, :, ri].reshape(32 * nc, 384).astype(jnp.float32)
                rows = slice(ri * n + plane * 32 * nc, ri * n + plane * 32 * nc + 32 * nc)
                lanes = slice(quarter * 384, quarter * 384 + 384)
                lhs[0, rows, lanes] = (low + high).astype(BF)
                lhs[1, rows, lanes] = (low - high).astype(BF)
    for parity in range(2):
        copies[parity].wait()
        by_cos, by_sin = (
            lax.dot_general(
                lhs[parity], table_ref[parity, i], (((1,), (1,)), ((), ())), preferred_element_type=jnp.float32
            )
            for i in range(2)
        )
        for ri, spectra in enumerate((by_cos[:n] + by_sin[n:], by_cos[n:] - by_sin[:n])):
            part = (spectra * scale).reshape(4, nc, 2, 2, 8, 512)
            for zl in range(2):
                for quarter in range(4):
                    for plane in range(4):
                        for c in range(nc):
                            piece = part[plane, c, :, zl, :, quarter * 128 : quarter * 128 + 128]
                            block, other = zl * 2 + quarter // 2, lax.rem(quarter + pos[3], 2)
                            lanes = slice(parity * 128, parity * 128 + 128)
                            out_ref[block, other, c, plane, ri, :, lanes] = piece.reshape(16, 128).astype(BF)


def solve_kernel(pos, count_ref, n_ref, other_ref, v_ref, w_ref, class_ref, out_ref, right, done, sems):
    move, sort = mover(1), sorter(1)
    row = lax.broadcasted_iota(jnp.int32, (16, 16, 128), 1)
    kx = lax.broadcasted_iota(jnp.int32, (16, 16, 128), 0)
    lane = lax.broadcasted_iota(jnp.int32, (16, 16, 128), 2)
    index = ((pos[2] // 2) * 2 + pos[3]) * 256 + lane + 128 * (lax.rem(row, 4) // 2)
    wavenumber = jnp.where(index < KZ // 2, index, index - KZ)
    counts = jnp.concatenate([jnp.full((1, 16, 128), count_ref[k], jnp.int32) for k in range(16)], axis=0)
    mean = (kx + pos[4] == 0) & (wavenumber == 0)
    half = jnp.where((jnp.abs(wavenumber) < counts) & jnp.logical_not(mean), 0.5, 0.0).astype(jnp.float32)
    places = [(block, other) for block in range(4) for other in range(2)]
    parts = [other_ref[block, c] if other else n_ref[block, 0, c] for block, other in places for c in range(3)]
    both = dot(jnp.concatenate([part.reshape(128, 256) for part in parts], axis=0), sort).astype(BF)
    both = [both[i * 128 : i * 128 + 128] for i in range(24)]
    both = [jnp.concatenate([part[:, :128], part[:, 128:]], axis=0) for part in both]
    moved = dot(move, jnp.concatenate(both, axis=1))
    for i, (block, other) in enumerate(places):
        z = (block % 2) * 2 + block // 2
        group = z * 2 + lax.rem(pos[3] + other, 2)
        rows = pl.ds(pl.multiple_of(group * 16, 16), 16)
        for c in range(3):
            old = v_ref[c, :, rows, :].astype(jnp.float32)
            lanes = slice((i * 3 + c) * 128, (i * 3 + c) * 128 + 128)
            new = (old + moved[:, lanes].reshape(16, 16, 128) * half).astype(BF)
            for k in range(16):
                right[k // 2, rows, (c * 2 + k % 2) * 128 : (c * 2 + k % 2) * 128 + 128] = new[k]

    early = (lax.broadcasted_iota(jnp.int32, (16, 128), 0) & 3) < 2
    copies = []
    for pair in range(8):
        classes = []
        for k in range(2):
            line = class_ref[pair * 2 + k : pair * 2 + k + 1, :]
            classes.append(jnp.where(early, line[:, :128], line[:, 128:]))
        classes = jnp.concatenate(classes * 3, axis=1)
        line = right[pair].reshape(8, 16, 768)
        masked = []
        for index in range(NCLASS):
            chosen = (classes == index).astype(jnp.float32).astype(BF)
            masked.append((line * chosen[None]).reshape(128, 768))
        total = dot(w_ref[...], jnp.concatenate(masked, axis=0))
        block = pl.ds(pair * 2, 2)
        for c in range(3):
            for k in range(2):
                done[c, pair * 2 + k] = total[:, (c * 2 + k) * 128 : (c * 2 + k) * 128 + 128]
            copies.append(pltpu.make_async_copy(done.at[c, block], out_ref.at[c, block], sems.at[c, pair]))
            copies[-1].start()
    wait(copies)


def params():
    return pltpu.CompilerParams(vmem_limit_bytes=VMEM)


def in_hbm(array):
    return pltpu.with_memory_space_constraint(array, pltpu.HBM)


def spec(memory):
    return pl.BlockSpec(memory_space=memory)


def along_z(block, step, core):
    pairs = []
    for z in range(4):
        to = (z + step) % 4
        pairs.append((((z % 2) * 2 + z // 2) * 2 + core, ((to % 2) * 2 + to // 2) * 2 + core))
    return lax.ppermute(block, ("zl", "zh", "core"), pairs)


def plane(blocks):
    return lax.all_to_all(blocks, ("x", "y"), split_axis=0, concat_axis=0, tiled=True)


def after(value, *earlier):
    return lax.optimization_barrier((value, *earlier))[0]


def body(velocity, inverses, class_index, keep_count):
    scale_x = (0.5 / math.sqrt(KX * KZ)) ** 2 / PX
    scale_z = 2.0 * math.sqrt(KX * KZ) / PZ
    z_basis, x_synth, x_fold = (in_hbm(jnp.asarray(t)) for t in (z_tables(), *x_tables()))
    z_scratch = [pltpu.VMEM((2, 2, 512, HALF), BF), pltpu.SemaphoreType.DMA((2,))]
    lines = velocity.reshape(3, 16, NY, 2, 2, 128).transpose(0, 1, 2, 4, 3, 5).reshape(3, 16, 128, 128)
    x, y, zl = (lax.axis_index(name) for name in ("x", "y", "zl"))
    pos = jnp.stack([x, y, lax.axis_index("zh") * 2 + zl, lax.axis_index("core"), (x * 8 + zl * 4 + y) * 16])

    mode_shape = jax.ShapeDtypeStruct((2, 3, 4, 2, 16, 256), BF)
    plane_shape = jax.ShapeDtypeStruct((16, 3, 2, 32, 384), BF)
    smem, vmem, hbm, free = (spec(m) for m in (pltpu.SMEM, pltpu.VMEM, pltpu.HBM, pl.ANY))

    def call(kernel, name, specs, args, outs, scratch, aliases={}, out_spec=vmem):
        return pl.pallas_call(
            kernel,
            in_specs=specs,
            out_specs=[out_spec] * len(outs),
            out_shape=outs,
            scratch_shapes=scratch,
            input_output_aliases=aliases,
            compiler_params=params(),
            name=name,
        )(*args)

    operators = pl.pallas_call(
        place_kernel,
        out_shape=jax.ShapeDtypeStruct((128, NCLASS * 128), BF),
        compiler_params=params(),
        name="place",
    )(inverses)

    dma = pltpu.SemaphoreType.DMA
    fixed = in_hbm(lines)
    piece_shape = jax.ShapeDtypeStruct((3, 4, 16, 16, 128), BF)
    (piece,) = call(cut_kernel, "cut", [smem, hbm], (pos, fixed), [piece_shape], [dma((3, 4))])
    piece = lax.ppermute(piece, "core", [(0, 1), (1, 0)])
    packed = call(
        pack_kernel, "pack", [smem, hbm, vmem], (pos, fixed, piece), [mode_shape] * 4,
        [pltpu.VMEM((3, 4, 16, 16, 128), BF), dma((3, 4))],
    )
    first = [along_z(packed[step], step, EARLY) for step in (1, 2, 3)]
    token = sum(block[0, 0, 0, 0, :, :128].astype(jnp.float32) for block in first[:1]).astype(BF)
    token = lax.ppermute(token, "core", [(EARLY, 1 - EARLY)])
    held = call(hold_kernel, "hold", [free] * 4, (token, *packed[1:]), [mode_shape] * 3, [], {1: 0, 2: 1, 3: 2}, free)
    second = [along_z(held[step - 1], step, 1 - EARLY) for step in (1, 2, 3)]
    (spread,) = call(
        synth_kernel, "synth", [smem] + [vmem] * 7 + [hbm], (pos, packed[0], *first, *second, z_basis), [plane_shape],
        [pltpu.VMEM((2, 768, 512), BF), *z_scratch],
    )
    (folded,) = call(
        functools.partial(middle_kernel, scale=scale_x), "middle", [vmem, hbm, hbm],
        (plane(spread), x_synth, x_fold), [plane_shape],
        [
            pltpu.VMEM((2, 512, 1152), BF), pltpu.VMEM((2, HALF, 1152), BF),
            pltpu.VMEM((2, HALF, 512), BF), pltpu.VMEM((2, 512, HALF), BF), dma((2,)),
        ],
    )
    (modes,) = call(
        functools.partial(analyse_kernel, scale=scale_z), "analyse", [smem, vmem, hbm],
        (pos, plane(folded), z_basis), [jax.ShapeDtypeStruct((4, *mode_shape.shape), BF)],
        [pltpu.VMEM((2, 768, HALF), BF), *z_scratch],
    )
    modes = lax.all_to_all(modes, COLUMN, split_axis=0, concat_axis=0, tiled=True)
    (other,) = call(gather_kernel, "gather", [vmem], (modes,), [jax.ShapeDtypeStruct((4, 3, 4, 2, 16, 256), BF)], [])
    other = lax.ppermute(other, "core", [(0, 1), (1, 0)])
    (solved,) = call(
        solve_kernel, "solve", [smem] * 2 + [vmem] * 5,
        (pos, keep_count, modes, other, lines, operators, class_index),
        [jax.ShapeDtypeStruct((3, 16, 128, 128), jnp.float32)],
        [pltpu.VMEM((8, 128, 768), BF), pltpu.VMEM((3, 16, 128, 128), jnp.float32), dma((3, 8))],
        out_spec=free,
    )
    return solved.reshape(3, 16, NY, 2, 2, 128).transpose(0, 1, 2, 4, 3, 5).reshape(3, 16, NY, 2, 256)


def solution(mesh):
    fine = Mesh(mesh.devices.reshape(4, 2, 4, 2, 2), ("x", "zl", "y", "zh", "core"))
    wide, narrow = ("x", "zl", "y"), ("zh", "core")
    in_specs = (P(None, wide, None, None, narrow), P(), P(wide, narrow), P(wide))
    out_specs = P(None, wide, None, None, narrow)
    return jax.shard_map(body, mesh=fine, in_specs=in_specs, out_specs=out_specs, check_vma=False)
```

time: 141 us -> 132 us (0.936)
  blocking collectives: 0 us -> 65.6 us
  waiting for transfers between devices: 39.5 us -> 8.25 us
  starting transfers between devices: 53.5 us -> 30.8 us
  Pallas kernels: 43.1 us -> 26.5 us
  local copies, waits for them, and re-layouts: 3.17 us -> 0.11 us
    all_to_all x0 -> x3, blocking collectives: none -> 65.6 us  [the longest x2 47.2 us: plane(): lax.all_to_all(blocks, ('x', 'y'), split_axis=0, concat_axis=0, tiled=True)]
    all_to_all x5 -> x0, waiting for transfers between devices: 28.8 us -> none  [plane(): lax.all_to_all(blocks, ('x', 'y'), split_axis=0, concat_axis=0, tiled=True)]
    all_to_all x5 -> x0, starting transfers between devices: 24.7 us -> none  [plane(): lax.all_to_all(blocks, ('x', 'y'), split_axis=0, concat_axis=0, tiled=True)]
    pallas_call x16 -> x8, Pallas kernels: 42.7 us -> 26.1 us  [call(): pl.pallas_call(kernel, in_specs=specs, out_specs=[out_spec] * len(outs),...]
    unnamed x12 -> x8, local copies, waits for them, and re-layouts: 3.09 us -> 0.03 us
    ppermute x21 -> x9, waiting for transfers between devices: 10.7 us -> 8.25 us  [the longest x6 4.81 us: along_z(): return lax.ppermute(block, ('zl', 'zh', 'core'), pairs)]
    ppermute x21 -> x9, starting transfers between devices: 28.8 us -> 30.8 us  [the longest x1 14.5 us: body(): other = lax.ppermute(other, 'core', [(0, 1), (1, 0)])]
  transfers between devices with their start and end apart: 26 -> 9, of which waited for: 13 -> 4; matrix products, arithmetic and copies ran while one was open for 0% -> 0% of each run, Pallas kernels for 28% -> 0%
where the time goes in v3:
time: 132 us
  blocking collectives  65.6 us (50%)
  starting transfers between devices  30.8 us (23%)
  Pallas kernels  26.5 us (20%)
  waiting for transfers between devices  8.25 us (6%)
    all_to_all x2, blocking collectives, plane(): lax.all_to_all(blocks, ('x', 'y'), split_axis=0, concat_axis=0, tiled=True)  47.2 us
    pallas_call x8, Pallas kernels, call(): pl.pallas_call(kernel, in_specs=specs, out_specs=[out_spec] * len(outs),...  26.1 us
    all_to_all x1, blocking collectives, body(): lax.all_to_all(modes, COLUMN, split_axis=0, concat_axis=0, tiled=True)  18.4 us
    ppermute x1, starting transfers between devices, body(): other = lax.ppermute(other, 'core', [(0, 1), (1, 0)])  14.5 us
    ppermute x6, starting transfers between devices, along_z(): return lax.ppermute(block, ('zl', 'zh', 'core'), pairs)  13.5 us
    ppermute x6, waiting for transfers between devices, along_z(): return lax.ppermute(block, ('zl', 'zh', 'core'), pairs)  4.81 us
  transfers between devices with their start and end apart: 9, of which 4 were waited for; matrix products, arithmetic and copies ran while one was open for 0% of the time, Pallas kernels for 0%

profile of v3, /device:TPU:1, one launch (start us, length us, event | category | flops | bytes accessed | tf_op | source)
XLA Modules:
  0.0 131.7 jit_solution(11648454890102267892)
XLA Ops:
  0.0 0.1 stack.23.pos
  0.1 1.8 %cut.1 = bf16[3,4,16,16,128]{4,3,2,1,0:T(8,128)(2,1)S(1)} custom-call(s32[5]{0:T(128)S(1)} %stack.23.pos, bf16[3,16,128,128]{3,2,1,0:T(8,128)(2,1)} %bitcast.17), custom_call_target="tpu_custom_call" | custom-call | tf_op jit(solution)/shard_map/cut/pallas_call | solution.py:340
  1.9 1.5 %collective-permute-start = (bf16[3,4,16,16,128]{4,3,2,1,0:T(8,128)(2,1)S(1)}, bf16[3,4,16,16,128]{4,3,2,1,0:T(8,128)(2,1)S(1)}, u32[]{:S(2)}, u32[]{:S(2)}) collective-permute-start(bf16[3,4,16,16,128]{4,3,2,1,0:T(8,128)(2,1)S(1)} %cut.1), channel_id=1, source_target_pairs={{0,1},{1,0},{2,3},{3,2},{4,5},{5,4},{6,7},{7,6},{8,9},{9,8},{10,11... | collective-permute-start | bytes 2359304 | tf_op jit(solution)/shard_map/ppermute | solution.py:362
  3.4 1.9 %collective-permute-done.other_ref = bf16[3,4,16,16,128]{4,3,2,1,0:T(8,128)(2,1)S(1)} collective-permute-done((bf16[3,4,16,16,128]{4,3,2,1,0:T(8,128)(2,1)S(1)}, bf16[3,4,16,16,128]{4,3,2,1,0:T(8,128)(2,1)S(1)}, u32[]{:S(2)}, u32[]{:S(2)}) %collective-permute-start) | collective-permute-done | bytes 786464 | tf_op jit(solution)/shard_map/ppermute | solution.py:362
  5.3 2.8 %pack.1 = (bf16[2,3,4,2,16,256]{5,4,3,2,1,0:T(8,128)(2,1)S(1)}, bf16[2,3,4,2,16,256]{5,4,3,2,1,0:T(8,128)(2,1)S(1)}, bf16[2,3,4,2,16,256]{5,4,3,2,1,0:T(8,128)(2,1)S(1)}, bf16[2,3,4,2,16,256]{5,4,3,2,1,0:T(8,128)(2,1)S(1)}) custom-call(s32[5]{0:T(128)S(1)} %stack.23.pos, bf16[3,16,128,128]{3,2,1,0:T(8,128)(2,1)} %bitcast.18, ...), custom_call_target="tpu_custom_call" | custom-call | tf_op jit(solution)/shard_map/pack/pallas_call | solution.py:340
  8.1 3.6 %collective-permute-start.1 = (bf16[2,3,4,2,16,256]{5,4,3,2,1,0:T(8,128)(2,1)S(1)}, bf16[2,3,4,2,16,256]{5,4,3,2,1,0:T(8,128)(2,1)S(1)}, u32[]{:S(2)}, u32[]{:S(2)}) collective-permute-start(bf16[2,3,4,2,16,256]{5,4,3,2,1,0:T(8,128)(2,1)S(1)} %get-tuple-element.13.a0), channel_id=1, source_target_pairs={{1,17},{17,3},{3,19},{19,1},{5,21},{21,7},{7,23},{23,5},{9,25},{25... | collective-permute-start | bytes 1179656 | tf_op jit(solution)/shard_map/ppermute | solution.py:315
  11.8 5.2 %collective-permute-start.2 = (bf16[2,3,4,2,16,256]{5,4,3,2,1,0:T(8,128)(2,1)S(1)}, bf16[2,3,4,2,16,256]{5,4,3,2,1,0:T(8,128)(2,1)S(1)}, u32[]{:S(2)}, u32[]{:S(2)}) collective-permute-start(bf16[2,3,4,2,16,256]{5,4,3,2,1,0:T(8,128)(2,1)S(1)} %get-tuple-element.14.a1), channel_id=1, source_target_pairs={{1,3},{17,19},{3,1},{19,17},{5,7},{21,23},{7,5},{23,21},{9,11},{25... | collective-permute-start | bytes 1179656 | tf_op jit(solution)/shard_map/ppermute | solution.py:315
  17.0 2.6 %collective-permute-start.3 = (bf16[2,3,4,2,16,256]{5,4,3,2,1,0:T(8,128)(2,1)S(1)}, bf16[2,3,4,2,16,256]{5,4,3,2,1,0:T(8,128)(2,1)S(1)}, u32[]{:S(2)}, u32[]{:S(2)}) collective-permute-start(bf16[2,3,4,2,16,256]{5,4,3,2,1,0:T(8,128)(2,1)S(1)} %get-tuple-element.15.a2), channel_id=1, source_target_pairs={{1,19},{17,1},{3,17},{19,3},{5,23},{21,5},{7,21},{23,7},{9,27},{25... | collective-permute-start | bytes 1179656 | tf_op jit(solution)/shard_map/ppermute | solution.py:315
  19.6 0.0 collective-permute-done.1.e1
  19.7 1.3 collective-permute-start.4
  21.0 3.5 %collective-permute-done.2.e2 = bf16[2,3,4,2,16,256]{5,4,3,2,1,0:T(8,128)(2,1)S(1)} collective-permute-done((bf16[2,3,4,2,16,256]{5,4,3,2,1,0:T(8,128)(2,1)S(1)}, bf16[2,3,4,2,16,256]{5,4,3,2,1,0:T(8,128)(2,1)S(1)}, u32[]{:S(2)}, u32[]{:S(2)}) %collective-permute-start.2) | collective-permute-done | bytes 393248 | tf_op jit(solution)/shard_map/ppermute | solution.py:315
  24.4 1.3 %collective-permute-done.3.e3 = bf16[2,3,4,2,16,256]{5,4,3,2,1,0:T(8,128)(2,1)S(1)} collective-permute-done((bf16[2,3,4,2,16,256]{5,4,3,2,1,0:T(8,128)(2,1)S(1)}, bf16[2,3,4,2,16,256]{5,4,3,2,1,0:T(8,128)(2,1)S(1)}, u32[]{:S(2)}, u32[]{:S(2)}) %collective-permute-start.3) | collective-permute-done | bytes 393248 | tf_op jit(solution)/shard_map/ppermute | solution.py:315
  25.8 0.0 collective-permute-done.4.token
  25.8 0.7 collective-permute-start.5
  26.4 0.7 collective-permute-start.6
  27.1 0.7 collective-permute-start.7
  27.8 0.0 collective-permute-done.5.l1
  27.8 0.0 collective-permute-done.6.l2
  27.9 0.0 collective-permute-done.7.l3
  27.9 5.6 %synth.1 = bf16[16,3,2,32,384]{4,3,2,1,0:T(8,128)(2,1)S(1)} custom-call(s32[5]{0:T(128)S(1)} %stack.23.pos, bf16[2,3,4,2,16,256]{5,4,3,2,1,0:T(8,128)(2,1)S(1)} %get-tuple-element.12.r0, bf16[2,3,4,2,16,256]{5,4,3,2,1,0:T(8,128)(2,1)S(1)} %collective-permute-done.1.e1, bf16[2,3,4,2,16,256]{5,4,3,2,1,0:T(8,128)(2,1)S(1)} %collective-permute-done.2.e2, ...), custom_call_target="tpu_custom_call" | custom-call | tf_op jit(solution)/shard_map/synth/pallas_call | solution.py:340
  33.5 25.2 %all_to_all.15.d_ref = bf16[16,3,2,32,384]{4,3,2,1,0:T(8,128)(2,1)S(1)} all-to-all(bf16[16,3,2,32,384]{4,3,2,1,0:T(8,128)(2,1)S(1)} %synth.1), channel_id=1, replica_groups=mesh['x'=4,'zl'=2,'y'=4,'zh'=2,'core'=2] {'x','y'}, dimensions={0} | all-to-all | bytes 4718592 | tf_op jit(solution)/shard_map/all_to_all | solution.py:319
  58.6 6.3 %middle.1 = bf16[16,3,2,32,384]{4,3,2,1,0:T(8,128)(2,1)S(1)} custom-call(bf16[16,3,2,32,384]{4,3,2,1,0:T(8,128)(2,1)S(1)} %all_to_all.15.d_ref, bf16[2,768,512]{2,1,0:T(8,128)(2,1)} %constant.34.clone.synth_hbm, bf16[2,512,768]{2,1,0:T(8,128)(2,1)} %constant.35.clone.fold_hbm), custom_call_target="tpu_custom_call" | custom-call | tf_op jit(solution)/shard_map/middle/pallas_call | solution.py:340
  64.9 22.0 %all_to_all.16.b_ref = bf16[16,3,2,32,384]{4,3,2,1,0:T(8,128)(2,1)S(1)} all-to-all(bf16[16,3,2,32,384]{4,3,2,1,0:T(8,128)(2,1)S(1)} %middle.1), channel_id=1, replica_groups=mesh['x'=4,'zl'=2,'y'=4,'zh'=2,'core'=2] {'x','y'}, dimensions={0} | all-to-all | bytes 4718592 | tf_op jit(solution)/shard_map/all_to_all | solution.py:319
  86.9 5.0 %analyse.1 = bf16[4,2,3,4,2,16,256]{6,5,4,3,2,1,0:T(8,128)(2,1)S(1)} custom-call(s32[5]{0:T(128)S(1)} %stack.23.pos, bf16[16,3,2,32,384]{4,3,2,1,0:T(8,128)(2,1)S(1)} %all_to_all.16.b_ref, bf16[2,2,512,768]{3,2,1,0:T(8,128)(2,1)} %constant.33.clone.table_hbm), custom_call_target="tpu_custom_call" | custom-call | tf_op jit(solution)/shard_map/analyse/pallas_call | solution.py:340
  91.9 0.0 copy-start.1
  91.9 0.0 copy-start
  91.9 0.0 copy-start.2
  91.9 0.0 copy-start.3
  92.0 18.4 %all_to_all.17.n_ref = bf16[4,2,3,4,2,16,256]{6,5,4,3,2,1,0:T(8,128)(2,1)S(1)} all-to-all(bf16[4,2,3,4,2,16,256]{6,5,4,3,2,1,0:T(8,128)(2,1)S(1)} %analyse.1), channel_id=1, replica_groups=mesh['x'=4,'zl'=2,'y'=4,'zh'=2,'core'=2] {'zl','zh'}, dimensions={0} | all-to-all | bytes 3145728 | tf_op jit(solution)/shard_map/all_to_all | solution.py:389
  110.4 0.1 gather.1
  110.4 14.5 %collective-permute-start.8 = (bf16[4,3,4,2,16,256]{5,4,3,2,1,0:T(8,128)(2,1)S(1)}, bf16[4,3,4,2,16,256]{5,4,3,2,1,0:T(8,128)(2,1)S(1)}, u32[]{:S(2)}, u32[]{:S(2)}) collective-permute-start(bf16[4,3,4,2,16,256]{5,4,3,2,1,0:T(8,128)(2,1)S(1)} %gather.1), channel_id=1, source_target_pairs={{0,1},{1,0},{2,3},{3,2},{4,5},{5,4},{6,7},{7,6},{8,9},{9,8},{10,11... | collective-permute-start | bytes 2359304 | tf_op jit(solution)/shard_map/ppermute | solution.py:391
  124.9 0.0 copy-done.1
  124.9 0.4 place.1.w_ref
  125.3 1.5 %collective-permute-done.8.other_ref = bf16[4,3,4,2,16,256]{5,4,3,2,1,0:T(8,128)(2,1)S(1)} collective-permute-done((bf16[4,3,4,2,16,256]{5,4,3,2,1,0:T(8,128)(2,1)S(1)}, bf16[4,3,4,2,16,256]{5,4,3,2,1,0:T(8,128)(2,1)S(1)}, u32[]{:S(2)}, u32[]{:S(2)}) %collective-permute-start.8) | collective-permute-done | bytes 786464 | tf_op jit(solution)/shard_map/ppermute | solution.py:391
  126.9 0.0 copy-done
  126.9 0.0 copy-done.2
  126.9 0.0 copy-done.3
  126.9 4.6 %solve.1 = f32[3,16,128,128]{3,2,1,0:T(8,128)} custom-call(s32[5]{0:T(128)S(1)} %stack.23.pos, s32[16]{0:T(128)S(1)} %copy-done.3, bf16[4,2,3,4,2,16,256]{6,5,4,3,2,1,0:T(8,128)(2,1)S(1)} %all_to_all.17.n_ref, bf16[4,3,4,2,16,256]{5,4,3,2,1,0:T(8,128)(2,1)S(1)} %collective-permute-done.8.other_ref, bf16[3,16,128,128]{3,2,1,0:T(8,128)(2,1)S(1)} %bitcast.19, ...), custom_call_target="tpu_custom_call" | custom-call | tf_op jit(solution)/shard_map/solve/pallas_call | solution.py:340
  (2 shorter events, 0.0 us)
Async XLA Ops:
  1.9 3.4 %collective-permute-start = (bf16[3,4,16,16,128]{4,3,2,1,0:T(8,128)(2,1)S(1)}, bf16[3,4,16,16,128]{4,3,2,1,0:T(8,128)(2,1)S(1)}, u32[]{:S(2)}, u32[]{:S(2)}) collective-permute-start(bf16[3,4,16,16,128]{4,3,2,1,0:T(8,128)(2,1)S(1)} %cut.1), channel_id=1, source_target_pairs={{0,1},{1,0},{2,3},{3,2},{4,5},{5,4},{6,7},{7,6},{8,9},{9,8},{10,11... | collective-permute-start | bytes 2359304 | tf_op jit(solution)/shard_map/ppermute | solution.py:362
  8.1 11.5 %collective-permute-start.1 = (bf16[2,3,4,2,16,256]{5,4,3,2,1,0:T(8,128)(2,1)S(1)}, bf16[2,3,4,2,16,256]{5,4,3,2,1,0:T(8,128)(2,1)S(1)}, u32[]{:S(2)}, u32[]{:S(2)}) collective-permute-start(bf16[2,3,4,2,16,256]{5,4,3,2,1,0:T(8,128)(2,1)S(1)} %get-tuple-element.13.a0), channel_id=1, source_target_pairs={{1,17},{17,3},{3,19},{19,1},{5,21},{21,7},{7,23},{23,5},{9,25},{25... | collective-permute-start | bytes 1179656 | tf_op jit(solution)/shard_map/ppermute | solution.py:315
  11.8 12.7 %collective-permute-start.2 = (bf16[2,3,4,2,16,256]{5,4,3,2,1,0:T(8,128)(2,1)S(1)}, bf16[2,3,4,2,16,256]{5,4,3,2,1,0:T(8,128)(2,1)S(1)}, u32[]{:S(2)}, u32[]{:S(2)}) collective-permute-start(bf16[2,3,4,2,16,256]{5,4,3,2,1,0:T(8,128)(2,1)S(1)} %get-tuple-element.14.a1), channel_id=1, source_target_pairs={{1,3},{17,19},{3,1},{19,17},{5,7},{21,23},{7,5},{23,21},{9,11},{25... | collective-permute-start | bytes 1179656 | tf_op jit(solution)/shard_map/ppermute | solution.py:315
  17.0 8.8 %collective-permute-start.3 = (bf16[2,3,4,2,16,256]{5,4,3,2,1,0:T(8,128)(2,1)S(1)}, bf16[2,3,4,2,16,256]{5,4,3,2,1,0:T(8,128)(2,1)S(1)}, u32[]{:S(2)}, u32[]{:S(2)}) collective-permute-start(bf16[2,3,4,2,16,256]{5,4,3,2,1,0:T(8,128)(2,1)S(1)} %get-tuple-element.15.a2), channel_id=1, source_target_pairs={{1,19},{17,1},{3,17},{19,3},{5,23},{21,5},{7,21},{23,7},{9,27},{25... | collective-permute-start | bytes 1179656 | tf_op jit(solution)/shard_map/ppermute | solution.py:315
  19.7 6.1 %collective-permute-start.4 = (bf16[16,128]{1,0:T(8,128)(2,1)S(1)}, bf16[16,128]{1,0:T(8,128)(2,1)S(1)}, u32[]{:S(2)}, u32[]{:S(2)}) collective-permute-start(bf16[16,128]{1,0:T(8,128)(2,1)S(1)} %slice_bitcast_fusion), channel_id=1, source_target_pairs={{1,0},{3,2},{5,4},{7,6},{9,8},{11,10},{13,12},{15,14},{17,16},{19,... | collective-permute-start | bytes 12296 | tf_op jit(solution)/shard_map/ppermute | solution.py:369
  25.8 2.1 %collective-permute-start.5 = (bf16[2,3,4,2,16,256]{5,4,3,2,1,0:T(8,128)(2,1)S(1)}, bf16[2,3,4,2,16,256]{5,4,3,2,1,0:T(8,128)(2,1)S(1)}, u32[]{:S(2)}, u32[]{:S(2)}) collective-permute-start(bf16[2,3,4,2,16,256]{5,4,3,2,1,0:T(8,128)(2,1)S(1)} %get-tuple-element.16), channel_id=1, source_target_pairs={{0,16},{16,2},{2,18},{18,0},{4,20},{20,6},{6,22},{22,4},{8,24},{24... | collective-permute-start | bytes 1179656 | tf_op jit(solution)/shard_map/ppermute | solution.py:315
  26.4 1.4 %collective-permute-start.6 = (bf16[2,3,4,2,16,256]{5,4,3,2,1,0:T(8,128)(2,1)S(1)}, bf16[2,3,4,2,16,256]{5,4,3,2,1,0:T(8,128)(2,1)S(1)}, u32[]{:S(2)}, u32[]{:S(2)}) collective-permute-start(bf16[2,3,4,2,16,256]{5,4,3,2,1,0:T(8,128)(2,1)S(1)} %get-tuple-element.17), channel_id=1, source_target_pairs={{0,2},{16,18},{2,0},{18,16},{4,6},{20,22},{6,4},{22,20},{8,10},{24... | collective-permute-start | bytes 1179656 | tf_op jit(solution)/shard_map/ppermute | solution.py:315
  27.1 0.7 collective-permute-start.7
  91.9 33.0 %copy-start.1 = (bf16[8,32,32]{2,1,0:T(8,128)(2,1)S(1)}, bf16[8,32,32]{2,1,0:T(8,128)(2,1)}, u32[]{:S(2)}) copy-start(bf16[8,32,32]{2,1,0:T(8,128)(2,1)} %inv_ref.1) | copy-start | bytes 49156
  91.9 34.9 %copy-start = (bf16[3,16,32,2,256]{4,3,2,1,0:T(2,128)(2,1)S(1)}, bf16[3,16,32,2,256]{4,3,2,1,0:T(2,128)(2,1)}, u32[]{:S(2)}) copy-start(bf16[3,16,32,2,256]{4,3,2,1,0:T(2,128)(2,1)} %param.7) | copy-start | bytes 4718596
  91.9 34.9 %copy-start.2 = (s32[16,256]{1,0:T(8,128)S(1)}, s32[16,256]{1,0:T(8,128)}, u32[]{:S(2)}) copy-start(s32[16,256]{1,0:T(8,128)} %class_ref.1) | copy-start | bytes 49156
  91.9 34.9 %copy-start.3 = (s32[16]{0:T(128)S(1)}, s32[16]{0:T(128)}, u32[]{:S(2)}) copy-start(s32[16]{0:T(128)} %count_ref.1) | copy-start | bytes 196
  110.4 16.4 %collective-permute-start.8 = (bf16[4,3,4,2,16,256]{5,4,3,2,1,0:T(8,128)(2,1)S(1)}, bf16[4,3,4,2,16,256]{5,4,3,2,1,0:T(8,128)(2,1)S(1)}, u32[]{:S(2)}, u32[]{:S(2)}) collective-permute-start(bf16[4,3,4,2,16,256]{5,4,3,2,1,0:T(8,128)(2,1)S(1)} %gather.1), channel_id=1, source_target_pairs={{0,1},{1,0},{2,3},{3,2},{4,5},{5,4},{6,7},{7,6},{8,9},{9,8},{10,11... | collective-permute-start | bytes 2359304 | tf_op jit(solution)/shard_map/ppermute | solution.py:391

commit v4 on v3

--- a/solution.py
+++ b/solution.py
@@ -87,18 +87,8 @@
         w_ref[:, index * 128 : index * 128 + 128] = jnp.where(same, dot(rows, wide), 0.0).astype(BF)
 
 
-def cut_kernel(pos, v_hbm, out_ref, sems):
-    copies = []
-    for c in range(3):
-        for z in range(4):
-            first = pl.multiple_of(z * 32 + (1 - pos[3]) * 16, 16)
-            copies.append(pltpu.make_async_copy(v_hbm.at[c, :, pl.ds(first, 16)], out_ref.at[c, z], sems.at[c, z]))
-            copies[-1].start()
-    wait(copies)
-
-
-def pack_kernel(pos, v_hbm, other_ref, o0, o1, o2, o3, v_ref, sems):
-    outs = (o0, o1, o2, o3)
+def pack_kernel(pos, v_hbm, *refs, half):
+    outs, (v_ref, sems) = refs[-6:-2], refs[-2:]
     copies = []
     for c in range(3):
         for z in range(4):
@@ -107,23 +97,30 @@
             copies[-1].start()
     move, sort = mover(0), sorter(0)
     wait(copies)
-    places = [(step, core) for step in range(4) for core in range(2)]
     parts = []
-    for step, core in places:
+    for step in range(4):
         z = lax.rem(pos[2] + step, 4)
-        parts += [(other_ref if core else v_ref)[c, z].reshape(256, 128) for c in range(3)]
+        parts += [v_ref[c, z].reshape(256, 128) for c in range(3)]
     moved = dot(move, jnp.concatenate(parts, axis=1)).astype(BF)
     parts = []
-    for i in range(24):
+    for i in range(12):
         part = moved[:, i * 128 : i * 128 + 128]
         parts.append(jnp.concatenate([part[:128], part[128:]], axis=1))
     moved = dot(jnp.concatenate(parts, axis=0), sort).astype(BF)
-    for i, (step, core) in enumerate(places):
-        outs[step][core] = moved[i * 384 : (i + 1) * 384].reshape(3, 4, 2, 16, 256)
-
-
-def hold_kernel(token, a0, a1, a2, o0, o1, o2):
+    for step in range(4):
+        outs[step][half] = moved[step * 384 : (step + 1) * 384].reshape(3, 4, 2, 16, 256)
+
+
+def hold_kernel(*refs):
     pass
+
+
+def preload_kernel(after_ref, inv_ref, *refs):
+    copies = [pltpu.make_async_copy(refs[i], refs[3 + i], refs[7].at[i]) for i in range(3)]
+    for copy in copies:
+        copy.start()
+    place_kernel(inv_ref, refs[6])
+    wait(copies)
 
 
 def gather_kernel(n_ref, out_ref):
@@ -134,11 +131,8 @@
     return [pltpu.make_async_copy(table_hbm.at[p], table_ref.at[p], sems.at[p]) for p in range(2)]
 
 
-def synth_kernel(pos, r0, e1, e2, e3, l1, l2, l3, table_hbm, out_ref, lhs, table_ref, sems):
+def synth_kernel(pos, r0, e1, e2, e3, l1, l2, l3, table_ref, out_ref, lhs):
     nc = 3
-    copies = z_copies(table_hbm, table_ref, sems)
-    for copy in copies:
-        copy.start()
 
     def fill(step, block):
         z = lax.rem(pos[2] + 4 - step, 4)
@@ -166,7 +160,6 @@
     n = 128 * nc
     sums = []
     for parity in range(2):
-        copies[parity].wait()
         by_cos = dot(lhs[parity], table_ref[parity, 0])
         by_sin = dot(lhs[parity], table_ref[parity, 1])
         sums.append((by_cos[:n] - by_sin[n:], by_sin[:n] + by_cos[n:]))
@@ -182,16 +175,13 @@
                         out_ref[plane * 4 + half * 2 + quarter, c, ri] = mixed[:, quarter * 384 : quarter * 384 + 384]
 
 
-def middle_kernel(d_ref, synth_hbm, fold_hbm, out_ref, data, prod, synth_ref, fold_ref, sems, *, scale):
-    synth_copy = pltpu.make_async_copy(synth_hbm, synth_ref, sems.at[0])
-    fold_copy = pltpu.make_async_copy(fold_hbm, fold_ref, sems.at[1])
-    synth_copy.start()
+def middle_kernel(d_ref, synth_ref, fold_ref, table_hbm, out_ref, table_ref, data, prod, sem, *, scale):
+    table_copy = pltpu.make_async_copy(table_hbm, table_ref, sem)
+    table_copy.start()
     for parity in range(2):
         for c in range(3):
             part = d_ref[:, c, :, parity * 16 : parity * 16 + 16, :].reshape(512, 384)
             data[parity, :, c * 384 : c * 384 + 384] = part
-    synth_copy.wait()
-    fold_copy.start()
     for step in range(3):
         rows = slice(step * 256, step * 256 + 256)
         even = dot(synth_ref[0, rows, :], data[0])
@@ -202,19 +192,16 @@
             one, two = low[:, lanes] * low[:, 384:768], high[:, lanes] * high[:, 384:768]
             prod[0, rows, lanes] = (one + two).astype(BF)
             prod[1, rows, lanes] = (one - two).astype(BF)
-    fold_copy.wait()
     for parity in range(2):
         spectra = (dot(fold_ref[parity], prod[parity]) * scale).astype(BF)
         for c in range(3):
             part = spectra[:, c * 384 : c * 384 + 384].reshape(16, 2, 16, 384)
             out_ref[:, c, :, parity * 16 : parity * 16 + 16, :] = part
-
-
-def analyse_kernel(pos, b_ref, table_hbm, out_ref, lhs, table_ref, sems, *, scale):
+    table_copy.wait()
+
+
+def analyse_kernel(pos, b_ref, table_ref, out_ref, lhs, *, scale):
     nc = 3
-    copies = z_copies(table_hbm, table_ref, sems)
-    for copy in copies:
-        copy.start()
     n = 128 * nc
     for plane in range(4):
         for quarter in range(2):
@@ -226,7 +213,6 @@
                 lhs[0, rows, lanes] = (low + high).astype(BF)
                 lhs[1, rows, lanes] = (low - high).astype(BF)
     for parity in range(2):
-        copies[parity].wait()
         by_cos, by_sin = (
             lax.dot_general(
                 lhs[parity], table_ref[parity, i], (((1,), (1,)), ((), ())), preferred_element_type=jnp.float32
@@ -245,7 +231,7 @@
                             out_ref[block, other, c, plane, ri, :, lanes] = piece.reshape(16, 128).astype(BF)
 
 
-def solve_kernel(pos, count_ref, n_ref, other_ref, v_ref, w_ref, class_ref, out_ref, right, done, sems):
+def right_rows(pos, count_ref, blocks, other, v_ref, store):
     move, sort = mover(1), sorter(1)
     row = lax.broadcasted_iota(jnp.int32, (16, 16, 128), 1)
     kx = lax.broadcasted_iota(jnp.int32, (16, 16, 128), 0)
@@ -255,23 +241,38 @@
     counts = jnp.concatenate([jnp.full((1, 16, 128), count_ref[k], jnp.int32) for k in range(16)], axis=0)
     mean = (kx + pos[4] == 0) & (wavenumber == 0)
     half = jnp.where((jnp.abs(wavenumber) < counts) & jnp.logical_not(mean), 0.5, 0.0).astype(jnp.float32)
-    places = [(block, other) for block in range(4) for other in range(2)]
-    parts = [other_ref[block, c] if other else n_ref[block, 0, c] for block, other in places for c in range(3)]
-    both = dot(jnp.concatenate([part.reshape(128, 256) for part in parts], axis=0), sort).astype(BF)
-    both = [both[i * 128 : i * 128 + 128] for i in range(24)]
+    both = dot(jnp.concatenate([block.reshape(128, 256) for block in blocks], axis=0), sort).astype(BF)
+    both = [both[i * 128 : i * 128 + 128] for i in range(12)]
     both = [jnp.concatenate([part[:, :128], part[:, 128:]], axis=0) for part in both]
     moved = dot(move, jnp.concatenate(both, axis=1))
-    for i, (block, other) in enumerate(places):
-        z = (block % 2) * 2 + block // 2
-        group = z * 2 + lax.rem(pos[3] + other, 2)
-        rows = pl.ds(pl.multiple_of(group * 16, 16), 16)
+    for place in range(4):
+        z = (place % 2) * 2 + place // 2
+        rows = pl.ds(pl.multiple_of((z * 2 + lax.rem(pos[3] + other, 2)) * 16, 16), 16)
         for c in range(3):
             old = v_ref[c, :, rows, :].astype(jnp.float32)
-            lanes = slice((i * 3 + c) * 128, (i * 3 + c) * 128 + 128)
+            lanes = slice((place * 3 + c) * 128, (place * 3 + c) * 128 + 128)
             new = (old + moved[:, lanes].reshape(16, 16, 128) * half).astype(BF)
             for k in range(16):
-                right[k // 2, rows, (c * 2 + k % 2) * 128 : (c * 2 + k % 2) * 128 + 128] = new[k]
-
+                store(rows, place, c, k, new[k])
+
+
+def right_kernel(pos, count_ref, n_ref, v_ref, out_ref):
+    def store(rows, place, c, k, value):
+        out_ref[k // 2, place, :, (c * 2 + k % 2) * 128 : (c * 2 + k % 2) * 128 + 128] = value
+
+    right_rows(pos, count_ref, [n_ref[place, 0, c] for place in range(4) for c in range(3)], 0, v_ref, store)
+
+
+def solve_kernel(pos, count_ref, right_ref, other_ref, v_ref, w_ref, class_ref, out_ref, right, done, sems):
+    def store(rows, place, c, k, value):
+        right[k // 2, rows, (c * 2 + k % 2) * 128 : (c * 2 + k % 2) * 128 + 128] = value
+
+    right_rows(pos, count_ref, [other_ref[place, c] for place in range(4) for c in range(3)], 1, v_ref, store)
+    for place in range(4):
+        z = (place % 2) * 2 + place // 2
+        rows = pl.ds(pl.multiple_of((z * 2 + pos[3]) * 16, 16), 16)
+        for pair in range(8):
+            right[pair, rows, :] = right_ref[pair, place]
     early = (lax.broadcasted_iota(jnp.int32, (16, 128), 0) & 3) < 2
     copies = []
     for pair in range(8):
@@ -334,6 +335,7 @@
 
     mode_shape = jax.ShapeDtypeStruct((2, 3, 4, 2, 16, 256), BF)
     plane_shape = jax.ShapeDtypeStruct((16, 3, 2, 32, 384), BF)
+    table_shape = pltpu.VMEM((2, 2, 512, HALF), BF)
     smem, vmem, hbm, free = (spec(m) for m in (pltpu.SMEM, pltpu.VMEM, pltpu.HBM, pl.ANY))
 
     def call(kernel, name, specs, args, outs, scratch, aliases={}, out_spec=vmem):
@@ -348,50 +350,61 @@
             name=name,
         )(*args)
 
-    operators = pl.pallas_call(
-        place_kernel,
-        out_shape=jax.ShapeDtypeStruct((128, NCLASS * 128), BF),
-        compiler_params=params(),
-        name="place",
-    )(inverses)
-
     dma = pltpu.SemaphoreType.DMA
     fixed = in_hbm(lines)
-    piece_shape = jax.ShapeDtypeStruct((3, 4, 16, 16, 128), BF)
-    (piece,) = call(cut_kernel, "cut", [smem, hbm], (pos, fixed), [piece_shape], [dma((3, 4))])
-    piece = lax.ppermute(piece, "core", [(0, 1), (1, 0)])
+    other = lax.ppermute(velocity, "core", [(0, 1), (1, 0)])
+    other = other.reshape(3, 16, NY, 2, 2, 128).transpose(0, 1, 2, 4, 3, 5).reshape(3, 16, 128, 128)
+    scratch = [pltpu.VMEM((3, 4, 16, 16, 128), BF), dma((3, 4))]
     packed = call(
-        pack_kernel, "pack", [smem, hbm, vmem], (pos, fixed, piece), [mode_shape] * 4,
-        [pltpu.VMEM((3, 4, 16, 16, 128), BF), dma((3, 4))],
+        functools.partial(pack_kernel, half=0), "pack", [smem, hbm], (pos, fixed), [mode_shape] * 4, scratch
+    )
+    packed = call(
+        functools.partial(pack_kernel, half=1), "pack", [smem, free] + [vmem] * 4, (pos, other, *packed),
+        [mode_shape] * 4, scratch, {2: 0, 3: 1, 4: 2, 5: 3},
     )
     first = [along_z(packed[step], step, EARLY) for step in (1, 2, 3)]
-    token = sum(block[0, 0, 0, 0, :, :128].astype(jnp.float32) for block in first[:1]).astype(BF)
+    table, *x_held, operators = call(
+        preload_kernel, "preload", [free, vmem] + [hbm] * 3, (packed[0], inverses, z_basis, x_synth, x_fold),
+        [
+            table_shape, pltpu.VMEM((2, HALF, 512), BF), pltpu.VMEM((2, 512, HALF), BF),
+            jax.ShapeDtypeStruct((128, NCLASS * 128), BF),
+        ],
+        [dma((3,))],
+    )
+    token = first[0][0, 0, 0, 0, :, :128]
     token = lax.ppermute(token, "core", [(EARLY, 1 - EARLY)])
-    held = call(hold_kernel, "hold", [free] * 4, (token, *packed[1:]), [mode_shape] * 3, [], {1: 0, 2: 1, 3: 2}, free)
-    second = [along_z(held[step - 1], step, 1 - EARLY) for step in (1, 2, 3)]
+    held = call(
+        hold_kernel, "hold", [free] * 5, (token, table, packed[1], packed[2], packed[3]), [mode_shape] * 3, [],
+        {2: 0, 3: 1, 4: 2}, free,
+    )
+    ready = {1: held[0], 2: held[1], 3: held[2]}
+    second = [along_z(ready[step], step, 1 - EARLY) for step in (1, 2, 3)]
     (spread,) = call(
-        synth_kernel, "synth", [smem] + [vmem] * 7 + [hbm], (pos, packed[0], *first, *second, z_basis), [plane_shape],
-        [pltpu.VMEM((2, 768, 512), BF), *z_scratch],
-    )
-    (folded,) = call(
-        functools.partial(middle_kernel, scale=scale_x), "middle", [vmem, hbm, hbm],
-        (plane(spread), x_synth, x_fold), [plane_shape],
+        synth_kernel, "synth", [smem] + [vmem] * 8, (pos, packed[0], *first, *second, table), [plane_shape],
+        [pltpu.VMEM((2, 768, 512), BF)],
+    )
+    folded, table = call(
+        functools.partial(middle_kernel, scale=scale_x), "middle", [vmem] * 3 + [hbm],
+        (plane(spread), *x_held, z_basis), [plane_shape, table_shape],
         [
-            pltpu.VMEM((2, 512, 1152), BF), pltpu.VMEM((2, HALF, 1152), BF),
-            pltpu.VMEM((2, HALF, 512), BF), pltpu.VMEM((2, 512, HALF), BF), dma((2,)),
+            pltpu.VMEM((2, 512, 1152), BF), pltpu.VMEM((2, HALF, 1152), BF), dma(()),
         ],
     )
     (modes,) = call(
-        functools.partial(analyse_kernel, scale=scale_z), "analyse", [smem, vmem, hbm],
-        (pos, plane(folded), z_basis), [jax.ShapeDtypeStruct((4, *mode_shape.shape), BF)],
-        [pltpu.VMEM((2, 768, HALF), BF), *z_scratch],
+        functools.partial(analyse_kernel, scale=scale_z), "analyse", [smem, vmem, vmem],
+        (pos, plane(folded), table), [jax.ShapeDtypeStruct((4, *mode_shape.shape), BF)],
+        [pltpu.VMEM((2, 768, HALF), BF)],
     )
     modes = lax.all_to_all(modes, COLUMN, split_axis=0, concat_axis=0, tiled=True)
     (other,) = call(gather_kernel, "gather", [vmem], (modes,), [jax.ShapeDtypeStruct((4, 3, 4, 2, 16, 256), BF)], [])
     other = lax.ppermute(other, "core", [(0, 1), (1, 0)])
+    (right,) = call(
+        right_kernel, "right", [smem] * 2 + [vmem] * 2, (pos, keep_count, modes, lines),
+        [jax.ShapeDtypeStruct((8, 4, 16, 768), BF)], [],
+    )
     (solved,) = call(
         solve_kernel, "solve", [smem] * 2 + [vmem] * 5,
-        (pos, keep_count, modes, other, lines, operators, class_index),
+        (pos, keep_count, right, other, lines, operators, class_index),
         [jax.ShapeDtypeStruct((3, 16, 128, 128), jnp.float32)],
         [pltpu.VMEM((8, 128, 768), BF), pltpu.VMEM((3, 16, 128, 128), jnp.float32), dma((3, 8))],
         out_spec=free,

time: 132 us -> 125 us (0.947)
  waiting for transfers between devices: 8.25 us -> 3.26 us
  Pallas kernels: 26.5 us -> 24 us
    ppermute x6, waiting for transfers between devices: 4.81 us -> 1.93 us  [along_z(): return lax.ppermute(block, ('zl', 'zh', 'core'), pairs)]
    pallas_call x8 -> x10, Pallas kernels: 26.1 us -> 24 us  [call(): pl.pallas_call(kernel, in_specs=specs, out_specs=[out_spec] * len(outs),...]
  transfers between devices with their start and end apart: 9 -> 9, of which waited for: 4 -> 4; matrix products, arithmetic and copies ran while one was open for 0% -> 0% of each run, Pallas kernels for 0% -> 5%
where the time goes in v4:
time: 125 us; the launch traced here: 124 us
  blocking collectives  65.6 us (52%)
  starting transfers between devices  30.7 us (25%)
  Pallas kernels  24 us (19%)
  waiting for transfers between devices  3.26 us (3%)
    all_to_all x2, blocking collectives, plane(): lax.all_to_all(blocks, ('x', 'y'), split_axis=0, concat_axis=0, tiled=True)  47.2 us
    pallas_call x10, Pallas kernels, call(): pl.pallas_call(kernel, in_specs=specs, out_specs=[out_spec] * len(outs),...  24 us
    all_to_all x1, blocking collectives, body(): lax.all_to_all(modes, COLUMN, split_axis=0, concat_axis=0, tiled=True)  18.4 us
    ppermute x1, starting transfers between devices, body(): other = lax.ppermute(other, 'core', [(0, 1), (1, 0)])  14.5 us
    ppermute x6, starting transfers between devices, along_z(): return lax.ppermute(block, ('zl', 'zh', 'core'), pairs)  13.5 us
  transfers between devices with their start and end apart: 9, of which 4 were waited for; matrix products, arithmetic and copies ran while one was open for 0% of the time, Pallas kernels for 5%

profile of v4, /device:TPU:1, one launch (start us, length us, event | category | flops | bytes accessed | tf_op | source)
XLA Modules:
  0.0 124.1 jit_solution(7307261384089341153)
XLA Ops:
  0.0 1.4 %collective-permute-start = (bf16[3,16,32,2,256]{4,3,2,1,0:T(2,128)(2,1)}, bf16[3,16,32,2,256]{4,3,2,1,0:T(2,128)(2,1)S(1)}, u32[]{:S(2)}, u32[]{:S(2)}) collective-permute-start(bf16[3,16,32,2,256]{4,3,2,1,0:T(2,128)(2,1)} %param.7), channel_id=1, source_target_pairs={{0,1},{1,0},{2,3},{3,2},{4,5},{5,4},{6,7},{7,6},{8,9},{9,8},{10,11... | collective-permute-start | bytes 4718600 | tf_op jit(solution)/shard_map/ppermute | solution.py:355
  1.4 0.1 stack.23.pos
  1.5 0.0 copy-start.1
  1.5 2.4 %pack.2 = (bf16[2,3,4,2,16,256]{5,4,3,2,1,0:T(8,128)(2,1)S(1)}, bf16[2,3,4,2,16,256]{5,4,3,2,1,0:T(8,128)(2,1)S(1)}, bf16[2,3,4,2,16,256]{5,4,3,2,1,0:T(8,128)(2,1)S(1)}, bf16[2,3,4,2,16,256]{5,4,3,2,1,0:T(8,128)(2,1)S(1)}) custom-call(s32[5]{0:T(128)S(1)} %stack.23.pos, bf16[3,16,128,128]{3,2,1,0:T(8,128)(2,1)} %bitcast.22), custom_call_target="tpu_custom_call" | custom-call | tf_op jit(solution)/shard_map/pack/pallas_call | solution.py:342
  3.9 0.7 collective-permute-done
  4.7 1.6 %pack.3 = (bf16[2,3,4,2,16,256]{5,4,3,2,1,0:T(8,128)(2,1)S(1)}, bf16[2,3,4,2,16,256]{5,4,3,2,1,0:T(8,128)(2,1)S(1)}, bf16[2,3,4,2,16,256]{5,4,3,2,1,0:T(8,128)(2,1)S(1)}, bf16[2,3,4,2,16,256]{5,4,3,2,1,0:T(8,128)(2,1)S(1)}) custom-call(s32[5]{0:T(128)S(1)} %stack.23.pos, ...), custom_call_target="tpu_custom_call", output_to_operand_aliasing={{0}: (2, {}), {1}: (3, {}), {2}: (4, {}), {3}: (5, {})} | custom-call | tf_op jit(solution)/shard_map/pack/pallas_call | solution.py:342
  6.3 3.6 %collective-permute-start.1 = (bf16[2,3,4,2,16,256]{5,4,3,2,1,0:T(8,128)(2,1)S(1)}, bf16[2,3,4,2,16,256]{5,4,3,2,1,0:T(8,128)(2,1)S(1)}, u32[]{:S(2)}, u32[]{:S(2)}) collective-permute-start(bf16[2,3,4,2,16,256]{5,4,3,2,1,0:T(8,128)(2,1)S(1)} %get-tuple-element.27.refs_2_), channel_id=1, source_target_pairs={{1,17},{17,3},{3,19},{19,1},{5,21},{21,7},{7,23},{23,5},{9,25},{25... | collective-permute-start | bytes 1179656 | tf_op jit(solution)/shard_map/ppermute | solution.py:316
  9.9 5.2 %collective-permute-start.2 = (bf16[2,3,4,2,16,256]{5,4,3,2,1,0:T(8,128)(2,1)S(1)}, bf16[2,3,4,2,16,256]{5,4,3,2,1,0:T(8,128)(2,1)S(1)}, u32[]{:S(2)}, u32[]{:S(2)}) collective-permute-start(bf16[2,3,4,2,16,256]{5,4,3,2,1,0:T(8,128)(2,1)S(1)} %get-tuple-element.28.refs_3_), channel_id=1, source_target_pairs={{1,3},{17,19},{3,1},{19,17},{5,7},{21,23},{7,5},{23,21},{9,11},{25... | collective-permute-start | bytes 1179656 | tf_op jit(solution)/shard_map/ppermute | solution.py:316
  15.1 2.6 %collective-permute-start.3 = (bf16[2,3,4,2,16,256]{5,4,3,2,1,0:T(8,128)(2,1)S(1)}, bf16[2,3,4,2,16,256]{5,4,3,2,1,0:T(8,128)(2,1)S(1)}, u32[]{:S(2)}, u32[]{:S(2)}) collective-permute-start(bf16[2,3,4,2,16,256]{5,4,3,2,1,0:T(8,128)(2,1)S(1)} %get-tuple-element.29.refs_4_), channel_id=1, source_target_pairs={{1,19},{17,1},{3,17},{19,3},{5,23},{21,5},{7,21},{23,7},{9,27},{25... | collective-permute-start | bytes 1179656 | tf_op jit(solution)/shard_map/ppermute | solution.py:316
  17.8 0.0 collective-permute-done.1.e1
  17.8 1.3 %collective-permute-start.4 = (bf16[16,128]{1,0:T(8,128)(2,1)S(1)}, bf16[16,128]{1,0:T(8,128)(2,1)S(1)}, u32[]{:S(2)}, u32[]{:S(2)}) collective-permute-start(bf16[16,128]{1,0:T(8,128)(2,1)S(1)} %slice_bitcast_fusion), channel_id=1, source_target_pairs={{1,0},{3,2},{5,4},{7,6},{9,8},{11,10},{13,12},{15,14},{17,16},{19,... | collective-permute-start | bytes 12296 | tf_op jit(solution)/shard_map/ppermute | solution.py:375
  19.1 0.0 copy-done.1
  19.1 2.9 %preload.1 = (bf16[2,2,512,768]{3,2,1,0:T(8,128)(2,1)S(1)}, bf16[2,768,512]{2,1,0:T(8,128)(2,1)S(1)}, bf16[2,512,768]{2,1,0:T(8,128)(2,1)S(1)}, bf16[128,1024]{1,0:T(8,128)(2,1)S(1)}) custom-call(bf16[2,3,4,2,16,256]{5,4,3,2,1,0:T(8,128)(2,1)S(1)} %get-tuple-element.26.after_ref.r0, bf16[8,32,32]{2,1,0:T(8,128)(2,1)S(1)} %copy-done.1, ...), custom_call_target="tpu_custom_call" | custom-call | tf_op jit(solution)/shard_map/preload/pallas_call | solution.py:342
  22.0 0.6 collective-permute-done.2.e2
  22.6 1.3 %collective-permute-done.3.e3 = bf16[2,3,4,2,16,256]{5,4,3,2,1,0:T(8,128)(2,1)S(1)} collective-permute-done((bf16[2,3,4,2,16,256]{5,4,3,2,1,0:T(8,128)(2,1)S(1)}, bf16[2,3,4,2,16,256]{5,4,3,2,1,0:T(8,128)(2,1)S(1)}, u32[]{:S(2)}, u32[]{:S(2)}) %collective-permute-start.3) | collective-permute-done | bytes 393248 | tf_op jit(solution)/shard_map/ppermute | solution.py:316
  23.9 0.0 collective-permute-done.4.refs_0_
  23.9 0.7 collective-permute-start.5
  24.6 0.7 collective-permute-start.6
  25.3 0.7 collective-permute-start.7
  25.9 0.0 collective-permute-done.5.l1
  26.0 0.0 collective-permute-done.6.l2
  26.0 0.0 collective-permute-done.7.l3
  26.0 3.5 %synth.1 = bf16[16,3,2,32,384]{4,3,2,1,0:T(8,128)(2,1)S(1)} custom-call(s32[5]{0:T(128)S(1)} %stack.23.pos, bf16[2,3,4,2,16,256]{5,4,3,2,1,0:T(8,128)(2,1)S(1)} %get-tuple-element.26.after_ref.r0, bf16[2,3,4,2,16,256]{5,4,3,2,1,0:T(8,128)(2,1)S(1)} %collective-permute-done.1.e1, bf16[2,3,4,2,16,256]{5,4,3,2,1,0:T(8,128)(2,1)S(1)} %collective-permute-done.2.e2, ...), custom_call_target="tpu_custom_call" | custom-call | tf_op jit(solution)/shard_map/synth/pallas_call | solution.py:342
  29.4 25.2 %all_to_all.15.d_ref = bf16[16,3,2,32,384]{4,3,2,1,0:T(8,128)(2,1)S(1)} all-to-all(bf16[16,3,2,32,384]{4,3,2,1,0:T(8,128)(2,1)S(1)} %synth.1), channel_id=1, replica_groups=mesh['x'=4,'zl'=2,'y'=4,'zh'=2,'core'=2] {'x','y'}, dimensions={0} | all-to-all | bytes 4718592 | tf_op jit(solution)/shard_map/all_to_all | solution.py:320
  54.6 4.7 %middle.1 = (bf16[16,3,2,32,384]{4,3,2,1,0:T(8,128)(2,1)S(1)}, bf16[2,2,512,768]{3,2,1,0:T(8,128)(2,1)S(1)}) custom-call(bf16[16,3,2,32,384]{4,3,2,1,0:T(8,128)(2,1)S(1)} %all_to_all.15.d_ref, bf16[2,768,512]{2,1,0:T(8,128)(2,1)S(1)} %get-tuple-element.34.synth_ref, bf16[2,512,768]{2,1,0:T(8,128)(2,1)S(1)} %get-tuple-element.35.fold_ref, ...), custom_call_target="tpu_custom_call" | custom-call | tf_op jit(solution)/shard_map/middle/pallas_call | solution.py:342
  59.3 22.0 %all_to_all.16.b_ref = bf16[16,3,2,32,384]{4,3,2,1,0:T(8,128)(2,1)S(1)} all-to-all(bf16[16,3,2,32,384]{4,3,2,1,0:T(8,128)(2,1)S(1)} %get-tuple-element.36), channel_id=1, replica_groups=mesh['x'=4,'zl'=2,'y'=4,'zh'=2,'core'=2] {'x','y'}, dimensions={0} | all-to-all | bytes 4718592 | tf_op jit(solution)/shard_map/all_to_all | solution.py:320
  81.4 3.5 %analyse.1 = bf16[4,2,3,4,2,16,256]{6,5,4,3,2,1,0:T(8,128)(2,1)S(1)} custom-call(s32[5]{0:T(128)S(1)} %stack.23.pos, bf16[16,3,2,32,384]{4,3,2,1,0:T(8,128)(2,1)S(1)} %all_to_all.16.b_ref, bf16[2,2,512,768]{3,2,1,0:T(8,128)(2,1)S(1)} %get-tuple-element.37.table_ref), custom_call_target="tpu_custom_call" | custom-call | tf_op jit(solution)/shard_map/analyse/pallas_call | solution.py:342
  84.9 0.0 copy-start
  84.9 0.0 copy-start.3
  84.9 18.4 %all_to_all.17.n_ref = bf16[4,2,3,4,2,16,256]{6,5,4,3,2,1,0:T(8,128)(2,1)S(1)} all-to-all(bf16[4,2,3,4,2,16,256]{6,5,4,3,2,1,0:T(8,128)(2,1)S(1)} %analyse.1), channel_id=1, replica_groups=mesh['x'=4,'zl'=2,'y'=4,'zh'=2,'core'=2] {'zl','zh'}, dimensions={0} | all-to-all | bytes 3145728 | tf_op jit(solution)/shard_map/all_to_all | solution.py:398
  103.3 0.1 gather.1
  103.4 0.0 copy-start.2
  103.4 14.5 %collective-permute-start.8 = (bf16[4,3,4,2,16,256]{5,4,3,2,1,0:T(8,128)(2,1)S(1)}, bf16[4,3,4,2,16,256]{5,4,3,2,1,0:T(8,128)(2,1)S(1)}, u32[]{:S(2)}, u32[]{:S(2)}) collective-permute-start(bf16[4,3,4,2,16,256]{5,4,3,2,1,0:T(8,128)(2,1)S(1)} %gather.1), channel_id=1, source_target_pairs={{0,1},{1,0},{2,3},{3,2},{4,5},{5,4},{6,7},{7,6},{8,9},{9,8},{10,11... | collective-permute-start | bytes 2359304 | tf_op jit(solution)/shard_map/ppermute | solution.py:400
  117.9 0.0 copy-done
  117.9 0.0 copy-done.3
  117.9 1.3 %right.1.right_ref = bf16[8,4,16,768]{3,2,1,0:T(8,128)(2,1)S(1)} custom-call(s32[5]{0:T(128)S(1)} %stack.23.pos, s32[16]{0:T(128)S(1)} %copy-done.3, bf16[4,2,3,4,2,16,256]{6,5,4,3,2,1,0:T(8,128)(2,1)S(1)} %all_to_all.17.n_ref, bf16[3,16,128,128]{3,2,1,0:T(8,128)(2,1)S(1)} %bitcast.23), custom_call_target="tpu_custom_call" | custom-call | tf_op jit(solution)/shard_map/right/pallas_call | solution.py:342
  119.2 0.6 collective-permute-done.8.other_ref
  119.8 0.0 copy-done.2
  119.8 4.2 %solve.1 = f32[3,16,128,128]{3,2,1,0:T(8,128)} custom-call(s32[5]{0:T(128)S(1)} %stack.23.pos, s32[16]{0:T(128)S(1)} %copy-done.3, bf16[8,4,16,768]{3,2,1,0:T(8,128)(2,1)S(1)} %right.1.right_ref, bf16[4,3,4,2,16,256]{5,4,3,2,1,0:T(8,128)(2,1)S(1)} %collective-permute-done.8.other_ref, bf16[3,16,128,128]{3,2,1,0:T(8,128)(2,1)S(1)} %bitcast.24, ...), custom_call_target="tpu_custom_call" | custom-call | tf_op jit(solution)/shard_map/solve/pallas_call | solution.py:342
  (2 shorter events, 0.0 us)
Async XLA Ops:
  0.0 4.7 %collective-permute-start = (bf16[3,16,32,2,256]{4,3,2,1,0:T(2,128)(2,1)}, bf16[3,16,32,2,256]{4,3,2,1,0:T(2,128)(2,1)S(1)}, u32[]{:S(2)}, u32[]{:S(2)}) collective-permute-start(bf16[3,16,32,2,256]{4,3,2,1,0:T(2,128)(2,1)} %param.7), channel_id=1, source_target_pairs={{0,1},{1,0},{2,3},{3,2},{4,5},{5,4},{6,7},{7,6},{8,9},{9,8},{10,11... | collective-permute-start | bytes 4718600 | tf_op jit(solution)/shard_map/ppermute | solution.py:355
  1.5 17.6 %copy-start.1 = (bf16[8,32,32]{2,1,0:T(8,128)(2,1)S(1)}, bf16[8,32,32]{2,1,0:T(8,128)(2,1)}, u32[]{:S(2)}) copy-start(bf16[8,32,32]{2,1,0:T(8,128)(2,1)} %inv_ref.1) | copy-start | bytes 49156
  6.3 11.5 %collective-permute-start.1 = (bf16[2,3,4,2,16,256]{5,4,3,2,1,0:T(8,128)(2,1)S(1)}, bf16[2,3,4,2,16,256]{5,4,3,2,1,0:T(8,128)(2,1)S(1)}, u32[]{:S(2)}, u32[]{:S(2)}) collective-permute-start(bf16[2,3,4,2,16,256]{5,4,3,2,1,0:T(8,128)(2,1)S(1)} %get-tuple-element.27.refs_2_), channel_id=1, source_target_pairs={{1,17},{17,3},{3,19},{19,1},{5,21},{21,7},{7,23},{23,5},{9,25},{25... | collective-permute-start | bytes 1179656 | tf_op jit(solution)/shard_map/ppermute | solution.py:316
  9.9 12.7 %collective-permute-start.2 = (bf16[2,3,4,2,16,256]{5,4,3,2,1,0:T(8,128)(2,1)S(1)}, bf16[2,3,4,2,16,256]{5,4,3,2,1,0:T(8,128)(2,1)S(1)}, u32[]{:S(2)}, u32[]{:S(2)}) collective-permute-start(bf16[2,3,4,2,16,256]{5,4,3,2,1,0:T(8,128)(2,1)S(1)} %get-tuple-element.28.refs_3_), channel_id=1, source_target_pairs={{1,3},{17,19},{3,1},{19,17},{5,7},{21,23},{7,5},{23,21},{9,11},{25... | collective-permute-start | bytes 1179656 | tf_op jit(solution)/shard_map/ppermute | solution.py:316
  15.1 8.8 %collective-permute-start.3 = (bf16[2,3,4,2,16,256]{5,4,3,2,1,0:T(8,128)(2,1)S(1)}, bf16[2,3,4,2,16,256]{5,4,3,2,1,0:T(8,128)(2,1)S(1)}, u32[]{:S(2)}, u32[]{:S(2)}) collective-permute-start(bf16[2,3,4,2,16,256]{5,4,3,2,1,0:T(8,128)(2,1)S(1)} %get-tuple-element.29.refs_4_), channel_id=1, source_target_pairs={{1,19},{17,1},{3,17},{19,3},{5,23},{21,5},{7,21},{23,7},{9,27},{25... | collective-permute-start | bytes 1179656 | tf_op jit(solution)/shard_map/ppermute | solution.py:316
  17.8 6.1 %collective-permute-start.4 = (bf16[16,128]{1,0:T(8,128)(2,1)S(1)}, bf16[16,128]{1,0:T(8,128)(2,1)S(1)}, u32[]{:S(2)}, u32[]{:S(2)}) collective-permute-start(bf16[16,128]{1,0:T(8,128)(2,1)S(1)} %slice_bitcast_fusion), channel_id=1, source_target_pairs={{1,0},{3,2},{5,4},{7,6},{9,8},{11,10},{13,12},{15,14},{17,16},{19,... | collective-permute-start | bytes 12296 | tf_op jit(solution)/shard_map/ppermute | solution.py:375
  23.9 2.1 %collective-permute-start.5 = (bf16[2,3,4,2,16,256]{5,4,3,2,1,0:T(8,128)(2,1)S(1)}, bf16[2,3,4,2,16,256]{5,4,3,2,1,0:T(8,128)(2,1)S(1)}, u32[]{:S(2)}, u32[]{:S(2)}) collective-permute-start(bf16[2,3,4,2,16,256]{5,4,3,2,1,0:T(8,128)(2,1)S(1)} %get-tuple-element.31), channel_id=1, source_target_pairs={{0,16},{16,2},{2,18},{18,0},{4,20},{20,6},{6,22},{22,4},{8,24},{24... | collective-permute-start | bytes 1179656 | tf_op jit(solution)/shard_map/ppermute | solution.py:316
  24.6 1.4 %collective-permute-start.6 = (bf16[2,3,4,2,16,256]{5,4,3,2,1,0:T(8,128)(2,1)S(1)}, bf16[2,3,4,2,16,256]{5,4,3,2,1,0:T(8,128)(2,1)S(1)}, u32[]{:S(2)}, u32[]{:S(2)}) collective-permute-start(bf16[2,3,4,2,16,256]{5,4,3,2,1,0:T(8,128)(2,1)S(1)} %get-tuple-element.32), channel_id=1, source_target_pairs={{0,2},{16,18},{2,0},{18,16},{4,6},{20,22},{6,4},{22,20},{8,10},{24... | collective-permute-start | bytes 1179656 | tf_op jit(solution)/shard_map/ppermute | solution.py:316
  25.3 0.7 collective-permute-start.7
  84.9 33.0 %copy-start = (bf16[3,16,32,2,256]{4,3,2,1,0:T(2,128)(2,1)S(1)}, bf16[3,16,32,2,256]{4,3,2,1,0:T(2,128)(2,1)}, u32[]{:S(2)}) copy-start(bf16[3,16,32,2,256]{4,3,2,1,0:T(2,128)(2,1)} %param.7) | copy-start | bytes 4718596
  84.9 33.0 %copy-start.3 = (s32[16]{0:T(128)S(1)}, s32[16]{0:T(128)}, u32[]{:S(2)}) copy-start(s32[16]{0:T(128)} %count_ref.3) | copy-start | bytes 196
  103.4 16.4 %copy-start.2 = (s32[16,256]{1,0:T(8,128)S(1)}, s32[16,256]{1,0:T(8,128)}, u32[]{:S(2)}) copy-start(s32[16,256]{1,0:T(8,128)} %class_ref.1) | copy-start | bytes 49156
  103.4 16.4 %collective-permute-start.8 = (bf16[4,3,4,2,16,256]{5,4,3,2,1,0:T(8,128)(2,1)S(1)}, bf16[4,3,4,2,16,256]{5,4,3,2,1,0:T(8,128)(2,1)S(1)}, u32[]{:S(2)}, u32[]{:S(2)}) collective-permute-start(bf16[4,3,4,2,16,256]{5,4,3,2,1,0:T(8,128)(2,1)S(1)} %gather.1), channel_id=1, source_target_pairs={{0,1},{1,0},{2,3},{3,2},{4,5},{5,4},{6,7},{7,6},{8,9},{9,8},{10,11... | collective-permute-start | bytes 2359304 | tf_op jit(solution)/shard_map/ppermute | solution.py:400

commit v5 on v4

--- a/solution.py
+++ b/solution.py
@@ -88,7 +88,7 @@
 
 
 def pack_kernel(pos, v_hbm, *refs, half):
-    outs, (v_ref, sems) = refs[-6:-2], refs[-2:]
+    own, outs, (v_ref, sems) = refs[:-6], refs[-6:-2], refs[-2:]
     copies = []
     for c in range(3):
         for z in range(4):
@@ -108,6 +108,8 @@
         parts.append(jnp.concatenate([part[:128], part[128:]], axis=1))
     moved = dot(jnp.concatenate(parts, axis=0), sort).astype(BF)
     for step in range(4):
+        if half:
+            outs[step][0] = own[step][0]
         outs[step][half] = moved[step * 384 : (step + 1) * 384].reshape(3, 4, 2, 16, 256)
 
 
@@ -350,17 +352,18 @@
             name=name,
         )(*args)
 
+    half_shape = jax.ShapeDtypeStruct((1, 3, 4, 2, 16, 256), BF)
     dma = pltpu.SemaphoreType.DMA
     fixed = in_hbm(lines)
     other = lax.ppermute(velocity, "core", [(0, 1), (1, 0)])
     other = other.reshape(3, 16, NY, 2, 2, 128).transpose(0, 1, 2, 4, 3, 5).reshape(3, 16, 128, 128)
     scratch = [pltpu.VMEM((3, 4, 16, 16, 128), BF), dma((3, 4))]
     packed = call(
-        functools.partial(pack_kernel, half=0), "pack", [smem, hbm], (pos, fixed), [mode_shape] * 4, scratch
+        functools.partial(pack_kernel, half=0), "pack", [smem, hbm], (pos, fixed), [half_shape] * 4, scratch
     )
     packed = call(
         functools.partial(pack_kernel, half=1), "pack", [smem, free] + [vmem] * 4, (pos, other, *packed),
-        [mode_shape] * 4, scratch, {2: 0, 3: 1, 4: 2, 5: 3},
+        [mode_shape] * 4, scratch,
     )
     first = [along_z(packed[step], step, EARLY) for step in (1, 2, 3)]
     table, *x_held, operators = call(

time: 125 us -> 125 us (level)
  no operation moved by 1% of the time
where the time goes in v5:
time: 125 us; the launch traced here: 124 us
  blocking collectives  65.6 us (52%)
  starting transfers between devices  30.7 us (25%)
  Pallas kernels  24.2 us (19%)
  waiting for transfers between devices  3.27 us (3%)
    all_to_all x2, blocking collectives, plane(): lax.all_to_all(blocks, ('x', 'y'), split_axis=0, concat_axis=0, tiled=True)  47.2 us
    pallas_call x10, Pallas kernels, call(): pl.pallas_call(kernel, in_specs=specs, out_specs=[out_spec] * len(outs),...  24.2 us
    all_to_all x1, blocking collectives, body(): lax.all_to_all(modes, COLUMN, split_axis=0, concat_axis=0, tiled=True)  18.4 us
    ppermute x1, starting transfers between devices, body(): other = lax.ppermute(other, 'core', [(0, 1), (1, 0)])  14.5 us
    ppermute x6, starting transfers between devices, along_z(): return lax.ppermute(block, ('zl', 'zh', 'core'), pairs)  13.5 us
  transfers between devices with their start and end apart: 9, of which 4 were waited for; matrix products, arithmetic and copies ran while one was open for 0% of the time, Pallas kernels for 5%

profile of v5, /device:TPU:1, one launch (start us, length us, event | category | flops | bytes accessed | tf_op | source)
XLA Modules:
  0.0 124.2 jit_solution(18089172711205567937)
XLA Ops:
  0.0 0.0 copy-start.1
  0.0 1.4 %collective-permute-start = (bf16[3,16,32,2,256]{4,3,2,1,0:T(2,128)(2,1)}, bf16[3,16,32,2,256]{4,3,2,1,0:T(2,128)(2,1)S(1)}, u32[]{:S(2)}, u32[]{:S(2)}) collective-permute-start(bf16[3,16,32,2,256]{4,3,2,1,0:T(2,128)(2,1)} %param.7), channel_id=1, source_target_pairs={{0,1},{1,0},{2,3},{3,2},{4,5},{5,4},{6,7},{7,6},{8,9},{9,8},{10,11... | collective-permute-start | bytes 4718600 | tf_op jit(solution)/shard_map/ppermute | solution.py:358
  1.4 0.1 stack.23.pos
  1.5 2.4 %pack.2 = (bf16[1,3,4,2,16,256]{5,4,3,2,1,0:T(8,128)(2,1)S(1)}, bf16[1,3,4,2,16,256]{5,4,3,2,1,0:T(8,128)(2,1)S(1)}, bf16[1,3,4,2,16,256]{5,4,3,2,1,0:T(8,128)(2,1)S(1)}, bf16[1,3,4,2,16,256]{5,4,3,2,1,0:T(8,128)(2,1)S(1)}) custom-call(s32[5]{0:T(128)S(1)} %stack.23.pos, bf16[3,16,128,128]{3,2,1,0:T(8,128)(2,1)} %bitcast.22), custom_call_target="tpu_custom_call" | custom-call | tf_op jit(solution)/shard_map/pack/pallas_call | solution.py:344
  3.9 0.7 collective-permute-done
  4.7 1.6 %pack.3 = (bf16[2,3,4,2,16,256]{5,4,3,2,1,0:T(8,128)(2,1)S(1)}, bf16[2,3,4,2,16,256]{5,4,3,2,1,0:T(8,128)(2,1)S(1)}, bf16[2,3,4,2,16,256]{5,4,3,2,1,0:T(8,128)(2,1)S(1)}, bf16[2,3,4,2,16,256]{5,4,3,2,1,0:T(8,128)(2,1)S(1)}) custom-call(s32[5]{0:T(128)S(1)} %stack.23.pos, bf16[3,16,128,128]{3,2,1,0:T(8,128)(2,1)S(1)} %bitcast.25, ...), custom_call_target="tpu_custom_call" | custom-call | tf_op jit(solution)/shard_map/pack/pallas_call | solution.py:344
  6.3 3.6 %collective-permute-start.1 = (bf16[2,3,4,2,16,256]{5,4,3,2,1,0:T(8,128)(2,1)S(1)}, bf16[2,3,4,2,16,256]{5,4,3,2,1,0:T(8,128)(2,1)S(1)}, u32[]{:S(2)}, u32[]{:S(2)}) collective-permute-start(bf16[2,3,4,2,16,256]{5,4,3,2,1,0:T(8,128)(2,1)S(1)} %get-tuple-element.27.refs_2_), channel_id=1, source_target_pairs={{1,17},{17,3},{3,19},{19,1},{5,21},{21,7},{7,23},{23,5},{9,25},{25... | collective-permute-start | bytes 1179656 | tf_op jit(solution)/shard_map/ppermute | solution.py:318
  9.9 5.2 %collective-permute-start.2 = (bf16[2,3,4,2,16,256]{5,4,3,2,1,0:T(8,128)(2,1)S(1)}, bf16[2,3,4,2,16,256]{5,4,3,2,1,0:T(8,128)(2,1)S(1)}, u32[]{:S(2)}, u32[]{:S(2)}) collective-permute-start(bf16[2,3,4,2,16,256]{5,4,3,2,1,0:T(8,128)(2,1)S(1)} %get-tuple-element.28.refs_3_), channel_id=1, source_target_pairs={{1,3},{17,19},{3,1},{19,17},{5,7},{21,23},{7,5},{23,21},{9,11},{25... | collective-permute-start | bytes 1179656 | tf_op jit(solution)/shard_map/ppermute | solution.py:318
  15.2 2.6 %collective-permute-start.3 = (bf16[2,3,4,2,16,256]{5,4,3,2,1,0:T(8,128)(2,1)S(1)}, bf16[2,3,4,2,16,256]{5,4,3,2,1,0:T(8,128)(2,1)S(1)}, u32[]{:S(2)}, u32[]{:S(2)}) collective-permute-start(bf16[2,3,4,2,16,256]{5,4,3,2,1,0:T(8,128)(2,1)S(1)} %get-tuple-element.29.refs_4_), channel_id=1, source_target_pairs={{1,19},{17,1},{3,17},{19,3},{5,23},{21,5},{7,21},{23,7},{9,27},{25... | collective-permute-start | bytes 1179656 | tf_op jit(solution)/shard_map/ppermute | solution.py:318
  17.8 0.0 collective-permute-done.1.e1
  17.8 1.3 %collective-permute-start.4 = (bf16[16,128]{1,0:T(8,128)(2,1)S(1)}, bf16[16,128]{1,0:T(8,128)(2,1)S(1)}, u32[]{:S(2)}, u32[]{:S(2)}) collective-permute-start(bf16[16,128]{1,0:T(8,128)(2,1)S(1)} %slice_bitcast_fusion), channel_id=1, source_target_pairs={{1,0},{3,2},{5,4},{7,6},{9,8},{11,10},{13,12},{15,14},{17,16},{19,... | collective-permute-start | bytes 12296 | tf_op jit(solution)/shard_map/ppermute | solution.py:378
  19.1 0.0 copy-done.1
  19.1 2.9 %preload.1 = (bf16[2,2,512,768]{3,2,1,0:T(8,128)(2,1)S(1)}, bf16[2,768,512]{2,1,0:T(8,128)(2,1)S(1)}, bf16[2,512,768]{2,1,0:T(8,128)(2,1)S(1)}, bf16[128,1024]{1,0:T(8,128)(2,1)S(1)}) custom-call(bf16[2,3,4,2,16,256]{5,4,3,2,1,0:T(8,128)(2,1)S(1)} %get-tuple-element.26.after_ref.r0, bf16[8,32,32]{2,1,0:T(8,128)(2,1)S(1)} %copy-done.1, ...), custom_call_target="tpu_custom_call" | custom-call | tf_op jit(solution)/shard_map/preload/pallas_call | solution.py:344
  22.0 0.6 collective-permute-done.2.e2
  22.6 1.3 %collective-permute-done.3.e3 = bf16[2,3,4,2,16,256]{5,4,3,2,1,0:T(8,128)(2,1)S(1)} collective-permute-done((bf16[2,3,4,2,16,256]{5,4,3,2,1,0:T(8,128)(2,1)S(1)}, bf16[2,3,4,2,16,256]{5,4,3,2,1,0:T(8,128)(2,1)S(1)}, u32[]{:S(2)}, u32[]{:S(2)}) %collective-permute-start.3) | collective-permute-done | bytes 393248 | tf_op jit(solution)/shard_map/ppermute | solution.py:318
  23.9 0.0 collective-permute-done.4.refs_0_
  23.9 0.7 collective-permute-start.5
  24.6 0.7 collective-permute-start.6
  25.3 0.7 collective-permute-start.7
  26.0 0.0 collective-permute-done.5.l1
  26.0 0.0 collective-permute-done.6.l2
  26.0 0.0 collective-permute-done.7.l3
  26.0 3.5 %synth.1 = bf16[16,3,2,32,384]{4,3,2,1,0:T(8,128)(2,1)S(1)} custom-call(s32[5]{0:T(128)S(1)} %stack.23.pos, bf16[2,3,4,2,16,256]{5,4,3,2,1,0:T(8,128)(2,1)S(1)} %get-tuple-element.26.after_ref.r0, bf16[2,3,4,2,16,256]{5,4,3,2,1,0:T(8,128)(2,1)S(1)} %collective-permute-done.1.e1, bf16[2,3,4,2,16,256]{5,4,3,2,1,0:T(8,128)(2,1)S(1)} %collective-permute-done.2.e2, ...), custom_call_target="tpu_custom_call" | custom-call | tf_op jit(solution)/shard_map/synth/pallas_call | solution.py:344
  29.5 25.2 %all_to_all.15.d_ref = bf16[16,3,2,32,384]{4,3,2,1,0:T(8,128)(2,1)S(1)} all-to-all(bf16[16,3,2,32,384]{4,3,2,1,0:T(8,128)(2,1)S(1)} %synth.1), channel_id=1, replica_groups=mesh['x'=4,'zl'=2,'y'=4,'zh'=2,'core'=2] {'x','y'}, dimensions={0} | all-to-all | bytes 4718592 | tf_op jit(solution)/shard_map/all_to_all | solution.py:322
  54.7 4.8 %middle.1 = (bf16[16,3,2,32,384]{4,3,2,1,0:T(8,128)(2,1)S(1)}, bf16[2,2,512,768]{3,2,1,0:T(8,128)(2,1)S(1)}) custom-call(bf16[16,3,2,32,384]{4,3,2,1,0:T(8,128)(2,1)S(1)} %all_to_all.15.d_ref, bf16[2,768,512]{2,1,0:T(8,128)(2,1)S(1)} %get-tuple-element.34.synth_ref, bf16[2,512,768]{2,1,0:T(8,128)(2,1)S(1)} %get-tuple-element.35.fold_ref, ...), custom_call_target="tpu_custom_call" | custom-call | tf_op jit(solution)/shard_map/middle/pallas_call | solution.py:344
  59.4 22.0 %all_to_all.16.b_ref = bf16[16,3,2,32,384]{4,3,2,1,0:T(8,128)(2,1)S(1)} all-to-all(bf16[16,3,2,32,384]{4,3,2,1,0:T(8,128)(2,1)S(1)} %get-tuple-element.36), channel_id=1, replica_groups=mesh['x'=4,'zl'=2,'y'=4,'zh'=2,'core'=2] {'x','y'}, dimensions={0} | all-to-all | bytes 4718592 | tf_op jit(solution)/shard_map/all_to_all | solution.py:322
  81.5 3.5 %analyse.1 = bf16[4,2,3,4,2,16,256]{6,5,4,3,2,1,0:T(8,128)(2,1)S(1)} custom-call(s32[5]{0:T(128)S(1)} %stack.23.pos, bf16[16,3,2,32,384]{4,3,2,1,0:T(8,128)(2,1)S(1)} %all_to_all.16.b_ref, bf16[2,2,512,768]{3,2,1,0:T(8,128)(2,1)S(1)} %get-tuple-element.37.table_ref), custom_call_target="tpu_custom_call" | custom-call | tf_op jit(solution)/shard_map/analyse/pallas_call | solution.py:344
  85.0 0.0 copy-start
  85.0 0.0 copy-start.3
  85.0 18.4 %all_to_all.17.n_ref = bf16[4,2,3,4,2,16,256]{6,5,4,3,2,1,0:T(8,128)(2,1)S(1)} all-to-all(bf16[4,2,3,4,2,16,256]{6,5,4,3,2,1,0:T(8,128)(2,1)S(1)} %analyse.1), channel_id=1, replica_groups=mesh['x'=4,'zl'=2,'y'=4,'zh'=2,'core'=2] {'zl','zh'}, dimensions={0} | all-to-all | bytes 3145728 | tf_op jit(solution)/shard_map/all_to_all | solution.py:401
  103.4 0.1 gather.1
  103.5 0.0 copy-start.2
  103.5 14.5 %collective-permute-start.8 = (bf16[4,3,4,2,16,256]{5,4,3,2,1,0:T(8,128)(2,1)S(1)}, bf16[4,3,4,2,16,256]{5,4,3,2,1,0:T(8,128)(2,1)S(1)}, u32[]{:S(2)}, u32[]{:S(2)}) collective-permute-start(bf16[4,3,4,2,16,256]{5,4,3,2,1,0:T(8,128)(2,1)S(1)} %gather.1), channel_id=1, source_target_pairs={{0,1},{1,0},{2,3},{3,2},{4,5},{5,4},{6,7},{7,6},{8,9},{9,8},{10,11... | collective-permute-start | bytes 2359304 | tf_op jit(solution)/shard_map/ppermute | solution.py:403
  118.0 0.0 copy-done
  118.0 0.0 copy-done.3
  118.0 1.3 %right.1.right_ref = bf16[8,4,16,768]{3,2,1,0:T(8,128)(2,1)S(1)} custom-call(s32[5]{0:T(128)S(1)} %stack.23.pos, s32[16]{0:T(128)S(1)} %copy-done.3, bf16[4,2,3,4,2,16,256]{6,5,4,3,2,1,0:T(8,128)(2,1)S(1)} %all_to_all.17.n_ref, bf16[3,16,128,128]{3,2,1,0:T(8,128)(2,1)S(1)} %bitcast.23), custom_call_target="tpu_custom_call" | custom-call | tf_op jit(solution)/shard_map/right/pallas_call | solution.py:344
  119.3 0.6 collective-permute-done.8.other_ref
  119.9 0.0 copy-done.2
  119.9 4.2 %solve.1 = f32[3,16,128,128]{3,2,1,0:T(8,128)} custom-call(s32[5]{0:T(128)S(1)} %stack.23.pos, s32[16]{0:T(128)S(1)} %copy-done.3, bf16[8,4,16,768]{3,2,1,0:T(8,128)(2,1)S(1)} %right.1.right_ref, bf16[4,3,4,2,16,256]{5,4,3,2,1,0:T(8,128)(2,1)S(1)} %collective-permute-done.8.other_ref, bf16[3,16,128,128]{3,2,1,0:T(8,128)(2,1)S(1)} %bitcast.24, ...), custom_call_target="tpu_custom_call" | custom-call | tf_op jit(solution)/shard_map/solve/pallas_call | solution.py:344
  (2 shorter events, 0.0 us)
Async XLA Ops:
  0.0 19.1 %copy-start.1 = (bf16[8,32,32]{2,1,0:T(8,128)(2,1)S(1)}, bf16[8,32,32]{2,1,0:T(8,128)(2,1)}, u32[]{:S(2)}) copy-start(bf16[8,32,32]{2,1,0:T(8,128)(2,1)} %inv_ref.1) | copy-start | bytes 49156
  0.0 4.7 %collective-permute-start = (bf16[3,16,32,2,256]{4,3,2,1,0:T(2,128)(2,1)}, bf16[3,16,32,2,256]{4,3,2,1,0:T(2,128)(2,1)S(1)}, u32[]{:S(2)}, u32[]{:S(2)}) collective-permute-start(bf16[3,16,32,2,256]{4,3,2,1,0:T(2,128)(2,1)} %param.7), channel_id=1, source_target_pairs={{0,1},{1,0},{2,3},{3,2},{4,5},{5,4},{6,7},{7,6},{8,9},{9,8},{10,11... | collective-permute-start | bytes 4718600 | tf_op jit(solution)/shard_map/ppermute | solution.py:358
  6.3 11.5 %collective-permute-start.1 = (bf16[2,3,4,2,16,256]{5,4,3,2,1,0:T(8,128)(2,1)S(1)}, bf16[2,3,4,2,16,256]{5,4,3,2,1,0:T(8,128)(2,1)S(1)}, u32[]{:S(2)}, u32[]{:S(2)}) collective-permute-start(bf16[2,3,4,2,16,256]{5,4,3,2,1,0:T(8,128)(2,1)S(1)} %get-tuple-element.27.refs_2_), channel_id=1, source_target_pairs={{1,17},{17,3},{3,19},{19,1},{5,21},{21,7},{7,23},{23,5},{9,25},{25... | collective-permute-start | bytes 1179656 | tf_op jit(solution)/shard_map/ppermute | solution.py:318
  9.9 12.7 %collective-permute-start.2 = (bf16[2,3,4,2,16,256]{5,4,3,2,1,0:T(8,128)(2,1)S(1)}, bf16[2,3,4,2,16,256]{5,4,3,2,1,0:T(8,128)(2,1)S(1)}, u32[]{:S(2)}, u32[]{:S(2)}) collective-permute-start(bf16[2,3,4,2,16,256]{5,4,3,2,1,0:T(8,128)(2,1)S(1)} %get-tuple-element.28.refs_3_), channel_id=1, source_target_pairs={{1,3},{17,19},{3,1},{19,17},{5,7},{21,23},{7,5},{23,21},{9,11},{25... | collective-permute-start | bytes 1179656 | tf_op jit(solution)/shard_map/ppermute | solution.py:318
  15.2 8.8 %collective-permute-start.3 = (bf16[2,3,4,2,16,256]{5,4,3,2,1,0:T(8,128)(2,1)S(1)}, bf16[2,3,4,2,16,256]{5,4,3,2,1,0:T(8,128)(2,1)S(1)}, u32[]{:S(2)}, u32[]{:S(2)}) collective-permute-start(bf16[2,3,4,2,16,256]{5,4,3,2,1,0:T(8,128)(2,1)S(1)} %get-tuple-element.29.refs_4_), channel_id=1, source_target_pairs={{1,19},{17,1},{3,17},{19,3},{5,23},{21,5},{7,21},{23,7},{9,27},{25... | collective-permute-start | bytes 1179656 | tf_op jit(solution)/shard_map/ppermute | solution.py:318
  17.8 6.1 %collective-permute-start.4 = (bf16[16,128]{1,0:T(8,128)(2,1)S(1)}, bf16[16,128]{1,0:T(8,128)(2,1)S(1)}, u32[]{:S(2)}, u32[]{:S(2)}) collective-permute-start(bf16[16,128]{1,0:T(8,128)(2,1)S(1)} %slice_bitcast_fusion), channel_id=1, source_target_pairs={{1,0},{3,2},{5,4},{7,6},{9,8},{11,10},{13,12},{15,14},{17,16},{19,... | collective-permute-start | bytes 12296 | tf_op jit(solution)/shard_map/ppermute | solution.py:378
  23.9 2.1 %collective-permute-start.5 = (bf16[2,3,4,2,16,256]{5,4,3,2,1,0:T(8,128)(2,1)S(1)}, bf16[2,3,4,2,16,256]{5,4,3,2,1,0:T(8,128)(2,1)S(1)}, u32[]{:S(2)}, u32[]{:S(2)}) collective-permute-start(bf16[2,3,4,2,16,256]{5,4,3,2,1,0:T(8,128)(2,1)S(1)} %get-tuple-element.31), channel_id=1, source_target_pairs={{0,16},{16,2},{2,18},{18,0},{4,20},{20,6},{6,22},{22,4},{8,24},{24... | collective-permute-start | bytes 1179656 | tf_op jit(solution)/shard_map/ppermute | solution.py:318
  24.6 1.4 %collective-permute-start.6 = (bf16[2,3,4,2,16,256]{5,4,3,2,1,0:T(8,128)(2,1)S(1)}, bf16[2,3,4,2,16,256]{5,4,3,2,1,0:T(8,128)(2,1)S(1)}, u32[]{:S(2)}, u32[]{:S(2)}) collective-permute-start(bf16[2,3,4,2,16,256]{5,4,3,2,1,0:T(8,128)(2,1)S(1)} %get-tuple-element.32), channel_id=1, source_target_pairs={{0,2},{16,18},{2,0},{18,16},{4,6},{20,22},{6,4},{22,20},{8,10},{24... | collective-permute-start | bytes 1179656 | tf_op jit(solution)/shard_map/ppermute | solution.py:318
  25.3 0.7 collective-permute-start.7
  85.0 33.0 %copy-start = (bf16[3,16,32,2,256]{4,3,2,1,0:T(2,128)(2,1)S(1)}, bf16[3,16,32,2,256]{4,3,2,1,0:T(2,128)(2,1)}, u32[]{:S(2)}) copy-start(bf16[3,16,32,2,256]{4,3,2,1,0:T(2,128)(2,1)} %param.7) | copy-start | bytes 4718596
  85.0 33.0 %copy-start.3 = (s32[16]{0:T(128)S(1)}, s32[16]{0:T(128)}, u32[]{:S(2)}) copy-start(s32[16]{0:T(128)} %count_ref.3) | copy-start | bytes 196
  103.5 16.4 %copy-start.2 = (s32[16,256]{1,0:T(8,128)S(1)}, s32[16,256]{1,0:T(8,128)}, u32[]{:S(2)}) copy-start(s32[16,256]{1,0:T(8,128)} %class_ref.1) | copy-start | bytes 49156
  103.5 16.4 %collective-permute-start.8 = (bf16[4,3,4,2,16,256]{5,4,3,2,1,0:T(8,128)(2,1)S(1)}, bf16[4,3,4,2,16,256]{5,4,3,2,1,0:T(8,128)(2,1)S(1)}, u32[]{:S(2)}, u32[]{:S(2)}) collective-permute-start(bf16[4,3,4,2,16,256]{5,4,3,2,1,0:T(8,128)(2,1)S(1)} %gather.1), channel_id=1, source_target_pairs={{0,1},{1,0},{2,3},{3,2},{4,5},{5,4},{6,7},{7,6},{8,9},{9,8},{10,11... | collective-permute-start | bytes 2359304 | tf_op jit(solution)/shard_map/ppermute | solution.py:403

commit v6 on v5

--- a/solution.py
+++ b/solution.py
@@ -374,7 +374,7 @@
         ],
         [dma((3,))],
     )
-    token = first[0][0, 0, 0, 0, :, :128]
+    token = packed[0][0, 0, 0, 0, :, :128]
     token = lax.ppermute(token, "core", [(EARLY, 1 - EARLY)])
     held = call(
         hold_kernel, "hold", [free] * 5, (token, table, packed[1], packed[2], packed[3]), [mode_shape] * 3, [],

time: 125 us -> 125 us (level)
  no operation moved by 1% of the time
where the time goes in v6:
time: 125 us; the launch traced here: 124 us
  blocking collectives  65.6 us (52%)
  starting transfers between devices  30.7 us (25%)
  Pallas kernels  24.2 us (19%)
  waiting for transfers between devices  3.26 us (3%)
    all_to_all x2, blocking collectives, plane(): lax.all_to_all(blocks, ('x', 'y'), split_axis=0, concat_axis=0, tiled=True)  47.2 us
    pallas_call x10, Pallas kernels, call(): pl.pallas_call(kernel, in_specs=specs, out_specs=[out_spec] * len(outs),...  24.2 us
    all_to_all x1, blocking collectives, body(): lax.all_to_all(modes, COLUMN, split_axis=0, concat_axis=0, tiled=True)  18.4 us
    ppermute x1, starting transfers between devices, body(): other = lax.ppermute(other, 'core', [(0, 1), (1, 0)])  14.5 us
    ppermute x6, starting transfers between devices, along_z(): return lax.ppermute(block, ('zl', 'zh', 'core'), pairs)  13.5 us
  transfers between devices with their start and end apart: 9, of which 4 were waited for; matrix products, arithmetic and copies ran while one was open for 0% of the time, Pallas kernels for 5%

profile of v6, /device:TPU:1, one launch (start us, length us, event | category | flops | bytes accessed | tf_op | source)
XLA Modules:
  0.0 124.2 jit_solution(16409332933213921673)
XLA Ops:
  0.0 0.0 copy-start.1
  0.0 1.4 %collective-permute-start = (bf16[3,16,32,2,256]{4,3,2,1,0:T(2,128)(2,1)}, bf16[3,16,32,2,256]{4,3,2,1,0:T(2,128)(2,1)S(1)}, u32[]{:S(2)}, u32[]{:S(2)}) collective-permute-start(bf16[3,16,32,2,256]{4,3,2,1,0:T(2,128)(2,1)} %param.7), channel_id=1, source_target_pairs={{0,1},{1,0},{2,3},{3,2},{4,5},{5,4},{6,7},{7,6},{8,9},{9,8},{10,11... | collective-permute-start | bytes 4718600 | tf_op jit(solution)/shard_map/ppermute | solution.py:358
  1.4 0.1 stack.23.pos
  1.5 2.4 %pack.2 = (bf16[1,3,4,2,16,256]{5,4,3,2,1,0:T(8,128)(2,1)S(1)}, bf16[1,3,4,2,16,256]{5,4,3,2,1,0:T(8,128)(2,1)S(1)}, bf16[1,3,4,2,16,256]{5,4,3,2,1,0:T(8,128)(2,1)S(1)}, bf16[1,3,4,2,16,256]{5,4,3,2,1,0:T(8,128)(2,1)S(1)}) custom-call(s32[5]{0:T(128)S(1)} %stack.23.pos, bf16[3,16,128,128]{3,2,1,0:T(8,128)(2,1)} %bitcast.22), custom_call_target="tpu_custom_call" | custom-call | tf_op jit(solution)/shard_map/pack/pallas_call | solution.py:344
  3.9 0.7 collective-permute-done
  4.7 1.6 %pack.3 = (bf16[2,3,4,2,16,256]{5,4,3,2,1,0:T(8,128)(2,1)S(1)}, bf16[2,3,4,2,16,256]{5,4,3,2,1,0:T(8,128)(2,1)S(1)}, bf16[2,3,4,2,16,256]{5,4,3,2,1,0:T(8,128)(2,1)S(1)}, bf16[2,3,4,2,16,256]{5,4,3,2,1,0:T(8,128)(2,1)S(1)}) custom-call(s32[5]{0:T(128)S(1)} %stack.23.pos, bf16[3,16,128,128]{3,2,1,0:T(8,128)(2,1)S(1)} %bitcast.25, ...), custom_call_target="tpu_custom_call" | custom-call | tf_op jit(solution)/shard_map/pack/pallas_call | solution.py:344
  6.3 3.6 %collective-permute-start.1 = (bf16[2,3,4,2,16,256]{5,4,3,2,1,0:T(8,128)(2,1)S(1)}, bf16[2,3,4,2,16,256]{5,4,3,2,1,0:T(8,128)(2,1)S(1)}, u32[]{:S(2)}, u32[]{:S(2)}) collective-permute-start(bf16[2,3,4,2,16,256]{5,4,3,2,1,0:T(8,128)(2,1)S(1)} %get-tuple-element.27.refs_2_), channel_id=1, source_target_pairs={{1,17},{17,3},{3,19},{19,1},{5,21},{21,7},{7,23},{23,5},{9,25},{25... | collective-permute-start | bytes 1179656 | tf_op jit(solution)/shard_map/ppermute | solution.py:318
  9.9 5.2 %collective-permute-start.2 = (bf16[2,3,4,2,16,256]{5,4,3,2,1,0:T(8,128)(2,1)S(1)}, bf16[2,3,4,2,16,256]{5,4,3,2,1,0:T(8,128)(2,1)S(1)}, u32[]{:S(2)}, u32[]{:S(2)}) collective-permute-start(bf16[2,3,4,2,16,256]{5,4,3,2,1,0:T(8,128)(2,1)S(1)} %get-tuple-element.28.refs_3_), channel_id=1, source_target_pairs={{1,3},{17,19},{3,1},{19,17},{5,7},{21,23},{7,5},{23,21},{9,11},{25... | collective-permute-start | bytes 1179656 | tf_op jit(solution)/shard_map/ppermute | solution.py:318
  15.2 2.6 %collective-permute-start.3 = (bf16[2,3,4,2,16,256]{5,4,3,2,1,0:T(8,128)(2,1)S(1)}, bf16[2,3,4,2,16,256]{5,4,3,2,1,0:T(8,128)(2,1)S(1)}, u32[]{:S(2)}, u32[]{:S(2)}) collective-permute-start(bf16[2,3,4,2,16,256]{5,4,3,2,1,0:T(8,128)(2,1)S(1)} %get-tuple-element.29.refs_4_), channel_id=1, source_target_pairs={{1,19},{17,1},{3,17},{19,3},{5,23},{21,5},{7,21},{23,7},{9,27},{25... | collective-permute-start | bytes 1179656 | tf_op jit(solution)/shard_map/ppermute | solution.py:318
  17.8 1.3 %collective-permute-start.4 = (bf16[16,128]{1,0:T(8,128)(2,1)S(1)}, bf16[16,128]{1,0:T(8,128)(2,1)S(1)}, u32[]{:S(2)}, u32[]{:S(2)}) collective-permute-start(bf16[16,128]{1,0:T(8,128)(2,1)S(1)} %slice_bitcast_fusion), channel_id=1, source_target_pairs={{1,0},{3,2},{5,4},{7,6},{9,8},{11,10},{13,12},{15,14},{17,16},{19,... | collective-permute-start | bytes 12296 | tf_op jit(solution)/shard_map/ppermute | solution.py:378
  19.1 0.0 copy-done.1
  19.1 2.9 %preload.1 = (bf16[2,2,512,768]{3,2,1,0:T(8,128)(2,1)S(1)}, bf16[2,768,512]{2,1,0:T(8,128)(2,1)S(1)}, bf16[2,512,768]{2,1,0:T(8,128)(2,1)S(1)}, bf16[128,1024]{1,0:T(8,128)(2,1)S(1)}) custom-call(bf16[2,3,4,2,16,256]{5,4,3,2,1,0:T(8,128)(2,1)S(1)} %get-tuple-element.26.after_ref.r0, bf16[8,32,32]{2,1,0:T(8,128)(2,1)S(1)} %copy-done.1, ...), custom_call_target="tpu_custom_call" | custom-call | tf_op jit(solution)/shard_map/preload/pallas_call | solution.py:344
  22.0 0.0 collective-permute-done.4.refs_0_
  22.0 0.0 collective-permute-done.1.e1
  22.0 0.6 collective-permute-done.2.e2
  22.6 1.3 %collective-permute-done.3.e3 = bf16[2,3,4,2,16,256]{5,4,3,2,1,0:T(8,128)(2,1)S(1)} collective-permute-done((bf16[2,3,4,2,16,256]{5,4,3,2,1,0:T(8,128)(2,1)S(1)}, bf16[2,3,4,2,16,256]{5,4,3,2,1,0:T(8,128)(2,1)S(1)}, u32[]{:S(2)}, u32[]{:S(2)}) %collective-permute-start.3) | collective-permute-done | bytes 393248 | tf_op jit(solution)/shard_map/ppermute | solution.py:318
  23.9 0.7 collective-permute-start.5
  24.6 0.7 collective-permute-start.6
  25.3 0.7 collective-permute-start.7
  26.0 0.0 collective-permute-done.5.l1
  26.0 0.0 collective-permute-done.6.l2
  26.0 0.0 collective-permute-done.7.l3
  26.0 3.5 %synth.1 = bf16[16,3,2,32,384]{4,3,2,1,0:T(8,128)(2,1)S(1)} custom-call(s32[5]{0:T(128)S(1)} %stack.23.pos, bf16[2,3,4,2,16,256]{5,4,3,2,1,0:T(8,128)(2,1)S(1)} %get-tuple-element.26.after_ref.r0, bf16[2,3,4,2,16,256]{5,4,3,2,1,0:T(8,128)(2,1)S(1)} %collective-permute-done.1.e1, bf16[2,3,4,2,16,256]{5,4,3,2,1,0:T(8,128)(2,1)S(1)} %collective-permute-done.2.e2, ...), custom_call_target="tpu_custom_call" | custom-call | tf_op jit(solution)/shard_map/synth/pallas_call | solution.py:344
  29.5 25.2 %all_to_all.15.d_ref = bf16[16,3,2,32,384]{4,3,2,1,0:T(8,128)(2,1)S(1)} all-to-all(bf16[16,3,2,32,384]{4,3,2,1,0:T(8,128)(2,1)S(1)} %synth.1), channel_id=1, replica_groups=mesh['x'=4,'zl'=2,'y'=4,'zh'=2,'core'=2] {'x','y'}, dimensions={0} | all-to-all | bytes 4718592 | tf_op jit(solution)/shard_map/all_to_all | solution.py:322
  54.7 4.8 %middle.1 = (bf16[16,3,2,32,384]{4,3,2,1,0:T(8,128)(2,1)S(1)}, bf16[2,2,512,768]{3,2,1,0:T(8,128)(2,1)S(1)}) custom-call(bf16[16,3,2,32,384]{4,3,2,1,0:T(8,128)(2,1)S(1)} %all_to_all.15.d_ref, bf16[2,768,512]{2,1,0:T(8,128)(2,1)S(1)} %get-tuple-element.34.synth_ref, bf16[2,512,768]{2,1,0:T(8,128)(2,1)S(1)} %get-tuple-element.35.fold_ref, ...), custom_call_target="tpu_custom_call" | custom-call | tf_op jit(solution)/shard_map/middle/pallas_call | solution.py:344
  59.4 22.0 %all_to_all.16.b_ref = bf16[16,3,2,32,384]{4,3,2,1,0:T(8,128)(2,1)S(1)} all-to-all(bf16[16,3,2,32,384]{4,3,2,1,0:T(8,128)(2,1)S(1)} %get-tuple-element.36), channel_id=1, replica_groups=mesh['x'=4,'zl'=2,'y'=4,'zh'=2,'core'=2] {'x','y'}, dimensions={0} | all-to-all | bytes 4718592 | tf_op jit(solution)/shard_map/all_to_all | solution.py:322
  81.5 3.5 %analyse.1 = bf16[4,2,3,4,2,16,256]{6,5,4,3,2,1,0:T(8,128)(2,1)S(1)} custom-call(s32[5]{0:T(128)S(1)} %stack.23.pos, bf16[16,3,2,32,384]{4,3,2,1,0:T(8,128)(2,1)S(1)} %all_to_all.16.b_ref, bf16[2,2,512,768]{3,2,1,0:T(8,128)(2,1)S(1)} %get-tuple-element.37.table_ref), custom_call_target="tpu_custom_call" | custom-call | tf_op jit(solution)/shard_map/analyse/pallas_call | solution.py:344
  85.0 0.0 copy-start
  85.0 0.0 copy-start.3
  85.0 18.4 %all_to_all.17.n_ref = bf16[4,2,3,4,2,16,256]{6,5,4,3,2,1,0:T(8,128)(2,1)S(1)} all-to-all(bf16[4,2,3,4,2,16,256]{6,5,4,3,2,1,0:T(8,128)(2,1)S(1)} %analyse.1), channel_id=1, replica_groups=mesh['x'=4,'zl'=2,'y'=4,'zh'=2,'core'=2] {'zl','zh'}, dimensions={0} | all-to-all | bytes 3145728 | tf_op jit(solution)/shard_map/all_to_all | solution.py:401
  103.4 0.1 gather.1
  103.4 0.0 copy-start.2
  103.5 14.5 %collective-permute-start.8 = (bf16[4,3,4,2,16,256]{5,4,3,2,1,0:T(8,128)(2,1)S(1)}, bf16[4,3,4,2,16,256]{5,4,3,2,1,0:T(8,128)(2,1)S(1)}, u32[]{:S(2)}, u32[]{:S(2)}) collective-permute-start(bf16[4,3,4,2,16,256]{5,4,3,2,1,0:T(8,128)(2,1)S(1)} %gather.1), channel_id=1, source_target_pairs={{0,1},{1,0},{2,3},{3,2},{4,5},{5,4},{6,7},{7,6},{8,9},{9,8},{10,11... | collective-permute-start | bytes 2359304 | tf_op jit(solution)/shard_map/ppermute | solution.py:403
  118.0 0.0 copy-done
  118.0 0.0 copy-done.3
  118.0 1.3 %right.1.right_ref = bf16[8,4,16,768]{3,2,1,0:T(8,128)(2,1)S(1)} custom-call(s32[5]{0:T(128)S(1)} %stack.23.pos, s32[16]{0:T(128)S(1)} %copy-done.3, bf16[4,2,3,4,2,16,256]{6,5,4,3,2,1,0:T(8,128)(2,1)S(1)} %all_to_all.17.n_ref, bf16[3,16,128,128]{3,2,1,0:T(8,128)(2,1)S(1)} %bitcast.23), custom_call_target="tpu_custom_call" | custom-call | tf_op jit(solution)/shard_map/right/pallas_call | solution.py:344
  119.3 0.6 collective-permute-done.8.other_ref
  119.9 0.0 copy-done.2
  119.9 4.2 %solve.1 = f32[3,16,128,128]{3,2,1,0:T(8,128)} custom-call(s32[5]{0:T(128)S(1)} %stack.23.pos, s32[16]{0:T(128)S(1)} %copy-done.3, bf16[8,4,16,768]{3,2,1,0:T(8,128)(2,1)S(1)} %right.1.right_ref, bf16[4,3,4,2,16,256]{5,4,3,2,1,0:T(8,128)(2,1)S(1)} %collective-permute-done.8.other_ref, bf16[3,16,128,128]{3,2,1,0:T(8,128)(2,1)S(1)} %bitcast.24, ...), custom_call_target="tpu_custom_call" | custom-call | tf_op jit(solution)/shard_map/solve/pallas_call | solution.py:344
  (2 shorter events, 0.0 us)
Async XLA Ops:
  0.0 19.1 %copy-start.1 = (bf16[8,32,32]{2,1,0:T(8,128)(2,1)S(1)}, bf16[8,32,32]{2,1,0:T(8,128)(2,1)}, u32[]{:S(2)}) copy-start(bf16[8,32,32]{2,1,0:T(8,128)(2,1)} %inv_ref.1) | copy-start | bytes 49156
  0.0 4.7 %collective-permute-start = (bf16[3,16,32,2,256]{4,3,2,1,0:T(2,128)(2,1)}, bf16[3,16,32,2,256]{4,3,2,1,0:T(2,128)(2,1)S(1)}, u32[]{:S(2)}, u32[]{:S(2)}) collective-permute-start(bf16[3,16,32,2,256]{4,3,2,1,0:T(2,128)(2,1)} %param.7), channel_id=1, source_target_pairs={{0,1},{1,0},{2,3},{3,2},{4,5},{5,4},{6,7},{7,6},{8,9},{9,8},{10,11... | collective-permute-start | bytes 4718600 | tf_op jit(solution)/shard_map/ppermute | solution.py:358
  6.3 15.7 %collective-permute-start.1 = (bf16[2,3,4,2,16,256]{5,4,3,2,1,0:T(8,128)(2,1)S(1)}, bf16[2,3,4,2,16,256]{5,4,3,2,1,0:T(8,128)(2,1)S(1)}, u32[]{:S(2)}, u32[]{:S(2)}) collective-permute-start(bf16[2,3,4,2,16,256]{5,4,3,2,1,0:T(8,128)(2,1)S(1)} %get-tuple-element.27.refs_2_), channel_id=1, source_target_pairs={{1,17},{17,3},{3,19},{19,1},{5,21},{21,7},{7,23},{23,5},{9,25},{25... | collective-permute-start | bytes 1179656 | tf_op jit(solution)/shard_map/ppermute | solution.py:318
  9.9 12.7 %collective-permute-start.2 = (bf16[2,3,4,2,16,256]{5,4,3,2,1,0:T(8,128)(2,1)S(1)}, bf16[2,3,4,2,16,256]{5,4,3,2,1,0:T(8,128)(2,1)S(1)}, u32[]{:S(2)}, u32[]{:S(2)}) collective-permute-start(bf16[2,3,4,2,16,256]{5,4,3,2,1,0:T(8,128)(2,1)S(1)} %get-tuple-element.28.refs_3_), channel_id=1, source_target_pairs={{1,3},{17,19},{3,1},{19,17},{5,7},{21,23},{7,5},{23,21},{9,11},{25... | collective-permute-start | bytes 1179656 | tf_op jit(solution)/shard_map/ppermute | solution.py:318
  15.2 8.8 %collective-permute-start.3 = (bf16[2,3,4,2,16,256]{5,4,3,2,1,0:T(8,128)(2,1)S(1)}, bf16[2,3,4,2,16,256]{5,4,3,2,1,0:T(8,128)(2,1)S(1)}, u32[]{:S(2)}, u32[]{:S(2)}) collective-permute-start(bf16[2,3,4,2,16,256]{5,4,3,2,1,0:T(8,128)(2,1)S(1)} %get-tuple-element.29.refs_4_), channel_id=1, source_target_pairs={{1,19},{17,1},{3,17},{19,3},{5,23},{21,5},{7,21},{23,7},{9,27},{25... | collective-permute-start | bytes 1179656 | tf_op jit(solution)/shard_map/ppermute | solution.py:318
  17.8 4.2 %collective-permute-start.4 = (bf16[16,128]{1,0:T(8,128)(2,1)S(1)}, bf16[16,128]{1,0:T(8,128)(2,1)S(1)}, u32[]{:S(2)}, u32[]{:S(2)}) collective-permute-start(bf16[16,128]{1,0:T(8,128)(2,1)S(1)} %slice_bitcast_fusion), channel_id=1, source_target_pairs={{1,0},{3,2},{5,4},{7,6},{9,8},{11,10},{13,12},{15,14},{17,16},{19,... | collective-permute-start | bytes 12296 | tf_op jit(solution)/shard_map/ppermute | solution.py:378
  23.9 2.1 %collective-permute-start.5 = (bf16[2,3,4,2,16,256]{5,4,3,2,1,0:T(8,128)(2,1)S(1)}, bf16[2,3,4,2,16,256]{5,4,3,2,1,0:T(8,128)(2,1)S(1)}, u32[]{:S(2)}, u32[]{:S(2)}) collective-permute-start(bf16[2,3,4,2,16,256]{5,4,3,2,1,0:T(8,128)(2,1)S(1)} %get-tuple-element.31), channel_id=1, source_target_pairs={{0,16},{16,2},{2,18},{18,0},{4,20},{20,6},{6,22},{22,4},{8,24},{24... | collective-permute-start | bytes 1179656 | tf_op jit(solution)/shard_map/ppermute | solution.py:318
  24.6 1.4 %collective-permute-start.6 = (bf16[2,3,4,2,16,256]{5,4,3,2,1,0:T(8,128)(2,1)S(1)}, bf16[2,3,4,2,16,256]{5,4,3,2,1,0:T(8,128)(2,1)S(1)}, u32[]{:S(2)}, u32[]{:S(2)}) collective-permute-start(bf16[2,3,4,2,16,256]{5,4,3,2,1,0:T(8,128)(2,1)S(1)} %get-tuple-element.32), channel_id=1, source_target_pairs={{0,2},{16,18},{2,0},{18,16},{4,6},{20,22},{6,4},{22,20},{8,10},{24... | collective-permute-start | bytes 1179656 | tf_op jit(solution)/shard_map/ppermute | solution.py:318
  25.3 0.7 collective-permute-start.7
  85.0 33.0 %copy-start = (bf16[3,16,32,2,256]{4,3,2,1,0:T(2,128)(2,1)S(1)}, bf16[3,16,32,2,256]{4,3,2,1,0:T(2,128)(2,1)}, u32[]{:S(2)}) copy-start(bf16[3,16,32,2,256]{4,3,2,1,0:T(2,128)(2,1)} %param.7) | copy-start | bytes 4718596
  85.0 33.0 %copy-start.3 = (s32[16]{0:T(128)S(1)}, s32[16]{0:T(128)}, u32[]{:S(2)}) copy-start(s32[16]{0:T(128)} %count_ref.3) | copy-start | bytes 196
  103.4 16.4 %copy-start.2 = (s32[16,256]{1,0:T(8,128)S(1)}, s32[16,256]{1,0:T(8,128)}, u32[]{:S(2)}) copy-start(s32[16,256]{1,0:T(8,128)} %class_ref.1) | copy-start | bytes 49156
  103.5 16.4 %collective-permute-start.8 = (bf16[4,3,4,2,16,256]{5,4,3,2,1,0:T(8,128)(2,1)S(1)}, bf16[4,3,4,2,16,256]{5,4,3,2,1,0:T(8,128)(2,1)S(1)}, u32[]{:S(2)}, u32[]{:S(2)}) collective-permute-start(bf16[4,3,4,2,16,256]{5,4,3,2,1,0:T(8,128)(2,1)S(1)} %gather.1), channel_id=1, source_target_pairs={{0,1},{1,0},{2,3},{3,2},{4,5},{5,4},{6,7},{7,6},{8,9},{9,8},{10,11... | collective-permute-start | bytes 2359304 | tf_op jit(solution)/shard_map/ppermute | solution.py:403
